TPU v7x, 256 devices: a whole 4x4x8 slice. The times are simulated.
256 devices in a mesh: tm: 16 (over y_lo, x, core), space: 16 (over y_hi, z).
Axes of the slice: x: 4, y: 4 (y_hi: 2, y_lo: 2; y = y_hi * 2 + y_lo), z: 8, core: 2. Of those that a mesh axis runs over, the one named last changes fastest.
Arguments:
- eigvecs: bfloat16 [2, 64, 21504, 256], P(None, 'tm', 'space'), may hold values from -0.03125 to 0.03125
- solutions: bfloat16 [2, 64, 21504, 256], P(None, 'tm', 'space'), may hold values from -6 to 6
- elementals: bfloat16 [2, 64, 256, 256], P(None, 'tm'), may hold values from -0.25 to 0.25
- source_list: int32 [4], replicated, may hold values from 0 to 63
- pair_owner: int32 [16, 16], replicated, may hold values from 0 to 15, each once within a row
- dilution_order: int32 [64], replicated, may hold values from 0 to 63, each once
Outputs:
- boxes: bfloat16 [256, 2, 256, 256], P('tm', None, 'space')
Inputs may be any that keep to these rules, and one draw needn't show every extreme that they name: `pair_owner`: each row is a permutation of the tm indices. `dilution_order`: a permutation of the dilution columns.
All inputs are finite; a program needn't handle non-finite values.
Results may differ from a plain program's by a relative error of at most 0.0064.
Values may be sent and summed in bfloat16 or wider, within the bound.
No kernel may reach another device: no remote copies, remote signals or barrier semaphores. Data moves between devices by JAX's collectives and lax.ppermute only.
A program may use at most 64 MiB of HBM per device.

v0:
```python
import jax
import jax.numpy as jnp
from jax import lax
from jax.sharding import PartitionSpec as P

SPINS = 4


def from_root(x, axis, root):
    mine = lax.axis_index(axis) == root
    return lax.psum(jnp.where(mine, x, jnp.zeros_like(x)), axis)


def conj_product(left, right, form, stack_axis):
    real_part = jnp.einsum(form, left[0], right[0], preferred_element_type=jnp.float32)
    real_part = real_part + jnp.einsum(form, left[1], right[1], preferred_element_type=jnp.float32)
    imag_part = jnp.einsum(form, left[0], right[1], preferred_element_type=jnp.float32)
    imag_part = imag_part - jnp.einsum(form, left[1], right[0], preferred_element_type=jnp.float32)
    return jnp.stack([real_part, imag_part], axis=stack_axis)


def per_device(eigvecs, solutions, elementals, source_list, pair_owner, dilution_order):
    tdev = eigvecs.shape[1]
    nev = eigvecs.shape[3]
    total_cols = solutions.shape[3]
    tm_count = lax.axis_size("tm")
    width = total_cols // lax.axis_size("space")
    source_count = source_list.shape[0]
    pieces = []
    partial_value = conj_product(eigvecs, solutions, "tkm,tkn->tmn", 0)
    summed = lax.psum(partial_value, "space").astype(jnp.bfloat16)
    slab = lax.dynamic_slice_in_dim(summed, lax.axis_index("space") * width, width, 3)
    for source in range(source_count):
        moment = source_list[source]
        local_tile = lax.dynamic_index_in_dim(summed, moment % tdev, 1, keepdims=False)
        pieces.append(from_root(local_tile, "tm", moment // tdev))
    sources = jnp.stack(pieces)
    weighted = conj_product(elementals, slab, "tkm,tkn->tmn", 0).astype(jnp.bfloat16)
    sources = sources.reshape(source_count, 2, nev, SPINS, total_cols // SPINS)
    sources = jnp.take(sources, dilution_order, axis=4).reshape(source_count, 2, nev, total_cols)
    sources = jnp.transpose(sources, (1, 0, 2, 3))
    scale = (2.0 * nev) ** (-0.5)
    tiles = (conj_product(weighted, sources, "tkm,skn->tsmn", 0) * scale).astype(jnp.bfloat16)
    tiles = jnp.transpose(tiles, (1, 2, 0, 3, 4)).reshape(tdev * source_count, 2, width, total_cols)
    owners = lax.dynamic_index_in_dim(pair_owner, lax.axis_index("tm"), 0, keepdims=False)
    targets = jnp.arange(tm_count)
    selector = (owners[None, :] == targets[:, None]).astype(jnp.bfloat16)
    outgoing = jnp.einsum(
        "dj,jabc->dabc", selector, tiles, preferred_element_type=jnp.float32
    ).astype(jnp.bfloat16)
    return lax.all_to_all(outgoing, "tm", split_axis=0, concat_axis=0, tiled=True)


def solution(mesh):
    in_specs = (
        P(None, "tm", "space", None),
        P(None, "tm", "space", None),
        P(None, "tm", None, None),
        P(),
        P(),
        P(),
    )
    out_specs = P("tm", None, "space", None)
    return jax.shard_map(
        per_device, mesh=mesh, in_specs=in_specs, out_specs=out_specs, check_vma=False
    )
```

profile of v0, /device:TPU:1, one launch (start us, length us, event | category | flops | bytes accessed | tf_op | source)
XLA Modules:
  0.0 281.7 jit_solution(1352897264279868630)
XLA Ops:
  6.5 0.0 copy-start
  6.5 0.0 all-reduce.4.cloned.1.call-start
  6.5 1.5 fusion.69
  18.2 0.0 copy-start.2
  18.2 4.0 %fusion.2 = f32[4,256,256]{2,1,0:T(8,128)S(1)} fusion(bf16[2,4,1344,256]{3,2,1,0:T(8,128)(2,1)} %param.7, bf16[2,4,1344,256]{3,2,1,0:T(8,128)(2,1)} %param.6), kind=kOutput, calls=%fused_computation.3 | convolution fusion | flops 704643072 | bytes 6553600 | tf_op jit(solution)/shard_map/tkm,tkn->tmn/dot_general | solution.py:16
  22.2 0.2 copy-done.2
  22.4 3.1 %fusion = f32[4,256,256]{2,1,0:T(8,128)S(1)} fusion(bf16[2,4,1344,256]{3,2,1,0:T(8,128)(2,1)S(1)} %copy-done.2, bf16[2,4,1344,256]{3,2,1,0:T(8,128)(2,1)} %param.6), kind=kOutput, calls=%fused_computation.1 | convolution fusion | flops 704643072 | bytes 6553600 | tf_op jit(solution)/shard_map/tkm,tkn->tmn/dot_general | solution.py:17
  25.6 0.0 slice-start.1
  25.7 4.0 %fusion.25 = f32[1,4,256,256]{3,2,1,0:T(8,128)S(1)} fusion(f32[4,256,256]{2,1,0:T(8,128)S(1)} %fusion.2, bf16[2,4,1344,256]{3,2,1,0:T(8,128)(2,1)} %param.7, bf16[2,4,1344,256]{3,2,1,0:T(8,128)(2,1)} %param.6), kind=kOutput, calls=%fused_computation.23 | convolution fusion | flops 704905216 | bytes 7602176 | tf_op jit(solution)/shard_map/tkm,tkn->tmn/dot_general | solution.py:15
  29.6 0.0 slice-done
  29.7 0.0 slice-done.1
  29.7 3.1 %fusion.35 = f32[1,4,256,256]{3,2,1,0:T(8,128)S(1)} fusion(f32[4,256,256]{2,1,0:T(8,128)S(1)} %fusion, bf16[2,4,1344,256]{3,2,1,0:T(8,128)(2,1)S(1)} %bitcast.122, bf16[2,4,1344,256]{3,2,1,0:T(8,128)(2,1)} %param.6), kind=kOutput, calls=%fused_computation.25 | convolution fusion | flops 704905216 | bytes 7602176 | tf_op jit(solution)/shard_map/tkm,tkn->tmn/dot_general | solution.py:18
  32.8 0.2 pad_maximum_fusion
  33.0 86.1 %all-reduce.5 = bf16[2,4,256,256]{3,2,1,0:T(8,128)(2,1)S(1)} all-reduce(f32[2,4,256,256]{3,2,1,0:T(8,128)S(1)} %pad_maximum_fusion), channel_id=1, replica_groups=mesh['tm'=16,'space'=16] {'space'}, use_global_device_ids=true, to_apply=%region_0.0 | all-reduce | flops 524288 | bytes 3145728 | tf_op jit(solution)/shard_map/psum | solution.py:31
  119.1 0.1 dynamic-slice_select_fusion.3
  119.2 0.0 copy-start.3
  119.2 0.0 copy-start.1
  119.2 0.1 copy.30
  119.3 0.9 copy.31
  120.2 0.1 copy.32
  120.4 0.9 copy.33
  121.3 0.1 copy.34
  121.4 0.9 copy.35
  122.3 0.1 copy.36
  122.4 0.9 copy.37
  123.4 0.0 all-reduce.4.cloned.1.call-update
  123.4 0.0 copy-done.3
  123.4 0.1 broadcast_in_dim.19
  123.5 0.0 copy-done.1
  123.5 0.3 fusion.51
  123.9 0.3 fusion.45
  124.2 0.3 fusion.49
  124.6 0.3 fusion.44
  124.9 130.5 %all-reduce.4.cloned.1.call-done = (bf16[1,2,256,4,64]{2,3,1,0,4:T(4,128)(2,1)}, bf16[1,2,256,4,64]{2,3,1,0,4:T(4,128)(2,1)}, bf16[1,2,256,4,64]{2,3,1,0,4:T(4,128)(2,1)}, bf16[1,2,256,4,64]{2,3,1,0,4:T(4,128)(2,1)}) async-done(((bf16[1,2,256,4,64]{2,3,1,0,4:T(4,128)(2,1)}, bf16[1,2,256,4,64]{2,3,1,0,4:T(4,128)(2,1)}, bf16[1,2,256,4,64]{2,3,1,0,4:T(4,128)(2,1)}, bf16[1,2,256,4,64]{2,3,1,0,4:T(4,128)(2,1)}), ...) | async-done | bytes 1048592 | tf_op jit(solution)/shard_map/psum | solution.py:11
  255.4 2.0 pad_maximum_fusion.1
  257.4 1.4 gather_fusion
  258.8 0.6 copy.38
  259.4 0.5 copy.39
  260.0 0.1 select_bitcast_fusion
  260.1 0.2 fusion.53
  260.3 0.2 fusion.54
  260.5 0.2 fusion.41
  260.7 0.2 fusion.40
  260.9 0.1 fusion.59
  261.0 0.3 convolution_convert_fusion
  261.3 0.1 copy.46
  261.4 12.8 %all_to_all.5 = bf16[16,2,16,256]{3,2,1,0:T(8,128)(2,1)S(1)} all-to-all(bf16[16,2,16,256]{3,2,1,0:T(8,128)(2,1)S(1)} %copy.46), channel_id=1, replica_groups=mesh['tm'=16,'space'=16] {'tm'}, dimensions={0} | all-to-all | bytes 524288 | tf_op jit(solution)/shard_map/all_to_all | solution.py:51
  274.1 0.7 copy.63
  (9 shorter events, 0.1 us)
Async XLA Ops:
  6.5 117.0 %copy-start = (s32[16,16]{1,0:T(8,128)S(1)}, s32[16,16]{1,0:T(8,128)}, u32[]{:S(2)}) copy-start(s32[16,16]{1,0:T(8,128)} %param.10) | copy-start | bytes 3076
  6.5 248.9 %all-reduce.4.cloned.1.call-start = ((), (), s32[]{:S(2)}) async-start(), calls=%async_computation.1 | async-start | bytes 2097152 | tf_op jit(solution)/shard_map/psum | solution.py:11
  18.2 4.2 %copy-start.2 = (bf16[2,4,1344,256]{3,2,1,0:T(8,128)(2,1)S(1)}, bf16[2,4,1344,256]{3,2,1,0:T(8,128)(2,1)}, u32[]{:S(2)}) copy-start(bf16[2,4,1344,256]{3,2,1,0:T(8,128)(2,1)} %param.7) | copy-start | bytes 16515076
  22.4 7.3 %slice-start = ((s8[5505024]{0:T(1024)(128)(4,1)}), s8[1310720]{0:T(1024)(128)(4,1)S(1)}, s32[]{:S(2)}) async-start(s8[5505024]{0:T(1024)(128)(4,1)} %bitcast.121), calls=%async_computation.2 | async-start | bytes 2621440
  25.6 4.0 %slice-start.1 = ((s8[5505024]{0:T(1024)(128)(4,1)}), s8[4194304]{0:T(1024)(128)(4,1)S(1)}, s32[]{:S(2)}) async-start(s8[5505024]{0:T(1024)(128)(4,1)} %bitcast.121), calls=%async_computation.3 | async-start | bytes 8388608
  119.2 4.2 %copy-start.3 = (s32[64]{0:T(128)S(1)}, s32[64]{0:T(128)}, u32[]{:S(2)}) copy-start(s32[64]{0:T(128)} %param.11) | copy-start | bytes 772
  119.2 4.4 %copy-start.1 = (bf16[2,4,256,256]{3,2,1,0:T(8,128)(2,1)S(1)}, bf16[2,4,256,256]{3,2,1,0:T(8,128)(2,1)}, u32[]{:S(2)}) copy-start(bf16[2,4,256,256]{3,2,1,0:T(8,128)(2,1)} %param.8) | copy-start | bytes 3145732
Sparse Core Ops, SparseCore 0:
  123.5 131.8 all-reduce.3
where the time goes:
time: 282 us
  waiting for transfers between devices  131 us (46%)
  blocking collectives  98.8 us (35%)
  between operations  24 us (9%)
  matrix products  16.6 us (6%)
  local copies, waits for them, and re-layouts  9.31 us (3%)
    psum x1, waiting for transfers between devices, from_root(): return lax.psum(jnp.where(mine, x, jnp.zeros_like(x)), axis)  131 us
    psum x1, blocking collectives, per_device(): summed = lax.psum(partial_value, 'space').astype(jnp.bfloat16)  86.1 us
    all_to_all x1, blocking collectives, per_device(): lax.all_to_all(outgoing, 'tm', split_axis=0, concat_axis=0, tiled=True)  12.8 us
  transfers between devices with their start and end apart: 1, of which 1 were waited for; matrix products, arithmetic and copies ran while one was open for 1% of the time, Pallas kernels for 0%

commit v1 on v0

v1 whole, which is shorter than its diff:
```python
import functools

import jax
import jax.numpy as jnp
from jax import lax
from jax.experimental import pallas as pl
from jax.experimental.pallas import tpu as pltpu
from jax.sharding import Mesh
from jax.sharding import PartitionSpec as P

TM = ("yl", "x", "core")
SPACE = ("yh", "z")
TD = 4
HALF = 2
NS = 4
NEV = 256
SC = 256
WIDTH = 16
SPINS = 4
F32 = jnp.float32
BF16 = jnp.bfloat16


def any_space():
    return pl.BlockSpec(memory_space=pl.ANY)


def smem():
    return pl.BlockSpec(memory_space=pltpu.SMEM)


def slot_timeslices(src, group):
    flags = []
    for t in range(TD):
        hit = src(0) == group * TD + t
        for s in range(1, NS):
            hit = jnp.logical_or(hit, src(s) == group * TD + t)
        flags.append(hit.astype(jnp.int32))
    total = flags[0] + flags[1] + flags[2] + flags[3]
    slots = []
    before = jnp.int32(0)
    for t in range(TD):
        slots.append(jnp.where(flags[t] == 1, before, total + t - before))
        before = before + flags[t]
    return slots


def slot_of(slots, t):
    out = slots[0]
    for k in range(1, TD):
        out = jnp.where(t == k, slots[k], out)
    return out


def timeslice_at(slots, place):
    out = jnp.int32(0)
    for t in range(1, TD):
        out = jnp.where(slots[t] == place, t, out)
    return out


def project_kernel(src_ref, group_ref, vec_ref, sol_ref, out_ref, acc_ref):
    del src_ref, group_ref
    kb = pl.program_id(1)
    depth = vec_ref.shape[2]
    vec = vec_ref[...].reshape(2, depth, NEV)
    sol = sol_ref[...].reshape(2 * depth, SC)
    straight = vec.reshape(2 * depth, NEV)
    turned = jnp.concatenate([-vec[1], vec[0]], axis=0)
    dims = (((0,), (0,)), ((), ()))
    real = lax.dot_general(sol, straight, dims, preferred_element_type=F32)
    imag = lax.dot_general(sol, turned, dims, preferred_element_type=F32)

    @pl.when(kb == 0)
    def _():
        acc_ref[0] = real
        acc_ref[1] = imag

    @pl.when(kb > 0)
    def _():
        acc_ref[0] += real
        acc_ref[1] += imag

    @pl.when(kb == pl.num_programs(1) - 1)
    def _():
        for part in range(2):
            out_ref[:, 0, part] = acc_ref[part].reshape(SC // WIDTH, WIDTH, NEV).astype(BF16)


def project(half, src, group, eigvecs, solutions, blocks=2):
    depth = eigvecs.shape[2] // blocks

    def place(i, kb, src_ref, group_ref):
        slots = slot_timeslices(lambda s: src_ref[s], group_ref[0])
        return (0, timeslice_at(slots, half * HALF + i), kb, 0)

    spec = pl.BlockSpec((2, 1, depth, NEV), place)
    return pl.pallas_call(
        project_kernel,
        grid_spec=pltpu.PrefetchScalarGridSpec(
            num_scalar_prefetch=2,
            grid=(HALF, blocks),
            in_specs=[spec, spec],
            out_specs=pl.BlockSpec((SC // WIDTH, 1, 2, WIDTH, NEV), lambda i, kb, *_: (0, i, 0, 0, 0)),
            scratch_shapes=[pltpu.VMEM((2, SC, NEV), F32)],
        ),
        out_shape=jax.ShapeDtypeStruct((SC // WIDTH, HALF, 2, WIDTH, NEV), BF16),
        compiler_params=pltpu.CompilerParams(vmem_limit_bytes=58 * 2**20),
        cost_estimate=pl.CostEstimate(flops=1_400_000_000, bytes_accessed=6_000_000, transcendentals=0),
        name="project%d" % half,
    )(src, group, eigvecs, solutions)


def gather_rows(src_ref, group, half, projected, scatter_ref):
    slots = slot_timeslices(lambda s: src_ref[s], group)
    for s in range(NS):
        place = slot_of(slots, lax.rem(src_ref[s], TD)) - half * HALF
        place = jnp.clip(place, 0, HALF - 1)
        for part in range(2):
            rows = projected[0, part]
            for k in range(1, HALF):
                rows = jnp.where(place == k, projected[k, part], rows)
            for side in range(2):
                scatter_ref[(s * 2 + part) * 2 + side] = rows[:, side * 128 : (side + 1) * 128]


def weigh(src_ref, group, half, projected, elem_ref, weighted):
    slots = slot_timeslices(lambda s: src_ref[s], group)
    for k in range(HALF):
        t = timeslice_at(slots, half * HALF + k)
        er = elem_ref[0, t]
        ei = elem_ref[1, t]
        both = projected[k].reshape(2 * WIDTH, NEV)
        by_real = jnp.dot(both, er, preferred_element_type=F32)
        by_imag = jnp.dot(both, ei, preferred_element_type=F32)
        weighted(k, 0, (by_real[:WIDTH] + by_imag[WIDTH:]).astype(BF16))
        weighted(k, 1, (by_real[WIDTH:] - by_imag[:WIDTH]).astype(BF16))


def reduced(recv_ref):
    total = recv_ref[0].astype(F32)
    for c in range(1, recv_ref.shape[0]):
        total = total + recv_ref[c].astype(F32)
    return total.astype(BF16)


def first_kernel(src_ref, group_ref, recv_ref, elem_ref, scatter_ref, weighted_ref):
    group = group_ref[0]
    projected = reduced(recv_ref)
    gather_rows(src_ref, group, 0, projected, scatter_ref)

    def store(k, part, value):
        weighted_ref[k, part] = value

    weigh(src_ref, group, 0, projected, elem_ref, store)


def second_kernel(src_ref, group_ref, owner_ref, recv_ref, elem_ref, before_ref, scatter_ref, out_ref, all_ref):
    group = group_ref[0]
    projected = reduced(recv_ref)
    gather_rows(src_ref, group, 1, projected, scatter_ref)
    for k in range(HALF):
        all_ref[k] = before_ref[k]

    def store(k, part, value):
        all_ref[HALF + k, part] = value

    weigh(src_ref, group, 1, projected, elem_ref, store)
    slots = slot_timeslices(lambda s: src_ref[s], group)
    for j in range(TD * NS):
        out_ref[owner_ref[group, j]] = all_ref[slots[j // NS]]


def final_kernel(owner_ref, order_ref, where_ref, weighted_ref, own_ref, other_ref, out_ref):
    me = where_ref[0]
    side = where_ref[1]
    order = order_ref[...]
    wide = jnp.concatenate([order + spin * (SC // SPINS) for spin in range(SPINS)], axis=1)
    rows = lax.broadcasted_iota(jnp.int32, (SC, SC), 0)
    chosen = (rows == wide).astype(BF16)
    scale = (2.0 * NEV) ** (-0.5)
    dims = (((1,), (1,)), ((), ()))
    for e in range(out_ref.shape[0]):
        source = jnp.int32(0)
        for j in range(TD * NS):
            source = jnp.where(owner_ref[e, j] == me, j % NS, source)
        both = weighted_ref[e].reshape(2 * WIDTH, NEV)
        low, high = both[:, :128], both[:, 128:]
        mine = jnp.where(side == 0, low, high)
        rest = jnp.where(side == 0, high, low)
        by = []
        for part in range(2):
            value = lax.dot_general(mine, own_ref[source * 2 + part], dims, preferred_element_type=F32)
            value += lax.dot_general(rest, other_ref[source * 2 + part], dims, preferred_element_type=F32)
            by.append(value)
        real = (by[0][:WIDTH] + by[1][WIDTH:]) * scale
        imag = (by[1][:WIDTH] - by[0][WIDTH:]) * scale
        tile = jnp.concatenate([real, imag], axis=0).astype(BF16)
        tile = jnp.dot(tile, chosen, preferred_element_type=F32).astype(BF16)
        out_ref[e] = tile.reshape(2, WIDTH, SC)


def vmem():
    return pl.BlockSpec(memory_space=pltpu.VMEM)


def all_to_all(x, axes):
    return lax.all_to_all(x, axes, split_axis=0, concat_axis=0, tiled=True)


def spread(scatter, src):
    parts = all_to_all(scatter, TM)
    root = src[lax.axis_index(TM) // 4] // TD
    piece = lax.dynamic_index_in_dim(parts, root, 0, keepdims=True)
    slabs = all_to_all(jnp.broadcast_to(piece, parts.shape), SPACE)
    slabs = slabs.reshape(1, SC, 128)
    own = all_to_all(jnp.broadcast_to(slabs, (8, SC, 128)), ("yl", "x"))
    other = lax.ppermute(own, "core", [(0, 1), (1, 0)])
    return own, other


def per_device(eigvecs, solutions, elementals, source_list, pair_owner, dilution_order):
    me = lax.axis_index(TM)
    group = me.reshape(1)
    params = pltpu.CompilerParams(vmem_limit_bytes=40 * 2**20)
    sums = []
    for half in range(2):
        sums.append(project(half, source_list, group, eigvecs, solutions))
    recv = all_to_all(sums[0], SPACE)
    scatter, weighted = pl.pallas_call(
        first_kernel,
        in_specs=[smem(), smem(), vmem(), vmem()],
        out_specs=[vmem(), vmem()],
        out_shape=[
            jax.ShapeDtypeStruct((16, WIDTH, 128), BF16),
            jax.ShapeDtypeStruct((HALF, 2, WIDTH, NEV), BF16),
        ],
        compiler_params=params,
        name="first",
    )(source_list, group, recv, elementals)
    own, other = spread(scatter, source_list)
    recv = all_to_all(sums[1], SPACE)
    late, outgoing = pl.pallas_call(
        second_kernel,
        in_specs=[smem(), smem(), smem(), vmem(), vmem(), vmem()],
        out_specs=[vmem(), vmem()],
        out_shape=[
            jax.ShapeDtypeStruct((16, WIDTH, 128), BF16),
            jax.ShapeDtypeStruct((16, 2, WIDTH, NEV), BF16),
        ],
        scratch_shapes=[pltpu.VMEM((TD, 2, WIDTH, NEV), BF16)],
        compiler_params=params,
        name="second",
    )(source_list, group, pair_owner, recv, elementals, weighted)
    weights = all_to_all(outgoing, TM)

    first = source_list
    groups = first // TD
    distinct = jnp.array(True)
    same = (first[:, None] == first[None, :]) & (jnp.arange(NS)[:, None] > jnp.arange(NS)[None, :])
    fresh = ~jnp.any(same, axis=1)
    lower = (groups[:, None] == groups[None, :]) & (first[None, :] < first[:, None]) & fresh[None, :]
    rank = jnp.sum(lower.astype(jnp.int32), axis=1)
    is_late = rank >= HALF
    del distinct

    def again(own, other, late):
        own2, other2 = spread(late, source_list)
        pick = jnp.repeat(is_late, 2)[:, None, None]
        return jnp.where(pick, own2, own), jnp.where(pick, other2, other)

    own, other = lax.cond(jnp.any(is_late), again, lambda own, other, late: (own, other), own, other, late)

    where = jnp.stack([me, lax.axis_index("core")])
    return pl.pallas_call(
        final_kernel,
        in_specs=[smem(), vmem(), smem(), vmem(), vmem(), vmem()],
        out_specs=vmem(),
        out_shape=jax.ShapeDtypeStruct((16, 2, WIDTH, SC), BF16),
        compiler_params=params,
        name="final",
    )(pair_owner, dilution_order.reshape(1, -1), where, weights, own, other)


def solution(mesh):
    fine = Mesh(mesh.devices.reshape(2, 4, 2, 2, 8), TM + SPACE)
    in_specs = (
        P(None, TM, SPACE, None),
        P(None, TM, SPACE, None),
        P(None, TM, None, None),
        P(),
        P(),
        P(),
    )
    return jax.shard_map(
        per_device, mesh=fine, in_specs=in_specs, out_specs=P(TM, None, SPACE, None), check_vma=False
    )
```

time: 282 us -> 115 us (0.41)
  waiting for transfers between devices: 131 us -> 24 us
  blocking collectives: 98.8 us -> 40.6 us
  starting transfers between devices: 0.01 us -> 22.6 us
  Pallas kernels: 0 us -> 21.3 us
  between operations: 24 us -> 3.24 us
  matrix products: 16.6 us -> 0 us
  local copies, waits for them, and re-layouts: 9.31 us -> 1.52 us
    psum x1 -> x0, waiting for transfers between devices: 131 us -> none  [from_root(): return lax.psum(jnp.where(mine, x, jnp.zeros_like(x)), axis)]
    psum x1 -> x0, blocking collectives: 86.1 us -> none  [per_device(): summed = lax.psum(partial_value, 'space').astype(jnp.bfloat16)]
    all_to_all x1 -> x2, blocking collectives: 12.8 us -> 40.6 us  [all_to_all(): return lax.all_to_all(x, axes, split_axis=0, concat_axis=0, tiled=True)]
    all_to_all x0 -> x4, waiting for transfers between devices: none -> 24 us  [all_to_all(): return lax.all_to_all(x, axes, split_axis=0, concat_axis=0, tiled=True)]
    pallas_call x0 -> x5, Pallas kernels: none -> 21.3 us  [the longest x2 12.8 us: project(): pl.pallas_call(project_kernel, grid_spec=pltpu.PrefetchScalarGridSpec(num...]
    all_to_all x0 -> x4, starting transfers between devices: none -> 21 us  [all_to_all(): return lax.all_to_all(x, axes, split_axis=0, concat_axis=0, tiled=True)]
    dot_general x13 -> x0, matrix products: 16.6 us -> none  [the longest x3 4.53 us: conj_product(): jnp.einsum(form, left[0], right[0], preferred_element_type=jnp.float32)]
    another operation x4 -> x0, local copies, waits for them, and re-layouts: 3.62 us -> none  [per_device(): sources = jnp.stack(pieces)]
  transfers between devices with their start and end apart: 1 -> 5, of which waited for: 1 -> 4; matrix products, arithmetic and copies ran while one was open for 1% -> 2% of each run, Pallas kernels for 0% -> 7%
where the time goes in v1:
time: 115 us; the launch traced here: 114 us
  blocking collectives  40.6 us (35%)
  waiting for transfers between devices  24 us (21%)
  starting transfers between devices  22.6 us (20%)
  Pallas kernels  21.3 us (19%)
  between operations  3.24 us (3%)
  local copies, waits for them, and re-layouts  1.52 us (1%)
    all_to_all x2, blocking collectives, all_to_all(): return lax.all_to_all(x, axes, split_axis=0, concat_axis=0, tiled=True)  40.6 us
    all_to_all x4, waiting for transfers between devices, all_to_all(): return lax.all_to_all(x, axes, split_axis=0, concat_axis=0, tiled=True)  24 us
    all_to_all x4, starting transfers between devices, all_to_all(): return lax.all_to_all(x, axes, split_axis=0, concat_axis=0, tiled=True)  21 us
    pallas_call x2, Pallas kernels, project(): pl.pallas_call(project_kernel, grid_spec=pltpu.PrefetchScalarGridSpec(num...  12.8 us
    pallas_call x1, Pallas kernels, per_device(): pl.pallas_call(final_kernel, in_specs=[smem(), vmem(), smem(), vmem(), vm...  5.63 us
  transfers between devices with their start and end apart: 5, of which 4 were waited for; matrix products, arithmetic and copies ran while one was open for 2% of the time, Pallas kernels for 7%

profile of v1, /device:TPU:1, one launch (start us, length us, event | category | flops | bytes accessed | tf_op | source)
XLA Modules:
  0.0 114.4 jit_solution(10600687460254780937)
XLA Ops:
  0.0 0.0 copy-start
  0.0 0.0 copy-start.3
  0.0 6.5 %project0.1 = bf16[16,2,2,16,256]{4,3,2,1,0:T(8,128)(2,1)} custom-call(s32[4]{0:T(128)} %src_ref.7, s32[1]{0:T(128)} %bitcast.4.group_ref, bf16[2,4,1344,256]{3,2,1,0:T(8,128)(2,1)} %vec_ref.3, bf16[2,4,1344,256]{3,2,1,0:T(8,128)(2,1)} %sol_ref.3), custom_call_target="tpu_custom_call" | custom-call | flops 1400000000 | bytes 6000000 | tf_op jit(solution)/shard_map/project0/pallas_call | solution.py:98
  6.5 27.0 %all_to_all.44.recv_ref = bf16[16,2,2,16,256]{4,3,2,1,0:T(8,128)(2,1)S(1)} all-to-all(bf16[16,2,2,16,256]{4,3,2,1,0:T(8,128)(2,1)} %project0.1), channel_id=1, replica_groups=mesh['yl'=2,'x'=4,'core'=2,'yh'=2,'z'=8] {'yh','z'}, dimensions={0} | all-to-all | bytes 1048576 | tf_op jit(solution)/shard_map/all_to_all | solution.py:208
  33.6 0.0 copy-done
  33.6 0.0 copy-done.3
  33.6 1.3 %first.1 = (bf16[16,16,128]{2,1,0:T(8,128)(2,1)}, bf16[2,2,16,256]{3,2,1,0:T(8,128)(2,1)S(1)}) custom-call(s32[4]{0:T(128)S(1)} %copy-done.3, s32[1]{0:T(128)} %bitcast.4.group_ref, bf16[16,2,2,16,256]{4,3,2,1,0:T(8,128)(2,1)S(1)} %all_to_all.44.recv_ref, bf16[2,4,256,256]{3,2,1,0:T(8,128)(2,1)S(1)} %copy-done), custom_call_target="tpu_custom_call" | custom-call | tf_op jit(solution)/shard_map/first/pallas_call | solution.py:230
  34.9 7.3 %all-to-all-start.6 = ((bf16[16,16,128]{2,1,0:T(8,128)(2,1)}), bf16[16,16,128]{2,1,0:T(8,128)(2,1)S(1)}, u32[]{:S(2)}, u32[]{:S(2)}) async-start(bf16[16,16,128]{2,1,0:T(8,128)(2,1)} %get-tuple-element.32), calls=%async_computation.6 | async-start | bytes 131072 | tf_op jit(solution)/shard_map/all_to_all | solution.py:208
  42.2 0.6 dynamic_slice.13
  45.3 2.7 %all-to-all-done.6 = bf16[16,16,128]{2,1,0:T(8,128)(2,1)S(1)} async-done(((bf16[16,16,128]{2,1,0:T(8,128)(2,1)}), bf16[16,16,128]{2,1,0:T(8,128)(2,1)S(1)}, u32[]{:S(2)}, u32[]{:S(2)}) %all-to-all-start.6) | async-done | bytes 65568 | tf_op jit(solution)/shard_map/all_to_all | solution.py:208
  48.0 13.6 %all_to_all.45 = bf16[16,16,128]{2,1,0:T(8,128)(2,1)S(1)} all-to-all(bf16[16,16,128]{2,1,0:T(8,128)(2,1)S(1)} %broadcast_in_dim.54), channel_id=1, replica_groups=mesh['yl'=2,'x'=4,'core'=2,'yh'=2,'z'=8] {'yh','z'}, dimensions={0} | all-to-all | bytes 131072 | tf_op jit(solution)/shard_map/all_to_all | solution.py:208
  61.6 0.9 broadcast_in_dim.56
  62.4 3.5 %all-to-all-start.8 = ((bf16[8,256,128]{2,1,0:T(8,128)(2,1)}), bf16[8,256,128]{2,1,0:T(8,128)(2,1)S(1)}, u32[]{:S(2)}, u32[]{:S(2)}) async-start(bf16[8,256,128]{2,1,0:T(8,128)(2,1)} %broadcast_in_dim.56), calls=%async_computation.8 | async-start | bytes 1048576 | tf_op jit(solution)/shard_map/all_to_all | solution.py:208
  65.9 0.0 copy-start.1
  65.9 6.3 %project1.1 = bf16[16,2,2,16,256]{4,3,2,1,0:T(8,128)(2,1)} custom-call(s32[4]{0:T(128)S(1)} %copy-done.3, s32[1]{0:T(128)} %bitcast.4.group_ref, bf16[2,4,1344,256]{3,2,1,0:T(8,128)(2,1)} %vec_ref.3, bf16[2,4,1344,256]{3,2,1,0:T(8,128)(2,1)} %sol_ref.3), custom_call_target="tpu_custom_call" | custom-call | flops 1400000000 | bytes 6000000 | tf_op jit(solution)/shard_map/project1/pallas_call | solution.py:98
  72.2 0.0 copy-start.2
  72.2 3.2 %all-to-all-done.8 = bf16[8,256,128]{2,1,0:T(8,128)(2,1)S(1)} async-done(((bf16[8,256,128]{2,1,0:T(8,128)(2,1)}), bf16[8,256,128]{2,1,0:T(8,128)(2,1)S(1)}, u32[]{:S(2)}, u32[]{:S(2)}) %all-to-all-start.8) | async-done | bytes 524320 | tf_op jit(solution)/shard_map/all_to_all | solution.py:208
  75.4 3.6 %all-to-all-start.3 = ((bf16[16,2,2,16,256]{4,3,2,1,0:T(8,128)(2,1)}), bf16[16,2,2,16,256]{4,3,2,1,0:T(8,128)(2,1)S(1)}, u32[]{:S(2)}, u32[]{:S(2)}) async-start(bf16[16,2,2,16,256]{4,3,2,1,0:T(8,128)(2,1)} %project1.1), calls=%async_computation.3 | async-start | bytes 1048576 | tf_op jit(solution)/shard_map/all_to_all | solution.py:208
  79.0 0.2 fusion.1
  79.2 1.5 %collective-permute-start.1 = (bf16[8,256,128]{2,1,0:T(8,128)(2,1)S(1)}, bf16[8,256,128]{2,1,0:T(8,128)(2,1)S(1)}, u32[]{:S(2)}, u32[]{:S(2)}) collective-permute-start(bf16[8,256,128]{2,1,0:T(8,128)(2,1)S(1)} %all-to-all-done.8), channel_id=1, source_target_pairs={{0,16},{16,0},{1,17},{17,1},{2,18},{18,2},{3,19},{19,3},{4,20},{20... | collective-permute-start | bytes 1572872 | tf_op jit(solution)/shard_map/ppermute | solution.py:218
  80.8 0.2 convert_reduce_fusion
  81.0 0.6 broadcast_compare_fusion
  82.2 10.9 %all-to-all-done.3.recv_ref = bf16[16,2,2,16,256]{4,3,2,1,0:T(8,128)(2,1)S(1)} async-done(((bf16[16,2,2,16,256]{4,3,2,1,0:T(8,128)(2,1)}), bf16[16,2,2,16,256]{4,3,2,1,0:T(8,128)(2,1)S(1)}, u32[]{:S(2)}, u32[]{:S(2)}) %all-to-all-start.3) | async-done | bytes 524320 | tf_op jit(solution)/shard_map/all_to_all | solution.py:208
  93.2 0.0 copy-done.1
  93.2 1.6 %second.1 = (bf16[16,16,128]{2,1,0:T(8,128)(2,1)}, bf16[16,2,16,256]{3,2,1,0:T(8,128)(2,1)}) custom-call(s32[4]{0:T(128)S(1)} %copy-done.3, s32[1]{0:T(128)} %bitcast.4.group_ref, s32[16,16]{1,0:T(8,128)S(1)} %copy-done.1, bf16[16,2,2,16,256]{4,3,2,1,0:T(8,128)(2,1)S(1)} %all-to-all-done.3.recv_ref, bf16[2,4,256,256]{3,2,1,0:T(8,128)(2,1)S(1)} %copy-done, ...), custom_call_target="tpu_custom_call" | custom-call | tf_op jit(solution)/shard_map/second/pallas_call | solution.py:243
  94.8 0.0 collective-permute-done.1
  94.8 6.7 %all-to-all-start.5 = ((bf16[16,2,16,256]{3,2,1,0:T(8,128)(2,1)}), bf16[16,2,16,256]{3,2,1,0:T(8,128)(2,1)S(1)}, u32[]{:S(2)}, u32[]{:S(2)}) async-start(bf16[16,2,16,256]{3,2,1,0:T(8,128)(2,1)} %get-tuple-element.31), calls=%async_computation.5 | async-start | bytes 524288 | tf_op jit(solution)/shard_map/all_to_all | solution.py:208
  101.5 0.1 pad_add_fusion.where_ref
  101.6 7.2 %all-to-all-done.5.weighted_ref = bf16[16,2,16,256]{3,2,1,0:T(8,128)(2,1)S(1)} async-done(((bf16[16,2,16,256]{3,2,1,0:T(8,128)(2,1)}), bf16[16,2,16,256]{3,2,1,0:T(8,128)(2,1)S(1)}, u32[]{:S(2)}, u32[]{:S(2)}) %all-to-all-start.5) | async-done | bytes 262176 | tf_op jit(solution)/shard_map/all_to_all | solution.py:208
  108.7 0.0 copy-done.2
  108.7 5.6 %final.1 = bf16[16,2,16,256]{3,2,1,0:T(8,128)(2,1)} custom-call(s32[16,16]{1,0:T(8,128)S(1)} %copy-done.1, s32[1,64]{1,0:T(1,128)S(1)} %bitcast.11, s32[2]{0:T(128)S(1)} %pad_add_fusion.where_ref, bf16[16,2,16,256]{3,2,1,0:T(8,128)(2,1)S(1)} %all-to-all-done.5.weighted_ref, bf16[8,256,128]{2,1,0:T(8,128)(2,1)S(1)} %get-tuple-element.34.own_ref, ...), custom_call_target="tpu_custom_call" | custom-call | tf_op jit(solution)/shard_map/final/pallas_call | solution.py:275
  (5 shorter events, 0.0 us)
Async XLA Ops:
  0.0 33.6 %copy-start = (bf16[2,4,256,256]{3,2,1,0:T(8,128)(2,1)S(1)}, bf16[2,4,256,256]{3,2,1,0:T(8,128)(2,1)}, u32[]{:S(2)}) copy-start(bf16[2,4,256,256]{3,2,1,0:T(8,128)(2,1)} %elem_ref.3) | copy-start | bytes 3145732
  0.0 33.6 %copy-start.3 = (s32[4]{0:T(128)S(1)}, s32[4]{0:T(128)}, u32[]{:S(2)}) copy-start(s32[4]{0:T(128)} %src_ref.7) | copy-start | bytes 52
  34.9 13.1 %all-to-all-start.6 = ((bf16[16,16,128]{2,1,0:T(8,128)(2,1)}), bf16[16,16,128]{2,1,0:T(8,128)(2,1)S(1)}, u32[]{:S(2)}, u32[]{:S(2)}) async-start(bf16[16,16,128]{2,1,0:T(8,128)(2,1)} %get-tuple-element.32), calls=%async_computation.6 | async-start | bytes 131072 | tf_op jit(solution)/shard_map/all_to_all | solution.py:208
  62.4 13.0 %all-to-all-start.8 = ((bf16[8,256,128]{2,1,0:T(8,128)(2,1)}), bf16[8,256,128]{2,1,0:T(8,128)(2,1)S(1)}, u32[]{:S(2)}, u32[]{:S(2)}) async-start(bf16[8,256,128]{2,1,0:T(8,128)(2,1)} %broadcast_in_dim.56), calls=%async_computation.8 | async-start | bytes 1048576 | tf_op jit(solution)/shard_map/all_to_all | solution.py:208
  65.9 27.3 %copy-start.1 = (s32[16,16]{1,0:T(8,128)S(1)}, s32[16,16]{1,0:T(8,128)}, u32[]{:S(2)}) copy-start(s32[16,16]{1,0:T(8,128)} %owner_ref.3) | copy-start | bytes 3076
  72.2 36.5 %copy-start.2 = (s32[64]{0:T(128)S(1)}, s32[64]{0:T(128)}, u32[]{:S(2)}) copy-start(s32[64]{0:T(128)} %param.13) | copy-start | bytes 772
  75.4 17.8 %all-to-all-start.3 = ((bf16[16,2,2,16,256]{4,3,2,1,0:T(8,128)(2,1)}), bf16[16,2,2,16,256]{4,3,2,1,0:T(8,128)(2,1)S(1)}, u32[]{:S(2)}, u32[]{:S(2)}) async-start(bf16[16,2,2,16,256]{4,3,2,1,0:T(8,128)(2,1)} %project1.1), calls=%async_computation.3 | async-start | bytes 1048576 | tf_op jit(solution)/shard_map/all_to_all | solution.py:208
  79.2 15.6 %collective-permute-start.1 = (bf16[8,256,128]{2,1,0:T(8,128)(2,1)S(1)}, bf16[8,256,128]{2,1,0:T(8,128)(2,1)S(1)}, u32[]{:S(2)}, u32[]{:S(2)}) collective-permute-start(bf16[8,256,128]{2,1,0:T(8,128)(2,1)S(1)} %all-to-all-done.8), channel_id=1, source_target_pairs={{0,16},{16,0},{1,17},{17,1},{2,18},{18,2},{3,19},{19,3},{4,20},{20... | collective-permute-start | bytes 1572872 | tf_op jit(solution)/shard_map/ppermute | solution.py:218
  94.8 13.9 %all-to-all-start.5 = ((bf16[16,2,16,256]{3,2,1,0:T(8,128)(2,1)}), bf16[16,2,16,256]{3,2,1,0:T(8,128)(2,1)S(1)}, u32[]{:S(2)}, u32[]{:S(2)}) async-start(bf16[16,2,16,256]{3,2,1,0:T(8,128)(2,1)} %get-tuple-element.31), calls=%async_computation.5 | async-start | bytes 524288 | tf_op jit(solution)/shard_map/all_to_all | solution.py:208

commit v2 on v0

v2 whole, which is shorter than its diff:
```python
import functools

import jax
import jax.numpy as jnp
from jax import lax
from jax.experimental import pallas as pl
from jax.experimental.pallas import tpu as pltpu
from jax.sharding import Mesh
from jax.sharding import PartitionSpec as P

TM = ("yl", "x", "core")
SPACE = ("yh", "z")
TD = 4
NS = 4
NC = 16
NEV = 256
SC = 256
WIDTH = 16
SPINS = 4
LANES = 128
F32 = jnp.float32
BF16 = jnp.bfloat16
PARAMS = pltpu.CompilerParams(vmem_limit_bytes=40 * 2**20)


def smem():
    return pl.BlockSpec(memory_space=pltpu.SMEM)


def vmem():
    return pl.BlockSpec(memory_space=pltpu.VMEM)


def project_kernel(vec_hbm, sol_hbm, out_ref, vec_ref, sol_ref, sems):
    copies = []
    for t in range(TD):
        for part in range(2):
            copies.append(pltpu.make_async_copy(vec_hbm.at[part, t], vec_ref.at[t, part], sems.at[t, part, 0]))
            copies.append(pltpu.make_async_copy(sol_hbm.at[part, t], sol_ref.at[t, part], sems.at[t, part, 1]))
    for copy in copies:
        copy.start()
    dims = (((0,), (0,)), ((), ()))
    for t in range(TD):
        for copy in copies[4 * t : 4 * t + 4]:
            copy.wait()
        depth = vec_ref.shape[2]
        sol = sol_ref[t].reshape(2 * depth, SC)
        straight = vec_ref[t].reshape(2 * depth, NEV)
        turned = jnp.concatenate([-vec_ref[t, 1], vec_ref[t, 0]], axis=0)
        for part, right in enumerate((straight, turned)):
            value = lax.dot_general(sol, right, dims, preferred_element_type=F32).astype(BF16)
            out_ref[:, t, part] = value.reshape(NC, WIDTH, NEV)


def project(eigvecs, solutions):
    depth = eigvecs.shape[2]
    return pl.pallas_call(
        project_kernel,
        in_specs=[pl.BlockSpec(memory_space=pl.ANY)] * 2,
        out_specs=vmem(),
        out_shape=jax.ShapeDtypeStruct((NC, TD, 2, WIDTH, NEV), BF16),
        scratch_shapes=[
            pltpu.VMEM((TD, 2, depth, NEV), BF16),
            pltpu.VMEM((TD, 2, depth, SC), BF16),
            pltpu.SemaphoreType.DMA((TD, 2, 2)),
        ],
        compiler_params=pltpu.CompilerParams(vmem_limit_bytes=58 * 2**20),
        cost_estimate=pl.CostEstimate(flops=2_800_000_000, bytes_accessed=12_000_000, transcendentals=0),
        name="project",
    )(eigvecs, solutions)


def masks_kernel(src_ref, owner_ref, place_ref, root_ref, source_ref):
    me = lax.axis_index(TM)
    full = functools.partial(jnp.full, (8, LANES), dtype=jnp.int32)
    for s in range(NS):
        for t in range(TD):
            place_ref[s * TD + t] = full((lax.rem(src_ref[s], TD) == t).astype(jnp.int32))
    mine = lax.div(src_ref[lax.div(me, 4)], TD)
    for e in range(NC):
        root_ref[e] = full((mine == e).astype(jnp.int32))
        source = jnp.int32(0)
        for j in range(TD * NS):
            source = jnp.where(owner_ref[e, j] == me, j % NS, source)
        source_ref[e] = full(source)


def reduce_kernel(place_ref, recv_ref, total_ref, scatter_ref):
    totals = []
    for t in range(TD):
        total = recv_ref[0, t].astype(F32)
        for c in range(1, NC):
            total = total + recv_ref[c, t].astype(F32)
        total_ref[t] = total.astype(BF16)
        totals.append(total)
    for s in range(NS):
        for part in range(2):
            for side in range(2):
                lanes = slice(side * LANES, (side + 1) * LANES)
                rows = totals[0][part, :, lanes]
                for t in range(1, TD):
                    mask = place_ref[s * TD + t]
                    rows = jnp.where(jnp.concatenate([mask, mask]) != 0, totals[t][part, :, lanes], rows)
                scatter_ref[(s * 2 + part) * 2 + side] = rows.astype(BF16)


def weigh_kernel(owner_ref, total_ref, elem_ref, out_ref, all_ref):
    for t in range(TD):
        both = total_ref[t].reshape(2 * WIDTH, NEV)
        by_real = jnp.dot(both, elem_ref[0, t], preferred_element_type=F32)
        by_imag = jnp.dot(both, elem_ref[1, t], preferred_element_type=F32)
        all_ref[t, :WIDTH] = (by_real[:WIDTH] + by_imag[WIDTH:]).astype(BF16)
        all_ref[t, WIDTH:] = (by_real[WIDTH:] - by_imag[:WIDTH]).astype(BF16)
    group = lax.axis_index(TM)
    for j in range(TD * NS):
        out_ref[owner_ref[group, j]] = all_ref[j // NS]


def pick_kernel(root_ref, parts_ref, out_ref):
    part = parts_ref[0].astype(F32)
    for e in range(1, NC):
        mask = root_ref[e]
        part = jnp.where(jnp.concatenate([mask, mask]) != 0, parts_ref[e].astype(F32), part)
    part = part.astype(BF16)
    for c in range(NC):
        out_ref[c] = part


def pack_kernel(order_ref, rows_ref, weighted_ref, out_ref):
    order = order_ref[...]
    wide = jnp.concatenate([order + spin * (SC // SPINS) for spin in range(SPINS)], axis=1)
    chosen = (lax.broadcasted_iota(jnp.int32, (SC, SC), 0) == wide).astype(BF16)
    rows = rows_ref[...].reshape(SC, LANES)
    dims = (((0,), (0,)), ((), ()))
    part = lax.dot_general(rows, chosen, dims, preferred_element_type=F32).astype(BF16)
    part = part.reshape(4, 2 * WIDTH, SC)
    for pair in range(8):
        out_ref[pair, :4] = part
        out_ref[pair, 4:] = weighted_ref[2 * pair : 2 * pair + 2]


def final_kernel(source_ref, own_ref, other_ref, out_ref, sources_ref, left_ref, sum_ref):
    side = lax.axis_index("core")
    refs = ((own_ref, side), (other_ref, 1 - side))
    for k in range(2 * NS):
        for ref, at in refs:
            rows = pl.ds(pl.multiple_of(at * LANES, LANES), LANES)
            sources_ref[k, rows] = ref[k, :4].reshape(LANES, SC)
    block = 2 * WIDTH
    for pair in range(8):
        for which, (ref, at) in enumerate(refs):
            left_ref[which * 8 + pair] = ref[pair, 4 + side]
    left = left_ref[...].reshape(NC * block, NEV)
    for s in range(NS):
        for part in range(2):
            value = jnp.dot(left, sources_ref[s * 2 + part], preferred_element_type=F32)
            value = value.reshape(NC, block, SC)
            if s == 0:
                sum_ref[part] = value
                continue
            for which, (ref, at) in enumerate(refs):
                for pair in range(8):
                    row = which * 8 + pair
                    mask = source_ref[2 * pair + at] == s
                    mask = jnp.tile(mask, (block // 8, SC // LANES))
                    sum_ref[part, row] = jnp.where(mask, value[row], sum_ref[part, row])
    scale = (2.0 * NEV) ** (-0.5)
    for pair in range(8):
        for which, (ref, at) in enumerate(refs):
            e = 2 * pair + at
            by_real = sum_ref[0, which * 8 + pair]
            by_imag = sum_ref[1, which * 8 + pair]
            out_ref[e, 0] = ((by_real[:WIDTH] + by_imag[WIDTH:]) * scale).astype(BF16)
            out_ref[e, 1] = ((by_imag[:WIDTH] - by_real[WIDTH:]) * scale).astype(BF16)


def all_to_all(x, axes):
    return lax.all_to_all(x, axes, split_axis=0, concat_axis=0, tiled=True)


def per_device(eigvecs, solutions, elementals, source_list, pair_owner, dilution_order):
    mask = jax.ShapeDtypeStruct((NC, 8, LANES), jnp.int32)
    place, root, source = pl.pallas_call(
        masks_kernel,
        in_specs=[smem(), smem()],
        out_specs=[vmem()] * 3,
        out_shape=[mask] * 3,
        compiler_params=PARAMS,
        name="masks",
    )(source_list, pair_owner)

    recv = all_to_all(project(eigvecs, solutions), SPACE)
    total, scatter = pl.pallas_call(
        reduce_kernel,
        in_specs=[vmem()] * 2,
        out_specs=[vmem()] * 2,
        out_shape=[
            jax.ShapeDtypeStruct((TD, 2, WIDTH, NEV), BF16),
            jax.ShapeDtypeStruct((NC, WIDTH, LANES), BF16),
        ],
        compiler_params=PARAMS,
        name="reduce",
    )(place, recv)

    picked = pl.pallas_call(
        pick_kernel,
        in_specs=[vmem()] * 2,
        out_specs=vmem(),
        out_shape=jax.ShapeDtypeStruct((NC, WIDTH, LANES), BF16),
        compiler_params=PARAMS,
        name="pick",
    )(root, all_to_all(scatter, TM))
    rows = all_to_all(picked, SPACE)

    weighted = pl.pallas_call(
        weigh_kernel,
        in_specs=[smem(), vmem(), vmem()],
        out_specs=vmem(),
        out_shape=jax.ShapeDtypeStruct((NC, 2 * WIDTH, NEV), BF16),
        scratch_shapes=[pltpu.VMEM((TD, 2 * WIDTH, NEV), BF16)],
        compiler_params=PARAMS,
        cost_estimate=pl.CostEstimate(flops=70_000_000, bytes_accessed=2_000_000, transcendentals=0),
        name="weigh",
    )(pair_owner, total, elementals)

    packed = pl.pallas_call(
        pack_kernel,
        in_specs=[vmem()] * 3,
        out_specs=vmem(),
        out_shape=jax.ShapeDtypeStruct((8, 6, 2 * WIDTH, NEV), BF16),
        compiler_params=PARAMS,
        name="pack",
    )(dilution_order.reshape(1, -1), rows, weighted)
    own = all_to_all(packed, ("yl", "x"))
    other = lax.ppermute(own, "core", [(0, 1), (1, 0)])

    return pl.pallas_call(
        final_kernel,
        in_specs=[vmem()] * 3,
        out_specs=vmem(),
        out_shape=jax.ShapeDtypeStruct((NC, 2, WIDTH, SC), BF16),
        scratch_shapes=[
            pltpu.VMEM((2 * NS, NEV, SC), BF16),
            pltpu.VMEM((NC, 2 * WIDTH, NEV), BF16),
            pltpu.VMEM((2, NC, 2 * WIDTH, SC), F32),
        ],
        compiler_params=PARAMS,
        name="final",
    )(source, own, other)


def solution(mesh):
    fine = Mesh(mesh.devices.reshape(2, 4, 2, 2, 8), TM + SPACE)
    in_specs = (
        P(None, TM, SPACE, None),
        P(None, TM, SPACE, None),
        P(None, TM, None, None),
        P(),
        P(),
        P(),
    )
    return jax.shard_map(
        per_device, mesh=fine, in_specs=in_specs, out_specs=P(TM, None, SPACE, None), check_vma=False
    )
```

time: 282 us -> 92.8 us (0.33)
  waiting for transfers between devices: 131 us -> 35.8 us
  blocking collectives: 98.8 us -> 26.7 us
  between operations: 24 us -> 0.09 us
  starting transfers between devices: 0.01 us -> 18.7 us
  matrix products: 16.6 us -> 0 us
  Pallas kernels: 0 us -> 11.2 us
  local copies, waits for them, and re-layouts: 9.31 us -> 0.02 us
    psum x1 -> x0, waiting for transfers between devices: 131 us -> none  [from_root(): return lax.psum(jnp.where(mine, x, jnp.zeros_like(x)), axis)]
    psum x1 -> x0, blocking collectives: 86.1 us -> none  [per_device(): summed = lax.psum(partial_value, 'space').astype(jnp.bfloat16)]
    all_to_all x0 -> x2, waiting for transfers between devices: none -> 33.9 us  [all_to_all(): return lax.all_to_all(x, axes, split_axis=0, concat_axis=0, tiled=True)]
    dot_general x13 -> x0, matrix products: 16.6 us -> none  [the longest x3 4.53 us: conj_product(): jnp.einsum(form, left[0], right[0], preferred_element_type=jnp.float32)]
    all_to_all x0 -> x2, starting transfers between devices: none -> 16.5 us  [all_to_all(): return lax.all_to_all(x, axes, split_axis=0, concat_axis=0, tiled=True)]
    all_to_all x1 -> x2, blocking collectives: 12.8 us -> 26.7 us  [all_to_all(): return lax.all_to_all(x, axes, split_axis=0, concat_axis=0, tiled=True)]
    pallas_call x0 -> x7, Pallas kernels: none -> 11.2 us  [the longest x1 6.7 us: project(): pl.pallas_call(project_kernel, in_specs=[pl.BlockSpec(memory_space=pl.ANY...]
    another operation x4 -> x0, local copies, waits for them, and re-layouts: 3.62 us -> none  [per_device(): sources = jnp.stack(pieces)]
  transfers between devices with their start and end apart: 1 -> 3, of which waited for: 1 -> 3; matrix products, arithmetic and copies ran while one was open for 1% -> 0% of each run, Pallas kernels for 0% -> 2%
where the time goes in v2:
time: 92.8 us; the launch traced here: 92.5 us
  waiting for transfers between devices  35.8 us (39%)
  blocking collectives  26.7 us (29%)
  starting transfers between devices  18.7 us (20%)
  Pallas kernels  11.2 us (12%)
    all_to_all x2, waiting for transfers between devices, all_to_all(): return lax.all_to_all(x, axes, split_axis=0, concat_axis=0, tiled=True)  33.9 us
    all_to_all x2, blocking collectives, all_to_all(): return lax.all_to_all(x, axes, split_axis=0, concat_axis=0, tiled=True)  26.7 us
    all_to_all x2, starting transfers between devices, all_to_all(): return lax.all_to_all(x, axes, split_axis=0, concat_axis=0, tiled=True)  16.5 us
    pallas_call x1, Pallas kernels, project(): pl.pallas_call(project_kernel, in_specs=[pl.BlockSpec(memory_space=pl.ANY...  6.7 us
    ppermute x1, starting transfers between devices, per_device(): other = lax.ppermute(own, 'core', [(0, 1), (1, 0)])  2.2 us
    ppermute x1, waiting for transfers between devices, per_device(): other = lax.ppermute(own, 'core', [(0, 1), (1, 0)])  1.91 us
  transfers between devices with their start and end apart: 3, of which 3 were waited for; matrix products, arithmetic and copies ran while one was open for 0% of the time, Pallas kernels for 2%

profile of v2, /device:TPU:1, one launch (start us, length us, event | category | flops | bytes accessed | tf_op | source)
XLA Modules:
  0.0 92.5 jit_solution(9649517578196495031)
XLA Ops:
  0.0 0.0 copy-start.1
  0.0 0.0 copy-start.3
  0.0 0.0 copy-start
  0.0 0.0 copy-start.2
  0.0 6.7 %project.1 = bf16[16,4,2,16,256]{4,3,2,1,0:T(8,128)(2,1)} custom-call(bf16[2,4,1344,256]{3,2,1,0:T(8,128)(2,1)} %vec_hbm.1, bf16[2,4,1344,256]{3,2,1,0:T(8,128)(2,1)} %sol_hbm.1), custom_call_target="tpu_custom_call" | custom-call | flops 2800000000 | bytes 12000000 | tf_op jit(solution)/shard_map/project/pallas_call | solution.py:57
  6.7 11.8 %all-to-all-start = ((bf16[16,4,2,16,256]{4,3,2,1,0:T(8,128)(2,1)}), bf16[16,4,2,16,256]{4,3,2,1,0:T(8,128)(2,1)S(1)}, u32[]{:S(2)}, u32[]{:S(2)}) async-start(bf16[16,4,2,16,256]{4,3,2,1,0:T(8,128)(2,1)} %project.1), calls=%async_computation | async-start | bytes 2097152 | tf_op jit(solution)/shard_map/all_to_all | solution.py:178
  18.5 0.0 copy-done.1
  18.5 0.0 copy-done.3
  18.5 0.9 masks.1
  19.4 26.0 %all-to-all-done.recv_ref = bf16[16,4,2,16,256]{4,3,2,1,0:T(8,128)(2,1)S(1)} async-done(((bf16[16,4,2,16,256]{4,3,2,1,0:T(8,128)(2,1)}), bf16[16,4,2,16,256]{4,3,2,1,0:T(8,128)(2,1)S(1)}, u32[]{:S(2)}, u32[]{:S(2)}) %all-to-all-start) | async-done | bytes 1048608 | tf_op jit(solution)/shard_map/all_to_all | solution.py:178
  45.4 0.2 reduce.1
  45.6 12.6 %all_to_all.20.parts_ref = bf16[16,16,128]{2,1,0:T(8,128)(2,1)S(1)} all-to-all(bf16[16,16,128]{2,1,0:T(8,128)(2,1)S(1)} %get-tuple-element.13), channel_id=1, replica_groups=mesh['yl'=2,'x'=4,'core'=2,'yh'=2,'z'=8] {'yl','x','core'}, dimensions={0} | all-to-all | bytes 131072 | tf_op jit(solution)/shard_map/all_to_all | solution.py:178
  58.2 0.6 pick.1
  58.9 4.7 %all-to-all-start.2 = ((bf16[16,16,128]{2,1,0:T(8,128)(2,1)}), bf16[16,16,128]{2,1,0:T(8,128)(2,1)S(1)}, u32[]{:S(2)}, u32[]{:S(2)}) async-start(bf16[16,16,128]{2,1,0:T(8,128)(2,1)} %pick.1), calls=%async_computation.2 | async-start | bytes 131072 | tf_op jit(solution)/shard_map/all_to_all | solution.py:178
  63.6 0.0 copy-done
  63.6 1.0 %weigh.1.weighted_ref = bf16[16,32,256]{2,1,0:T(8,128)(2,1)S(1)} custom-call(s32[16,16]{1,0:T(8,128)S(1)} %copy-done.1, bf16[4,2,16,256]{3,2,1,0:T(8,128)(2,1)S(1)} %get-tuple-element.14.total_ref, bf16[2,4,256,256]{3,2,1,0:T(8,128)(2,1)S(1)} %copy-done), custom_call_target="tpu_custom_call" | custom-call | flops 70000000 | bytes 2000000 | tf_op jit(solution)/shard_map/weigh/pallas_call | solution.py:215
  64.6 7.9 %all-to-all-done.2.rows_ref = bf16[16,16,128]{2,1,0:T(8,128)(2,1)S(1)} async-done(((bf16[16,16,128]{2,1,0:T(8,128)(2,1)}), bf16[16,16,128]{2,1,0:T(8,128)(2,1)S(1)}, u32[]{:S(2)}, u32[]{:S(2)}) %all-to-all-start.2) | async-done | bytes 65568 | tf_op jit(solution)/shard_map/all_to_all | solution.py:178
  72.5 0.0 copy-done.2
  72.5 0.3 pack.1
  72.8 14.1 %all_to_all.21.own_ref = bf16[8,6,32,256]{3,2,1,0:T(8,128)(2,1)S(1)} all-to-all(bf16[8,6,32,256]{3,2,1,0:T(8,128)(2,1)S(1)} %pack.1), channel_id=1, replica_groups=mesh['yl'=2,'x'=4,'core'=2,'yh'=2,'z'=8] {'yl','x'}, dimensions={0} | all-to-all | bytes 1572864 | tf_op jit(solution)/shard_map/all_to_all | solution.py:178
  86.8 2.2 %collective-permute-start = (bf16[8,6,32,256]{3,2,1,0:T(8,128)(2,1)S(1)}, bf16[8,6,32,256]{3,2,1,0:T(8,128)(2,1)S(1)}, u32[]{:S(2)}, u32[]{:S(2)}) collective-permute-start(bf16[8,6,32,256]{3,2,1,0:T(8,128)(2,1)S(1)} %all_to_all.21.own_ref), channel_id=1, source_target_pairs={{0,16},{16,0},{1,17},{17,1},{2,18},{18,2},{3,19},{19,3},{4,20},{20... | collective-permute-start | bytes 2359304 | tf_op jit(solution)/shard_map/ppermute | solution.py:235
  89.0 1.9 %collective-permute-done.other_ref = bf16[8,6,32,256]{3,2,1,0:T(8,128)(2,1)S(1)} collective-permute-done((bf16[8,6,32,256]{3,2,1,0:T(8,128)(2,1)S(1)}, bf16[8,6,32,256]{3,2,1,0:T(8,128)(2,1)S(1)}, u32[]{:S(2)}, u32[]{:S(2)}) %collective-permute-start) | collective-permute-done | bytes 786464 | tf_op jit(solution)/shard_map/ppermute | solution.py:235
  90.9 1.5 %final.1 = bf16[16,2,16,256]{3,2,1,0:T(8,128)(2,1)} custom-call(s32[16,8,128]{2,1,0:T(8,128)S(1)} %get-tuple-element.10.source_ref, bf16[8,6,32,256]{3,2,1,0:T(8,128)(2,1)S(1)} %all_to_all.21.own_ref, bf16[8,6,32,256]{3,2,1,0:T(8,128)(2,1)S(1)} %collective-permute-done.other_ref), custom_call_target="tpu_custom_call" | custom-call | tf_op jit(solution)/shard_map/final/pallas_call | solution.py:237
Async XLA Ops:
  0.0 18.5 %copy-start.1 = (s32[16,16]{1,0:T(8,128)S(1)}, s32[16,16]{1,0:T(8,128)}, u32[]{:S(2)}) copy-start(s32[16,16]{1,0:T(8,128)} %owner_ref.3) | copy-start | bytes 3076
  0.0 18.5 %copy-start.3 = (s32[4]{0:T(128)S(1)}, s32[4]{0:T(128)}, u32[]{:S(2)}) copy-start(s32[4]{0:T(128)} %src_ref.1) | copy-start | bytes 52
  0.0 63.6 %copy-start = (bf16[2,4,256,256]{3,2,1,0:T(8,128)(2,1)S(1)}, bf16[2,4,256,256]{3,2,1,0:T(8,128)(2,1)}, u32[]{:S(2)}) copy-start(bf16[2,4,256,256]{3,2,1,0:T(8,128)(2,1)} %elem_ref.1) | copy-start | bytes 3145732
  0.0 72.5 %copy-start.2 = (s32[64]{0:T(128)S(1)}, s32[64]{0:T(128)}, u32[]{:S(2)}) copy-start(s32[64]{0:T(128)} %param.11) | copy-start | bytes 772
  6.7 38.7 %all-to-all-start = ((bf16[16,4,2,16,256]{4,3,2,1,0:T(8,128)(2,1)}), bf16[16,4,2,16,256]{4,3,2,1,0:T(8,128)(2,1)S(1)}, u32[]{:S(2)}, u32[]{:S(2)}) async-start(bf16[16,4,2,16,256]{4,3,2,1,0:T(8,128)(2,1)} %project.1), calls=%async_computation | async-start | bytes 2097152 | tf_op jit(solution)/shard_map/all_to_all | solution.py:178
  58.9 13.6 %all-to-all-start.2 = ((bf16[16,16,128]{2,1,0:T(8,128)(2,1)}), bf16[16,16,128]{2,1,0:T(8,128)(2,1)S(1)}, u32[]{:S(2)}, u32[]{:S(2)}) async-start(bf16[16,16,128]{2,1,0:T(8,128)(2,1)} %pick.1), calls=%async_computation.2 | async-start | bytes 131072 | tf_op jit(solution)/shard_map/all_to_all | solution.py:178
  86.8 4.1 %collective-permute-start = (bf16[8,6,32,256]{3,2,1,0:T(8,128)(2,1)S(1)}, bf16[8,6,32,256]{3,2,1,0:T(8,128)(2,1)S(1)}, u32[]{:S(2)}, u32[]{:S(2)}) collective-permute-start(bf16[8,6,32,256]{3,2,1,0:T(8,128)(2,1)S(1)} %all_to_all.21.own_ref), channel_id=1, source_target_pairs={{0,16},{16,0},{1,17},{17,1},{2,18},{18,2},{3,19},{19,3},{4,20},{20... | collective-permute-start | bytes 2359304 | tf_op jit(solution)/shard_map/ppermute | solution.py:235

commit v3 on v2

v3 whole, which is shorter than its diff:
```python
import functools

import jax
import jax.numpy as jnp
from jax import lax
from jax.experimental import pallas as pl
from jax.experimental.pallas import tpu as pltpu
from jax.sharding import Mesh
from jax.sharding import PartitionSpec as P

TM = ("yl", "x", "core")
SPACE = ("yh", "z")
TD = 4
HALF = 2
NZ = 8
NS = 4
NC = 16
NEV = 256
SC = 256
WIDTH = 16
SPINS = 4
LANES = 128
F32 = jnp.float32
BF16 = jnp.bfloat16
PARAMS = pltpu.CompilerParams(vmem_limit_bytes=40 * 2**20)


def smem():
    return pl.BlockSpec(memory_space=pltpu.SMEM)


def vmem():
    return pl.BlockSpec(memory_space=pltpu.VMEM)


def slot_list(src, group):
    flags = []
    for t in range(TD):
        hit = src(0) == group * TD + t
        for s in range(1, NS):
            hit = jnp.logical_or(hit, src(s) == group * TD + t)
        flags.append(hit.astype(jnp.int32))
    total = flags[0] + flags[1] + flags[2] + flags[3]
    slots = []
    before = jnp.int32(0)
    for t in range(TD):
        slots.append(jnp.where(flags[t] == 1, before, total + t - before))
        before = before + flags[t]
    return slots


def slot_of(slots, t):
    out = slots[0]
    for k in range(1, TD):
        out = jnp.where(t == k, slots[k], out)
    return out


def timeslice_at(slots, place):
    out = jnp.int32(0)
    for t in range(1, TD):
        out = jnp.where(slots[t] == place, t, out)
    return out


def my_slots(src_ref):
    return slot_list(lambda s: src_ref[s], lax.axis_index(TM))


def project_kernel(half, src_ref, vec_hbm, sol_hbm, *refs):
    outs, (vec_ref, sol_ref, sems) = refs[: 1 + half * 7], refs[1 + half * 7 : 4 + half * 7]
    slots = my_slots(src_ref)
    copies = []
    for k in range(HALF):
        t = timeslice_at(slots, half * HALF + k)
        for part in range(2):
            copies.append(pltpu.make_async_copy(vec_hbm.at[part, t], vec_ref.at[k, part], sems.at[k, part, 0]))
            copies.append(pltpu.make_async_copy(sol_hbm.at[part, t], sol_ref.at[k, part], sems.at[k, part, 1]))
    for copy in copies:
        copy.start()
    dims = (((0,), (0,)), ((), ()))
    for k in range(HALF):
        for copy in copies[4 * k : 4 * k + 4]:
            copy.wait()
        depth = vec_ref.shape[2]
        sol = sol_ref[k].reshape(2 * depth, SC)
        straight = vec_ref[k].reshape(2 * depth, NEV)
        turned = jnp.concatenate([-vec_ref[k, 1], vec_ref[k, 0]], axis=0)
        for part, right in enumerate((straight, turned)):
            value = lax.dot_general(sol, right, dims, preferred_element_type=F32).astype(BF16)
            if half == 0:
                outs[0][:, k, part] = value.reshape(NC, WIDTH, NEV)
            else:
                value = value.reshape(2, NZ, WIDTH, NEV)
                for yh in range(2):
                    refs[-1][:, yh, k, part] = value[yh]
    if half == 1:
        z = lax.axis_index("z")
        for d in range(NZ):
            outs[d][...] = refs[-1][lax.rem(z + d, NZ)]


def project(half, src, eigvecs, solutions):
    depth = eigvecs.shape[2]
    scratch = [
        pltpu.VMEM((HALF, 2, depth, NEV), BF16),
        pltpu.VMEM((HALF, 2, depth, SC), BF16),
        pltpu.SemaphoreType.DMA((HALF, 2, 2)),
    ]
    if half == 0:
        shapes = [jax.ShapeDtypeStruct((NC, HALF, 2, WIDTH, NEV), BF16)]
    else:
        shapes = [jax.ShapeDtypeStruct((2, HALF, 2, WIDTH, NEV), BF16)] * NZ
        scratch.append(pltpu.VMEM((NZ, 2, HALF, 2, WIDTH, NEV), BF16))
    return pl.pallas_call(
        functools.partial(project_kernel, half),
        in_specs=[smem()] + [pl.BlockSpec(memory_space=pl.ANY)] * 2,
        out_specs=[vmem()] * len(shapes),
        out_shape=shapes,
        scratch_shapes=scratch,
        compiler_params=pltpu.CompilerParams(vmem_limit_bytes=(58, 50)[half] * 2**20),
        cost_estimate=pl.CostEstimate(flops=1_400_000_000, bytes_accessed=6_000_000, transcendentals=0),
        name="project%d" % half,
    )(src, eigvecs, solutions)


def masks_kernel(src_ref, owner_ref, place_ref, root_ref, source_ref):
    me = lax.axis_index(TM)
    slots = my_slots(src_ref)
    full = functools.partial(jnp.full, (8, LANES), dtype=jnp.int32)
    for s in range(NS):
        place = slot_of(slots, lax.rem(src_ref[s], TD))
        for k in range(TD):
            place_ref[s * TD + k] = full((place == k).astype(jnp.int32))
    mine = lax.div(src_ref[lax.div(me, 4)], TD)
    for e in range(NC):
        root_ref[e] = full((mine == e).astype(jnp.int32))
        source = jnp.int32(0)
        for j in range(TD * NS):
            source = jnp.where(owner_ref[e, j] == me, j % NS, source)
        source_ref[e] = full(source)


def scatter_sources(place_ref, half, totals, scatter_ref):
    for s in range(NS):
        for part in range(2):
            for side in range(2):
                lanes = slice(side * LANES, (side + 1) * LANES)
                rows = totals[0][part, :, lanes]
                for k in range(1, HALF):
                    mask = place_ref[s * TD + half * HALF + k]
                    rows = jnp.where(jnp.concatenate([mask, mask]) != 0, totals[k][part, :, lanes], rows)
                scatter_ref[(s * 2 + part) * 2 + side] = rows.astype(BF16)


def reduce_kernel(place_ref, recv_ref, total_ref, scatter_ref):
    totals = []
    for k in range(HALF):
        total = recv_ref[0, k].astype(F32)
        for c in range(1, NC):
            total = total + recv_ref[c, k].astype(F32)
        total_ref[k] = total.astype(BF16)
        totals.append(total)
    scatter_sources(place_ref, 0, totals, scatter_ref)


def sum_kernel(after_ref, *refs):
    del after_ref
    terms, (keep_ref, send_ref) = refs[:NZ], refs[NZ:]
    yh = lax.axis_index("yh")
    for ref, at in ((keep_ref, yh), (send_ref, 1 - yh)):
        total = terms[0][at].astype(F32)
        for term in terms[1:]:
            total = total + term[at].astype(F32)
        ref[...] = total


def second_sum(terms, after):
    keep, send = pl.pallas_call(
        sum_kernel,
        in_specs=[pl.BlockSpec(memory_space=pl.ANY)] + [vmem()] * NZ,
        out_specs=[vmem()] * 2,
        out_shape=[jax.ShapeDtypeStruct((HALF, 2, WIDTH, NEV), F32)] * 2,
        compiler_params=PARAMS,
        cost_estimate=pl.CostEstimate(flops=500_000, bytes_accessed=500_000, transcendentals=0),
        name="second_sum",
    )(after, *terms)
    return keep, lax.ppermute(send, "yh", [(0, 1), (1, 0)])


def weigh_kernel(src_ref, owner_ref, place_ref, early_ref, keep_ref, recv_ref, elem_ref, out_ref, late_ref, all_ref):
    slots = my_slots(src_ref)
    totals = [keep_ref[k] + recv_ref[k] for k in range(HALF)]
    scatter_sources(place_ref, 1, totals, late_ref)
    for k in range(TD):
        t = timeslice_at(slots, k)
        both = early_ref[k] if k < HALF else totals[k - HALF].astype(BF16)
        both = both.reshape(2 * WIDTH, NEV)
        by_real = jnp.dot(both, elem_ref[0, t], preferred_element_type=F32)
        by_imag = jnp.dot(both, elem_ref[1, t], preferred_element_type=F32)
        all_ref[k, :WIDTH] = (by_real[:WIDTH] + by_imag[WIDTH:]).astype(BF16)
        all_ref[k, WIDTH:] = (by_real[WIDTH:] - by_imag[:WIDTH]).astype(BF16)
    group = lax.axis_index(TM)
    for j in range(TD * NS):
        out_ref[owner_ref[group, j]] = all_ref[slots[j // NS]]


def pick_kernel(root_ref, parts_ref, out_ref):
    part = parts_ref[0].astype(F32)
    for e in range(1, NC):
        mask = root_ref[e]
        part = jnp.where(jnp.concatenate([mask, mask]) != 0, parts_ref[e].astype(F32), part)
    part = part.astype(BF16)
    for c in range(NC):
        out_ref[c] = part


def pack_kernel(order_ref, rows_ref, *refs):
    out_ref = refs[-1]
    order = order_ref[...]
    wide = jnp.concatenate([order + spin * (SC // SPINS) for spin in range(SPINS)], axis=1)
    chosen = (lax.broadcasted_iota(jnp.int32, (SC, SC), 0) == wide).astype(BF16)
    rows = rows_ref[...].reshape(SC, LANES)
    dims = (((0,), (0,)), ((), ()))
    part = lax.dot_general(rows, chosen, dims, preferred_element_type=F32).astype(BF16)
    part = part.reshape(4, 2 * WIDTH, SC)
    for pair in range(8):
        out_ref[pair, :4] = part
        if len(refs) > 1:
            out_ref[pair, 4:] = refs[0][2 * pair : 2 * pair + 2]


def final_kernel(source_ref, own_ref, other_ref, out_ref, sources_ref, left_ref, sum_ref):
    side = lax.axis_index("core")
    refs = ((own_ref, side), (other_ref, 1 - side))
    for k in range(2 * NS):
        for ref, at in refs:
            rows = pl.ds(pl.multiple_of(at * LANES, LANES), LANES)
            sources_ref[k, rows] = ref[k, :4].reshape(LANES, SC)
    block = 2 * WIDTH
    for pair in range(8):
        for which, (ref, at) in enumerate(refs):
            left_ref[which * 8 + pair] = ref[pair, 4 + side]
    left = left_ref[...].reshape(NC * block, NEV)
    for s in range(NS):
        for part in range(2):
            value = jnp.dot(left, sources_ref[s * 2 + part], preferred_element_type=F32)
            value = value.reshape(NC, block, SC)
            if s == 0:
                sum_ref[part] = value
                continue
            for which, (ref, at) in enumerate(refs):
                for pair in range(8):
                    row = which * 8 + pair
                    mask = source_ref[2 * pair + at] == s
                    mask = jnp.tile(mask, (block // 8, SC // LANES))
                    sum_ref[part, row] = jnp.where(mask, value[row], sum_ref[part, row])
    scale = (2.0 * NEV) ** (-0.5)
    for pair in range(8):
        for which, (ref, at) in enumerate(refs):
            e = 2 * pair + at
            by_real = sum_ref[0, which * 8 + pair]
            by_imag = sum_ref[1, which * 8 + pair]
            out_ref[e, 0] = ((by_real[:WIDTH] + by_imag[WIDTH:]) * scale).astype(BF16)
            out_ref[e, 1] = ((by_imag[:WIDTH] - by_real[WIDTH:]) * scale).astype(BF16)


def all_to_all(x, axes):
    return lax.all_to_all(x, axes, split_axis=0, concat_axis=0, tiled=True)


def spread(scatter, root):
    return pl.pallas_call(
        pick_kernel,
        in_specs=[vmem()] * 2,
        out_specs=vmem(),
        out_shape=jax.ShapeDtypeStruct((NC, WIDTH, LANES), BF16),
        compiler_params=PARAMS,
        cost_estimate=pl.CostEstimate(flops=100_000, bytes_accessed=200_000, transcendentals=0),
        name="pick",
    )(root, all_to_all(scatter, TM))


def gather(rows, order, *weighted):
    packed = pl.pallas_call(
        pack_kernel,
        in_specs=[vmem()] * (2 + len(weighted)),
        out_specs=vmem(),
        out_shape=jax.ShapeDtypeStruct((8, 4 + 2 * len(weighted), 2 * WIDTH, NEV), BF16),
        compiler_params=PARAMS,
        name="pack",
    )(order, rows, *weighted)
    own = all_to_all(packed, ("yl", "x"))
    return own, lax.ppermute(own, "core", [(0, 1), (1, 0)])


def late_sources(src):
    same = src[:, None] == src[None, :]
    earlier = jnp.arange(NS)[:, None] > jnp.arange(NS)[None, :]
    fresh = ~jnp.any(same & earlier, axis=1)
    groups = src // TD
    lower = (groups[:, None] == groups[None, :]) & (src[None, :] < src[:, None]) & fresh[None, :]
    return jnp.sum(lower.astype(jnp.int32), axis=1) >= HALF


def per_device(eigvecs, solutions, elementals, source_list, pair_owner, dilution_order):
    order = dilution_order.reshape(1, -1)
    mask = jax.ShapeDtypeStruct((NC, 8, LANES), jnp.int32)
    place, root, source = pl.pallas_call(
        masks_kernel,
        in_specs=[smem(), smem()],
        out_specs=[vmem()] * 3,
        out_shape=[mask] * 3,
        compiler_params=PARAMS,
        cost_estimate=pl.CostEstimate(flops=100_000, bytes_accessed=200_000, transcendentals=0),
        name="masks",
    )(source_list, pair_owner)

    (first,) = project(0, source_list, eigvecs, solutions)
    first, later = lax.optimization_barrier((first, source_list))
    recv = all_to_all(first, SPACE)
    early, scatter = pl.pallas_call(
        reduce_kernel,
        in_specs=[vmem()] * 2,
        out_specs=[vmem()] * 2,
        out_shape=[
            jax.ShapeDtypeStruct((HALF, 2, WIDTH, NEV), BF16),
            jax.ShapeDtypeStruct((NC, WIDTH, LANES), BF16),
        ],
        compiler_params=PARAMS,
        cost_estimate=pl.CostEstimate(flops=500_000, bytes_accessed=500_000, transcendentals=0),
        name="reduce",
    )(place, recv)

    terms = list(project(1, later, eigvecs, solutions))
    for d in range(1, NZ):
        terms[d] = lax.ppermute(terms[d], "z", [(z, (z + d) % NZ) for z in range(NZ)])
    picked = spread(scatter, root)
    rows = all_to_all(picked, SPACE)
    keep, added = second_sum(terms, picked)
    weighted, late = pl.pallas_call(
        weigh_kernel,
        in_specs=[smem(), smem()] + [vmem()] * 5,
        out_specs=[vmem()] * 2,
        out_shape=[
            jax.ShapeDtypeStruct((NC, 2 * WIDTH, NEV), BF16),
            jax.ShapeDtypeStruct((NC, WIDTH, LANES), BF16),
        ],
        scratch_shapes=[pltpu.VMEM((TD, 2 * WIDTH, NEV), BF16)],
        compiler_params=PARAMS,
        cost_estimate=pl.CostEstimate(flops=70_000_000, bytes_accessed=2_000_000, transcendentals=0),
        name="weigh",
    )(source_list, pair_owner, place, early, keep, added, elementals)

    own, other = gather(rows, order, weighted)

    is_late = late_sources(source_list)

    def again(own, other, late):
        own_late, other_late = gather(all_to_all(spread(late, root), SPACE), order)
        pick = jnp.repeat(is_late, 2)[:, None, None, None]
        own = own.at[:, :4].set(jnp.where(pick, own_late, own[:, :4]))
        other = other.at[:, :4].set(jnp.where(pick, other_late, other[:, :4]))
        return own, other

    own, other = lax.cond(jnp.any(is_late), again, lambda own, other, late: (own, other), own, other, late)

    return pl.pallas_call(
        final_kernel,
        in_specs=[vmem()] * 3,
        out_specs=vmem(),
        out_shape=jax.ShapeDtypeStruct((NC, 2, WIDTH, SC), BF16),
        scratch_shapes=[
            pltpu.VMEM((2 * NS, NEV, SC), BF16),
            pltpu.VMEM((NC, 2 * WIDTH, NEV), BF16),
            pltpu.VMEM((2, NC, 2 * WIDTH, SC), F32),
        ],
        compiler_params=PARAMS,
        name="final",
    )(source, own, other)


def solution(mesh):
    fine = Mesh(mesh.devices.reshape(2, 4, 2, 2, 8), TM + SPACE)
    in_specs = (
        P(None, TM, SPACE, None),
        P(None, TM, SPACE, None),
        P(None, TM, None, None),
        P(),
        P(),
        P(),
    )
    return jax.shard_map(
        per_device, mesh=fine, in_specs=in_specs, out_specs=P(TM, None, SPACE, None), check_vma=False
    )
```

time: 92.8 us -> 88 us (0.948)
  starting transfers between devices: 18.7 us -> 44.7 us
  waiting for transfers between devices: 35.8 us -> 12.1 us
  blocking collectives: 26.7 us -> 14.1 us
  Pallas kernels: 11.2 us -> 14.8 us
  other arithmetic: 0 us -> 1.03 us
    all_to_all x2 -> x3, waiting for transfers between devices: 33.9 us -> 8.65 us  [all_to_all(): return lax.all_to_all(x, axes, split_axis=0, concat_axis=0, tiled=True)]
    ppermute x1 -> x9, starting transfers between devices: 2.2 us -> 19.9 us  [the longest x7 13.5 us: per_device(): lax.ppermute(terms[d], 'z', [(z, (z + d) % NZ) for z in range(NZ)])]
    all_to_all x2 -> x1, blocking collectives: 26.7 us -> 14.1 us  [all_to_all(): return lax.all_to_all(x, axes, split_axis=0, concat_axis=0, tiled=True)]
    all_to_all x2 -> x3, starting transfers between devices: 16.5 us -> 24.9 us  [all_to_all(): return lax.all_to_all(x, axes, split_axis=0, concat_axis=0, tiled=True)]
    pallas_call x4 -> x6, Pallas kernels: 8.57 us -> 11.6 us  [the longest x2 9.6 us: project(): pl.pallas_call(functools.partial(project_kernel, half), in_specs=[smem()]...]
    ppermute x1 -> x9, waiting for transfers between devices: 1.91 us -> 3.46 us  [the longest x1 2.45 us: second_sum(): return (keep, lax.ppermute(send, 'yh', [(0, 1), (1, 0)]))]
  transfers between devices with their start and end apart: 3 -> 12, of which waited for: 3 -> 6; matrix products, arithmetic and copies ran while one was open for 0% -> 1% of each run, Pallas kernels for 2% -> 9%
where the time goes in v3:
time: 88 us; the launch traced here: 87.6 us
  starting transfers between devices  44.7 us (51%)
  Pallas kernels  14.8 us (17%)
  blocking collectives  14.1 us (16%)
  waiting for transfers between devices  12.1 us (14%)
  other arithmetic  1.03 us (1%)
    all_to_all x3, starting transfers between devices, all_to_all(): return lax.all_to_all(x, axes, split_axis=0, concat_axis=0, tiled=True)  24.9 us
    all_to_all x1, blocking collectives, all_to_all(): return lax.all_to_all(x, axes, split_axis=0, concat_axis=0, tiled=True)  14.1 us
    ppermute x7, starting transfers between devices, per_device(): lax.ppermute(terms[d], 'z', [(z, (z + d) % NZ) for z in range(NZ)])  13.5 us
    pallas_call x2, Pallas kernels, project(): pl.pallas_call(functools.partial(project_kernel, half), in_specs=[smem()]...  9.6 us
    all_to_all x3, waiting for transfers between devices, all_to_all(): return lax.all_to_all(x, axes, split_axis=0, concat_axis=0, tiled=True)  8.65 us
    ppermute x1, starting transfers between devices, gather(): return (own, lax.ppermute(own, 'core', [(0, 1), (1, 0)]))  4.05 us
    ppermute x1, waiting for transfers between devices, second_sum(): return (keep, lax.ppermute(send, 'yh', [(0, 1), (1, 0)]))  2.45 us
    ppermute x1, starting transfers between devices, second_sum(): return (keep, lax.ppermute(send, 'yh', [(0, 1), (1, 0)]))  2.3 us
  transfers between devices with their start and end apart: 12, of which 6 were waited for; matrix products, arithmetic and copies ran while one was open for 1% of the time, Pallas kernels for 9%

profile of v3, /device:TPU:1, one launch (start us, length us, event | category | flops | bytes accessed | tf_op | source)
XLA Modules:
  0.0 87.6 jit_solution(1048532914829442775)
XLA Ops:
  0.0 0.0 copy-start.2
  0.0 5.3 %project0.1 = bf16[16,2,2,16,256]{4,3,2,1,0:T(8,128)(2,1)} custom-call(s32[4]{0:T(128)} %src_ref.6, bf16[2,4,1344,256]{3,2,1,0:T(8,128)(2,1)} %vec_hbm.3, bf16[2,4,1344,256]{3,2,1,0:T(8,128)(2,1)} %sol_hbm.3), custom_call_target="tpu_custom_call" | custom-call | flops 1400000000 | bytes 6000000 | tf_op jit(solution)/shard_map/project0/pallas_call | solution.py:115
  5.3 11.8 %all-to-all-start.3 = ((bf16[16,2,2,16,256]{4,3,2,1,0:T(8,128)(2,1)}), bf16[16,2,2,16,256]{4,3,2,1,0:T(8,128)(2,1)S(1)}, u32[]{:S(2)}, u32[]{:S(2)}) async-start(bf16[16,2,2,16,256]{4,3,2,1,0:T(8,128)(2,1)} %project0.1), calls=%async_computation.3 | async-start | bytes 1048576 | tf_op jit(solution)/shard_map/all_to_all | solution.py:269
  17.1 0.0 copy-done.2
  17.1 0.0 copy-start.1
  17.1 0.0 copy-start
  17.1 0.0 copy-start.3
  17.1 4.3 %project1.1 = (bf16[2,2,2,16,256]{4,3,2,1,0:T(8,128)(2,1)S(1)}, bf16[2,2,2,16,256]{4,3,2,1,0:T(8,128)(2,1)S(1)}, bf16[2,2,2,16,256]{4,3,2,1,0:T(8,128)(2,1)S(1)}...) custom-call(s32[4]{0:T(128)S(1)} %copy-done.2, ...), custom_call_target="tpu_custom_call" | custom-call | flops 1400000000 | bytes 6000000 | tf_op jit(solution)/shard_map/project1/pallas_call | solution.py:115
  21.4 1.4 %collective-permute-start.1 = (bf16[2,2,2,16,256]{4,3,2,1,0:T(8,128)(2,1)S(1)}, bf16[2,2,2,16,256]{4,3,2,1,0:T(8,128)(2,1)S(1)}, u32[]{:S(2)}, u32[]{:S(2)}) collective-permute-start(bf16[2,2,2,16,256]{4,3,2,1,0:T(8,128)(2,1)S(1)} %get-tuple-element.80), channel_id=1, source_target_pairs={{0,1},{1,2},{2,3},{3,4},{4,5},{5,6},{6,7},{7,0},{8,9},{9,10},{10,1... | collective-permute-start | bytes 196616 | tf_op jit(solution)/shard_map/ppermute | solution.py:337
  22.9 2.1 %collective-permute-start.2 = (bf16[2,2,2,16,256]{4,3,2,1,0:T(8,128)(2,1)S(1)}, bf16[2,2,2,16,256]{4,3,2,1,0:T(8,128)(2,1)S(1)}, u32[]{:S(2)}, u32[]{:S(2)}) collective-permute-start(bf16[2,2,2,16,256]{4,3,2,1,0:T(8,128)(2,1)S(1)} %get-tuple-element.81), channel_id=1, source_target_pairs={{0,2},{1,3},{2,4},{3,5},{4,6},{5,7},{6,0},{7,1},{8,10},{9,11},{10,... | collective-permute-start | bytes 196616 | tf_op jit(solution)/shard_map/ppermute | solution.py:337
  25.0 0.0 copy-done.1
  25.0 0.9 %masks.1 = (s32[16,8,128]{2,1,0:T(8,128)S(1)}, s32[16,8,128]{2,1,0:T(8,128)S(1)}, s32[16,8,128]{2,1,0:T(8,128)S(1)}) custom-call(s32[4]{0:T(128)S(1)} %copy-done.2, s32[16,16]{1,0:T(8,128)S(1)} %copy-done.1), custom_call_target="tpu_custom_call" | custom-call | flops 100000 | bytes 200000 | tf_op jit(solution)/shard_map/masks/pallas_call | solution.py:309
  25.9 6.4 %all-to-all-done.3.recv_ref = bf16[16,2,2,16,256]{4,3,2,1,0:T(8,128)(2,1)S(1)} async-done(((bf16[16,2,2,16,256]{4,3,2,1,0:T(8,128)(2,1)}), bf16[16,2,2,16,256]{4,3,2,1,0:T(8,128)(2,1)S(1)}, u32[]{:S(2)}, u32[]{:S(2)}) %all-to-all-start.3) | async-done | bytes 524320 | tf_op jit(solution)/shard_map/all_to_all | solution.py:269
  32.3 0.7 reduce.5
  33.0 8.8 %all-to-all-start.4 = ((bf16[16,16,128]{2,1,0:T(8,128)(2,1)}), bf16[16,16,128]{2,1,0:T(8,128)(2,1)S(1)}, u32[]{:S(2)}, u32[]{:S(2)}) async-start(bf16[16,16,128]{2,1,0:T(8,128)(2,1)} %get-tuple-element.76), calls=%async_computation.4 | async-start | bytes 131072 | tf_op jit(solution)/shard_map/all_to_all | solution.py:269
  41.9 0.0 collective-permute-start.3
  41.9 4.2 %collective-permute-start.4 = (bf16[2,2,2,16,256]{4,3,2,1,0:T(8,128)(2,1)S(1)}, bf16[2,2,2,16,256]{4,3,2,1,0:T(8,128)(2,1)S(1)}, u32[]{:S(2)}, u32[]{:S(2)}) collective-permute-start(bf16[2,2,2,16,256]{4,3,2,1,0:T(8,128)(2,1)S(1)} %get-tuple-element.83), channel_id=1, source_target_pairs={{0,4},{1,5},{2,6},{3,7},{4,0},{5,1},{6,2},{7,3},{8,12},{9,13},{10,... | collective-permute-start | bytes 196616 | tf_op jit(solution)/shard_map/ppermute | solution.py:337
  46.1 1.1 %collective-permute-start.5 = (bf16[2,2,2,16,256]{4,3,2,1,0:T(8,128)(2,1)S(1)}, bf16[2,2,2,16,256]{4,3,2,1,0:T(8,128)(2,1)S(1)}, u32[]{:S(2)}, u32[]{:S(2)}) collective-permute-start(bf16[2,2,2,16,256]{4,3,2,1,0:T(8,128)(2,1)S(1)} %get-tuple-element.84), channel_id=1, source_target_pairs={{0,5},{1,6},{2,7},{3,0},{4,1},{5,2},{6,3},{7,4},{8,13},{9,14},{10,... | collective-permute-start | bytes 196616 | tf_op jit(solution)/shard_map/ppermute | solution.py:337
  47.2 0.0 collective-permute-done.1.refs_1_
  47.2 1.4 %collective-permute-start.6 = (bf16[2,2,2,16,256]{4,3,2,1,0:T(8,128)(2,1)S(1)}, bf16[2,2,2,16,256]{4,3,2,1,0:T(8,128)(2,1)S(1)}, u32[]{:S(2)}, u32[]{:S(2)}) collective-permute-start(bf16[2,2,2,16,256]{4,3,2,1,0:T(8,128)(2,1)S(1)} %get-tuple-element.85), channel_id=1, source_target_pairs={{0,6},{1,7},{2,0},{3,1},{4,2},{5,3},{6,4},{7,5},{8,14},{9,15},{10,... | collective-permute-start | bytes 196616 | tf_op jit(solution)/shard_map/ppermute | solution.py:337
  48.6 0.0 collective-permute-done.2.refs_2_
  48.6 3.3 %collective-permute-start.7 = (bf16[2,2,2,16,256]{4,3,2,1,0:T(8,128)(2,1)S(1)}, bf16[2,2,2,16,256]{4,3,2,1,0:T(8,128)(2,1)S(1)}, u32[]{:S(2)}, u32[]{:S(2)}) collective-permute-start(bf16[2,2,2,16,256]{4,3,2,1,0:T(8,128)(2,1)S(1)} %get-tuple-element.86), channel_id=1, source_target_pairs={{0,7},{1,0},{2,1},{3,2},{4,3},{5,4},{6,5},{7,6},{8,15},{9,8},{10,9... | collective-permute-start | bytes 196616 | tf_op jit(solution)/shard_map/ppermute | solution.py:337
  51.9 0.0 all-to-all-done.4.parts_ref
  51.9 0.7 pick.3.after_ref
  52.5 4.3 %all-to-all-start.5 = ((bf16[16,16,128]{2,1,0:T(8,128)(2,1)}), bf16[16,16,128]{2,1,0:T(8,128)(2,1)S(1)}, u32[]{:S(2)}, u32[]{:S(2)}) async-start(bf16[16,16,128]{2,1,0:T(8,128)(2,1)} %pick.3.after_ref), calls=%async_computation.5 | async-start | bytes 131072 | tf_op jit(solution)/shard_map/all_to_all | solution.py:269
  56.8 0.0 collective-permute-done.3.refs_3_
  56.8 0.0 collective-permute-done.4.refs_4_
  56.8 0.0 collective-permute-done.5.refs_5_
  56.9 0.2 collective-permute-done.6.refs_6_
  57.1 0.5 collective-permute-done.7.refs_7_
  57.6 0.1 second_sum.1
  57.7 2.3 %collective-permute-start.8 = (f32[2,2,16,256]{3,2,1,0:T(8,128)S(1)}, f32[2,2,16,256]{3,2,1,0:T(8,128)S(1)}, u32[]{:S(2)}, u32[]{:S(2)}) collective-permute-start(f32[2,2,16,256]{3,2,1,0:T(8,128)S(1)} %get-tuple-element.88), channel_id=1, source_target_pairs={{0,8},{8,0},{1,9},{9,1},{2,10},{10,2},{3,11},{11,3},{4,12},{12,4},... | collective-permute-start | bytes 196616 | tf_op jit(solution)/shard_map/ppermute | solution.py:188
  60.0 2.4 %collective-permute-done.8.recv_ref = f32[2,2,16,256]{3,2,1,0:T(8,128)S(1)} collective-permute-done((f32[2,2,16,256]{3,2,1,0:T(8,128)S(1)}, f32[2,2,16,256]{3,2,1,0:T(8,128)S(1)}, u32[]{:S(2)}, u32[]{:S(2)}) %collective-permute-start.8) | collective-permute-done | bytes 65568 | tf_op jit(solution)/shard_map/ppermute | solution.py:188
  62.4 0.0 copy-done
  62.4 1.0 %weigh.1 = (bf16[16,32,256]{2,1,0:T(8,128)(2,1)S(1)}, bf16[16,16,128]{2,1,0:T(8,128)(2,1)S(1)}) custom-call(s32[4]{0:T(128)S(1)} %copy-done.2, s32[16,16]{1,0:T(8,128)S(1)} %copy-done.1, s32[16,8,128]{2,1,0:T(8,128)S(1)} %get-tuple-element.74.place_ref, bf16[2,2,16,256]{3,2,1,0:T(8,128)(2,1)S(1)} %get-tuple-element.77.early_ref, ...), custom_call_target="tpu_custom_call" | custom-call | flops 70000000 | bytes 2000000 | tf_op jit(solution)/shard_map/weigh/pallas_call | solution.py:341
  63.5 2.2 %all-to-all-done.5.rows_ref = bf16[16,16,128]{2,1,0:T(8,128)(2,1)S(1)} async-done(((bf16[16,16,128]{2,1,0:T(8,128)(2,1)}), bf16[16,16,128]{2,1,0:T(8,128)(2,1)S(1)}, u32[]{:S(2)}, u32[]{:S(2)}) %all-to-all-start.5) | async-done | bytes 65568 | tf_op jit(solution)/shard_map/all_to_all | solution.py:269
  65.7 0.0 copy-done.3
  65.7 0.3 pack.3
  66.0 14.1 %all_to_all.35 = bf16[8,6,32,256]{3,2,1,0:T(8,128)(2,1)S(1)} all-to-all(bf16[8,6,32,256]{3,2,1,0:T(8,128)(2,1)S(1)} %pack.3), channel_id=1, replica_groups=mesh['yl'=2,'x'=4,'core'=2,'yh'=2,'z'=8] {'yl','x'}, dimensions={0} | all-to-all | bytes 1572864 | tf_op jit(solution)/shard_map/all_to_all | solution.py:269
  80.1 4.0 %collective-permute-start.9 = (bf16[8,6,32,256]{3,2,1,0:T(8,128)(2,1)S(1)}, bf16[8,6,32,256]{3,2,1,0:T(8,128)(2,1)S(1)}, u32[]{:S(2)}, u32[]{:S(2)}) collective-permute-start(bf16[8,6,32,256]{3,2,1,0:T(8,128)(2,1)S(1)} %all_to_all.35), channel_id=1, source_target_pairs={{0,16},{16,0},{1,17},{17,1},{2,18},{18,2},{3,19},{19,3},{4,20},{20... | collective-permute-start | bytes 2359304 | tf_op jit(solution)/shard_map/ppermute | solution.py:294
  84.2 0.2 fusion.1
  84.4 0.2 convert_reduce_fusion
  84.5 0.6 broadcast_compare_fusion
  85.8 0.2 collective-permute-done.9
  86.1 1.5 %final.1 = bf16[16,2,16,256]{3,2,1,0:T(8,128)(2,1)} custom-call(s32[16,8,128]{2,1,0:T(8,128)S(1)} %get-tuple-element.72.source_ref, bf16[8,6,32,256]{3,2,1,0:T(8,128)(2,1)S(1)} %get-tuple-element.91.own_ref, bf16[8,6,32,256]{3,2,1,0:T(8,128)(2,1)S(1)} %get-tuple-element.92.other_ref), custom_call_target="tpu_custom_call" | custom-call | tf_op jit(solution)/shard_map/final/pallas_call | solution.py:368
  (3 shorter events, 0.0 us)
Async XLA Ops:
  0.0 17.1 %copy-start.2 = (s32[4]{0:T(128)S(1)}, s32[4]{0:T(128)}, u32[]{:S(2)}) copy-start(s32[4]{0:T(128)} %src_ref.6) | copy-start | bytes 52
  5.3 27.0 %all-to-all-start.3 = ((bf16[16,2,2,16,256]{4,3,2,1,0:T(8,128)(2,1)}), bf16[16,2,2,16,256]{4,3,2,1,0:T(8,128)(2,1)S(1)}, u32[]{:S(2)}, u32[]{:S(2)}) async-start(bf16[16,2,2,16,256]{4,3,2,1,0:T(8,128)(2,1)} %project0.1), calls=%async_computation.3 | async-start | bytes 1048576 | tf_op jit(solution)/shard_map/all_to_all | solution.py:269
  17.1 7.9 %copy-start.1 = (s32[16,16]{1,0:T(8,128)S(1)}, s32[16,16]{1,0:T(8,128)}, u32[]{:S(2)}) copy-start(s32[16,16]{1,0:T(8,128)} %owner_ref.3) | copy-start | bytes 3076
  17.1 45.3 %copy-start = (bf16[2,4,256,256]{3,2,1,0:T(8,128)(2,1)S(1)}, bf16[2,4,256,256]{3,2,1,0:T(8,128)(2,1)}, u32[]{:S(2)}) copy-start(bf16[2,4,256,256]{3,2,1,0:T(8,128)(2,1)} %elem_ref.1) | copy-start | bytes 3145732
  17.1 48.6 %copy-start.3 = (s32[64]{0:T(128)S(1)}, s32[64]{0:T(128)}, u32[]{:S(2)}) copy-start(s32[64]{0:T(128)} %param.17) | copy-start | bytes 772
  21.4 25.8 %collective-permute-start.1 = (bf16[2,2,2,16,256]{4,3,2,1,0:T(8,128)(2,1)S(1)}, bf16[2,2,2,16,256]{4,3,2,1,0:T(8,128)(2,1)S(1)}, u32[]{:S(2)}, u32[]{:S(2)}) collective-permute-start(bf16[2,2,2,16,256]{4,3,2,1,0:T(8,128)(2,1)S(1)} %get-tuple-element.80), channel_id=1, source_target_pairs={{0,1},{1,2},{2,3},{3,4},{4,5},{5,6},{6,7},{7,0},{8,9},{9,10},{10,1... | collective-permute-start | bytes 196616 | tf_op jit(solution)/shard_map/ppermute | solution.py:337
  22.9 25.7 %collective-permute-start.2 = (bf16[2,2,2,16,256]{4,3,2,1,0:T(8,128)(2,1)S(1)}, bf16[2,2,2,16,256]{4,3,2,1,0:T(8,128)(2,1)S(1)}, u32[]{:S(2)}, u32[]{:S(2)}) collective-permute-start(bf16[2,2,2,16,256]{4,3,2,1,0:T(8,128)(2,1)S(1)} %get-tuple-element.81), channel_id=1, source_target_pairs={{0,2},{1,3},{2,4},{3,5},{4,6},{5,7},{6,0},{7,1},{8,10},{9,11},{10,... | collective-permute-start | bytes 196616 | tf_op jit(solution)/shard_map/ppermute | solution.py:337
  33.0 18.8 %all-to-all-start.4 = ((bf16[16,16,128]{2,1,0:T(8,128)(2,1)}), bf16[16,16,128]{2,1,0:T(8,128)(2,1)S(1)}, u32[]{:S(2)}, u32[]{:S(2)}) async-start(bf16[16,16,128]{2,1,0:T(8,128)(2,1)} %get-tuple-element.76), calls=%async_computation.4 | async-start | bytes 131072 | tf_op jit(solution)/shard_map/all_to_all | solution.py:269
  41.9 15.0 %collective-permute-start.3 = (bf16[2,2,2,16,256]{4,3,2,1,0:T(8,128)(2,1)S(1)}, bf16[2,2,2,16,256]{4,3,2,1,0:T(8,128)(2,1)S(1)}, u32[]{:S(2)}, u32[]{:S(2)}) collective-permute-start(bf16[2,2,2,16,256]{4,3,2,1,0:T(8,128)(2,1)S(1)} %get-tuple-element.82), channel_id=1, source_target_pairs={{0,3},{1,4},{2,5},{3,6},{4,7},{5,0},{6,1},{7,2},{8,11},{9,12},{10,... | collective-permute-start | bytes 196616 | tf_op jit(solution)/shard_map/ppermute | solution.py:337
  41.9 15.0 %collective-permute-start.4 = (bf16[2,2,2,16,256]{4,3,2,1,0:T(8,128)(2,1)S(1)}, bf16[2,2,2,16,256]{4,3,2,1,0:T(8,128)(2,1)S(1)}, u32[]{:S(2)}, u32[]{:S(2)}) collective-permute-start(bf16[2,2,2,16,256]{4,3,2,1,0:T(8,128)(2,1)S(1)} %get-tuple-element.83), channel_id=1, source_target_pairs={{0,4},{1,5},{2,6},{3,7},{4,0},{5,1},{6,2},{7,3},{8,12},{9,13},{10,... | collective-permute-start | bytes 196616 | tf_op jit(solution)/shard_map/ppermute | solution.py:337
  46.1 10.7 %collective-permute-start.5 = (bf16[2,2,2,16,256]{4,3,2,1,0:T(8,128)(2,1)S(1)}, bf16[2,2,2,16,256]{4,3,2,1,0:T(8,128)(2,1)S(1)}, u32[]{:S(2)}, u32[]{:S(2)}) collective-permute-start(bf16[2,2,2,16,256]{4,3,2,1,0:T(8,128)(2,1)S(1)} %get-tuple-element.84), channel_id=1, source_target_pairs={{0,5},{1,6},{2,7},{3,0},{4,1},{5,2},{6,3},{7,4},{8,13},{9,14},{10,... | collective-permute-start | bytes 196616 | tf_op jit(solution)/shard_map/ppermute | solution.py:337
  47.2 9.9 %collective-permute-start.6 = (bf16[2,2,2,16,256]{4,3,2,1,0:T(8,128)(2,1)S(1)}, bf16[2,2,2,16,256]{4,3,2,1,0:T(8,128)(2,1)S(1)}, u32[]{:S(2)}, u32[]{:S(2)}) collective-permute-start(bf16[2,2,2,16,256]{4,3,2,1,0:T(8,128)(2,1)S(1)} %get-tuple-element.85), channel_id=1, source_target_pairs={{0,6},{1,7},{2,0},{3,1},{4,2},{5,3},{6,4},{7,5},{8,14},{9,15},{10,... | collective-permute-start | bytes 196616 | tf_op jit(solution)/shard_map/ppermute | solution.py:337
  48.6 9.0 %collective-permute-start.7 = (bf16[2,2,2,16,256]{4,3,2,1,0:T(8,128)(2,1)S(1)}, bf16[2,2,2,16,256]{4,3,2,1,0:T(8,128)(2,1)S(1)}, u32[]{:S(2)}, u32[]{:S(2)}) collective-permute-start(bf16[2,2,2,16,256]{4,3,2,1,0:T(8,128)(2,1)S(1)} %get-tuple-element.86), channel_id=1, source_target_pairs={{0,7},{1,0},{2,1},{3,2},{4,3},{5,4},{6,5},{7,6},{8,15},{9,8},{10,9... | collective-permute-start | bytes 196616 | tf_op jit(solution)/shard_map/ppermute | solution.py:337
  52.5 13.2 %all-to-all-start.5 = ((bf16[16,16,128]{2,1,0:T(8,128)(2,1)}), bf16[16,16,128]{2,1,0:T(8,128)(2,1)S(1)}, u32[]{:S(2)}, u32[]{:S(2)}) async-start(bf16[16,16,128]{2,1,0:T(8,128)(2,1)} %pick.3.after_ref), calls=%async_computation.5 | async-start | bytes 131072 | tf_op jit(solution)/shard_map/all_to_all | solution.py:269
  57.7 4.8 %collective-permute-start.8 = (f32[2,2,16,256]{3,2,1,0:T(8,128)S(1)}, f32[2,2,16,256]{3,2,1,0:T(8,128)S(1)}, u32[]{:S(2)}, u32[]{:S(2)}) collective-permute-start(f32[2,2,16,256]{3,2,1,0:T(8,128)S(1)} %get-tuple-element.88), channel_id=1, source_target_pairs={{0,8},{8,0},{1,9},{9,1},{2,10},{10,2},{3,11},{11,3},{4,12},{12,4},... | collective-permute-start | bytes 196616 | tf_op jit(solution)/shard_map/ppermute | solution.py:188
  80.1 6.0 %collective-permute-start.9 = (bf16[8,6,32,256]{3,2,1,0:T(8,128)(2,1)S(1)}, bf16[8,6,32,256]{3,2,1,0:T(8,128)(2,1)S(1)}, u32[]{:S(2)}, u32[]{:S(2)}) collective-permute-start(bf16[8,6,32,256]{3,2,1,0:T(8,128)(2,1)S(1)} %all_to_all.35), channel_id=1, source_target_pairs={{0,16},{16,0},{1,17},{17,1},{2,18},{18,2},{3,19},{19,3},{4,20},{20... | collective-permute-start | bytes 2359304 | tf_op jit(solution)/shard_map/ppermute | solution.py:294

commit v4 on v3

--- a/solution.py
+++ b/solution.py
@@ -20,6 +20,7 @@
 WIDTH = 16
 SPINS = 4
 LANES = 128
+BLOCK = (2, HALF, 2, WIDTH, 256)
 F32 = jnp.float32
 BF16 = jnp.bfloat16
 PARAMS = pltpu.CompilerParams(vmem_limit_bytes=40 * 2**20)
@@ -67,64 +68,7 @@
     return slot_list(lambda s: src_ref[s], lax.axis_index(TM))
 
 
-def project_kernel(half, src_ref, vec_hbm, sol_hbm, *refs):
-    outs, (vec_ref, sol_ref, sems) = refs[: 1 + half * 7], refs[1 + half * 7 : 4 + half * 7]
-    slots = my_slots(src_ref)
-    copies = []
-    for k in range(HALF):
-        t = timeslice_at(slots, half * HALF + k)
-        for part in range(2):
-            copies.append(pltpu.make_async_copy(vec_hbm.at[part, t], vec_ref.at[k, part], sems.at[k, part, 0]))
-            copies.append(pltpu.make_async_copy(sol_hbm.at[part, t], sol_ref.at[k, part], sems.at[k, part, 1]))
-    for copy in copies:
-        copy.start()
-    dims = (((0,), (0,)), ((), ()))
-    for k in range(HALF):
-        for copy in copies[4 * k : 4 * k + 4]:
-            copy.wait()
-        depth = vec_ref.shape[2]
-        sol = sol_ref[k].reshape(2 * depth, SC)
-        straight = vec_ref[k].reshape(2 * depth, NEV)
-        turned = jnp.concatenate([-vec_ref[k, 1], vec_ref[k, 0]], axis=0)
-        for part, right in enumerate((straight, turned)):
-            value = lax.dot_general(sol, right, dims, preferred_element_type=F32).astype(BF16)
-            if half == 0:
-                outs[0][:, k, part] = value.reshape(NC, WIDTH, NEV)
-            else:
-                value = value.reshape(2, NZ, WIDTH, NEV)
-                for yh in range(2):
-                    refs[-1][:, yh, k, part] = value[yh]
-    if half == 1:
-        z = lax.axis_index("z")
-        for d in range(NZ):
-            outs[d][...] = refs[-1][lax.rem(z + d, NZ)]
-
-
-def project(half, src, eigvecs, solutions):
-    depth = eigvecs.shape[2]
-    scratch = [
-        pltpu.VMEM((HALF, 2, depth, NEV), BF16),
-        pltpu.VMEM((HALF, 2, depth, SC), BF16),
-        pltpu.SemaphoreType.DMA((HALF, 2, 2)),
-    ]
-    if half == 0:
-        shapes = [jax.ShapeDtypeStruct((NC, HALF, 2, WIDTH, NEV), BF16)]
-    else:
-        shapes = [jax.ShapeDtypeStruct((2, HALF, 2, WIDTH, NEV), BF16)] * NZ
-        scratch.append(pltpu.VMEM((NZ, 2, HALF, 2, WIDTH, NEV), BF16))
-    return pl.pallas_call(
-        functools.partial(project_kernel, half),
-        in_specs=[smem()] + [pl.BlockSpec(memory_space=pl.ANY)] * 2,
-        out_specs=[vmem()] * len(shapes),
-        out_shape=shapes,
-        scratch_shapes=scratch,
-        compiler_params=pltpu.CompilerParams(vmem_limit_bytes=(58, 50)[half] * 2**20),
-        cost_estimate=pl.CostEstimate(flops=1_400_000_000, bytes_accessed=6_000_000, transcendentals=0),
-        name="project%d" % half,
-    )(src, eigvecs, solutions)
-
-
-def masks_kernel(src_ref, owner_ref, place_ref, root_ref, source_ref):
+def write_masks(src_ref, owner_ref, place_ref, root_ref, source_ref):
     me = lax.axis_index(TM)
     slots = my_slots(src_ref)
     full = functools.partial(jnp.full, (8, LANES), dtype=jnp.int32)
@@ -141,6 +85,67 @@
         source_ref[e] = full(source)
 
 
+def project_kernel(half, src_ref, owner_ref, vec_hbm, sol_hbm, *refs):
+    outs, (vec_ref, sol_ref, sems) = refs[: 1 + half * 4], refs[1 + half * 4 : 4 + half * 4]
+    slots = my_slots(src_ref)
+    copies = []
+    for k in range(HALF):
+        t = timeslice_at(slots, half * HALF + k)
+        for part in range(2):
+            copies.append(pltpu.make_async_copy(vec_hbm.at[part, t], vec_ref.at[k, part], sems.at[k, part, 0]))
+            copies.append(pltpu.make_async_copy(sol_hbm.at[part, t], sol_ref.at[k, part], sems.at[k, part, 1]))
+    for copy in copies:
+        copy.start()
+    if half == 1:
+        write_masks(src_ref, owner_ref, *outs[2:])
+    dims = (((0,), (0,)), ((), ()))
+    for k in range(HALF):
+        for copy in copies[4 * k : 4 * k + 4]:
+            copy.wait()
+        depth = vec_ref.shape[2]
+        sol = sol_ref[k].reshape(2 * depth, SC)
+        straight = vec_ref[k].reshape(2 * depth, NEV)
+        turned = jnp.concatenate([-vec_ref[k, 1], vec_ref[k, 0]], axis=0)
+        for part, right in enumerate((straight, turned)):
+            value = lax.dot_general(sol, right, dims, preferred_element_type=F32)
+            if half == 0:
+                outs[0][:, k, part] = value.astype(BF16).reshape(NC, WIDTH, NEV)
+            else:
+                value = value.reshape(2, NZ, WIDTH, NEV)
+                for yh in range(2):
+                    refs[-1][:, yh, k, part] = value[yh]
+    if half == 1:
+        parity = lax.rem(lax.axis_index("z"), 2)
+        for k in range(NZ // 2):
+            outs[0][k] = refs[-1][2 * k + parity]
+            outs[1][k] = refs[-1][2 * k + 1 - parity].astype(BF16)
+
+
+def project(half, src, owner, eigvecs, solutions):
+    depth = eigvecs.shape[2]
+    scratch = [
+        pltpu.VMEM((HALF, 2, depth, NEV), BF16),
+        pltpu.VMEM((HALF, 2, depth, SC), BF16),
+        pltpu.SemaphoreType.DMA((HALF, 2, 2)),
+    ]
+    if half == 0:
+        shapes = [jax.ShapeDtypeStruct((NC, HALF, 2, WIDTH, NEV), BF16)]
+    else:
+        shapes = [jax.ShapeDtypeStruct((NZ // 2,) + BLOCK, dtype) for dtype in (F32, BF16)]
+        shapes += [jax.ShapeDtypeStruct((NC, 8, LANES), jnp.int32)] * 3
+        scratch.append(pltpu.VMEM((NZ,) + BLOCK, F32))
+    return pl.pallas_call(
+        functools.partial(project_kernel, half),
+        in_specs=[smem()] * 2 + [pl.BlockSpec(memory_space=pl.ANY)] * 2,
+        out_specs=[vmem()] * len(shapes),
+        out_shape=shapes,
+        scratch_shapes=scratch,
+        compiler_params=pltpu.CompilerParams(vmem_limit_bytes=(58, 50)[half] * 2**20),
+        cost_estimate=pl.CostEstimate(flops=1_400_000_000, bytes_accessed=6_000_000, transcendentals=0),
+        name="project%d" % half,
+    )(src, owner, eigvecs, solutions)
+
+
 def scatter_sources(place_ref, half, totals, scatter_ref):
     for s in range(NS):
         for part in range(2):
@@ -164,28 +169,40 @@
     scatter_sources(place_ref, 0, totals, scatter_ref)
 
 
-def sum_kernel(after_ref, *refs):
+def pair_kernel(after_ref, kept_ref, came_ref, own_ref, *send_refs):
     del after_ref
-    terms, (keep_ref, send_ref) = refs[:NZ], refs[NZ:]
+    half = lax.div(lax.axis_index("z"), 2)
+    own_ref[...] = kept_ref[half] + came_ref[half].astype(F32)
+    for d, ref in enumerate(send_refs):
+        at = lax.rem(half + d + 1, NZ // 2)
+        ref[...] = (kept_ref[at] + came_ref[at].astype(F32)).astype(BF16)
+
+
+def sum_kernel(after_ref, own_ref, *refs):
+    del after_ref
+    terms, (keep_ref, send_ref) = refs[:-2], refs[-2:]
     yh = lax.axis_index("yh")
     for ref, at in ((keep_ref, yh), (send_ref, 1 - yh)):
-        total = terms[0][at].astype(F32)
-        for term in terms[1:]:
+        total = own_ref[at]
+        for term in terms:
             total = total + term[at].astype(F32)
         ref[...] = total
 
 
-def second_sum(terms, after):
-    keep, send = pl.pallas_call(
-        sum_kernel,
-        in_specs=[pl.BlockSpec(memory_space=pl.ANY)] + [vmem()] * NZ,
-        out_specs=[vmem()] * 2,
-        out_shape=[jax.ShapeDtypeStruct((HALF, 2, WIDTH, NEV), F32)] * 2,
+def second_call(kernel, name, shapes, *operands):
+    return pl.pallas_call(
+        kernel,
+        in_specs=[pl.BlockSpec(memory_space=pl.ANY)] + [vmem()] * (len(operands) - 1),
+        out_specs=[vmem()] * len(shapes),
+        out_shape=shapes,
         compiler_params=PARAMS,
         cost_estimate=pl.CostEstimate(flops=500_000, bytes_accessed=500_000, transcendentals=0),
-        name="second_sum",
-    )(after, *terms)
-    return keep, lax.ppermute(send, "yh", [(0, 1), (1, 0)])
+        name=name,
+    )(*operands)
+
+
+def along_z(x, to):
+    return lax.ppermute(x, "z", [(z, to(z)) for z in range(NZ)])
 
 
 def weigh_kernel(src_ref, owner_ref, place_ref, early_ref, keep_ref, recv_ref, elem_ref, out_ref, late_ref, all_ref):
@@ -305,20 +322,10 @@
 
 def per_device(eigvecs, solutions, elementals, source_list, pair_owner, dilution_order):
     order = dilution_order.reshape(1, -1)
-    mask = jax.ShapeDtypeStruct((NC, 8, LANES), jnp.int32)
-    place, root, source = pl.pallas_call(
-        masks_kernel,
-        in_specs=[smem(), smem()],
-        out_specs=[vmem()] * 3,
-        out_shape=[mask] * 3,
-        compiler_params=PARAMS,
-        cost_estimate=pl.CostEstimate(flops=100_000, bytes_accessed=200_000, transcendentals=0),
-        name="masks",
-    )(source_list, pair_owner)
-
-    (first,) = project(0, source_list, eigvecs, solutions)
+    (first,) = project(0, source_list, pair_owner, eigvecs, solutions)
     first, later = lax.optimization_barrier((first, source_list))
     recv = all_to_all(first, SPACE)
+    kept, send, place, root, source = project(1, later, pair_owner, eigvecs, solutions)
     early, scatter = pl.pallas_call(
         reduce_kernel,
         in_specs=[vmem()] * 2,
@@ -332,12 +339,14 @@
         name="reduce",
     )(place, recv)
 
-    terms = list(project(1, later, eigvecs, solutions))
-    for d in range(1, NZ):
-        terms[d] = lax.ppermute(terms[d], "z", [(z, (z + d) % NZ) for z in range(NZ)])
+    block = [jax.ShapeDtypeStruct(BLOCK, dtype) for dtype in (F32, BF16, BF16, BF16)]
+    terms = list(second_call(pair_kernel, "pair", block, scatter, kept, along_z(send, lambda z: z ^ 1)))
+    for d in range(1, NZ // 2):
+        terms[d] = along_z(terms[d], lambda z: (z + 2 * d) % NZ)
     picked = spread(scatter, root)
     rows = all_to_all(picked, SPACE)
-    keep, added = second_sum(terms, picked)
+    keep, send = second_call(sum_kernel, "sum", [jax.ShapeDtypeStruct(BLOCK[1:], F32)] * 2, picked, *terms)
+    added = lax.ppermute(send, "yh", [(0, 1), (1, 0)])
     weighted, late = pl.pallas_call(
         weigh_kernel,
         in_specs=[smem(), smem()] + [vmem()] * 5,

time: 88 us -> 85 us (0.966)
  starting transfers between devices: 44.7 us -> 37.6 us
  waiting for transfers between devices: 12.1 us -> 16.5 us
    ppermute x8 -> x5, starting transfers between devices: 15.8 us -> 8.09 us  [the longest x4 5.13 us: along_z(): return lax.ppermute(x, 'z', [(z, to(z)) for z in range(NZ)])]
    all_to_all x3, waiting for transfers between devices: 8.65 us -> 14.5 us  [all_to_all(): return lax.all_to_all(x, axes, split_axis=0, concat_axis=0, tiled=True)]
    ppermute x8 -> x5, waiting for transfers between devices: 3.23 us -> 1.76 us  [the longest x1 1.75 us: per_device(): added = lax.ppermute(send, 'yh', [(0, 1), (1, 0)])]
    all_to_all x3, starting transfers between devices: 24.9 us -> 26 us  [all_to_all(): return lax.all_to_all(x, axes, split_axis=0, concat_axis=0, tiled=True)]
    pallas_call x2, Pallas kernels: 1 us -> 0.11 us  [second_call(): pl.pallas_call(kernel, in_specs=[pl.BlockSpec(memory_space=pl.ANY)] + [vm...]
  transfers between devices with their start and end apart: 12 -> 9, of which waited for: 6 -> 5; matrix products, arithmetic and copies ran while one was open for 1% -> 1% of each run, Pallas kernels for 9% -> 8%
where the time goes in v4:
time: 85 us; the launch traced here: 84.6 us
  starting transfers between devices  37.6 us (44%)
  waiting for transfers between devices  16.5 us (19%)
  blocking collectives  14.5 us (17%)
  Pallas kernels  14.2 us (17%)
  other arithmetic  1.03 us (1%)
    all_to_all x3, starting transfers between devices, all_to_all(): return lax.all_to_all(x, axes, split_axis=0, concat_axis=0, tiled=True)  26 us
    all_to_all x3, waiting for transfers between devices, all_to_all(): return lax.all_to_all(x, axes, split_axis=0, concat_axis=0, tiled=True)  14.5 us
    all_to_all x1, blocking collectives, all_to_all(): return lax.all_to_all(x, axes, split_axis=0, concat_axis=0, tiled=True)  14.5 us
    pallas_call x2, Pallas kernels, project(): pl.pallas_call(functools.partial(project_kernel, half), in_specs=[smem()]...  9.91 us
    ppermute x4, starting transfers between devices, along_z(): return lax.ppermute(x, 'z', [(z, to(z)) for z in range(NZ)])  5.13 us
    ppermute x1, starting transfers between devices, gather(): return (own, lax.ppermute(own, 'core', [(0, 1), (1, 0)]))  3.59 us
    ppermute x1, starting transfers between devices, per_device(): added = lax.ppermute(send, 'yh', [(0, 1), (1, 0)])  2.96 us
    ppermute x1, waiting for transfers between devices, per_device(): added = lax.ppermute(send, 'yh', [(0, 1), (1, 0)])  1.75 us
  transfers between devices with their start and end apart: 9, of which 5 were waited for; matrix products, arithmetic and copies ran while one was open for 1% of the time, Pallas kernels for 8%

profile of v4, /device:TPU:1, one launch (start us, length us, event | category | flops | bytes accessed | tf_op | source)
XLA Modules:
  0.0 84.6 jit_solution(15572471635796466216)
XLA Ops:
  0.0 0.0 copy-start.2
  0.0 0.0 copy-start.1
  0.0 5.4 %project0.1 = bf16[16,2,2,16,256]{4,3,2,1,0:T(8,128)(2,1)} custom-call(s32[4]{0:T(128)} %src_ref.4, s32[16,16]{1,0:T(8,128)} %owner_ref.5, bf16[2,4,1344,256]{3,2,1,0:T(8,128)(2,1)} %vec_hbm.3, bf16[2,4,1344,256]{3,2,1,0:T(8,128)(2,1)} %sol_hbm.3), custom_call_target="tpu_custom_call" | custom-call | flops 1400000000 | bytes 6000000 | tf_op jit(solution)/shard_map/project0/pallas_call | solution.py:137
  5.5 11.8 %all-to-all-start.3 = ((bf16[16,2,2,16,256]{4,3,2,1,0:T(8,128)(2,1)}), bf16[16,2,2,16,256]{4,3,2,1,0:T(8,128)(2,1)S(1)}, u32[]{:S(2)}, u32[]{:S(2)}) async-start(bf16[16,2,2,16,256]{4,3,2,1,0:T(8,128)(2,1)} %project0.1), calls=%async_computation.3 | async-start | bytes 1048576 | tf_op jit(solution)/shard_map/all_to_all | solution.py:286
  17.2 0.0 copy-done.2
  17.2 0.0 copy-done.1
  17.2 0.0 copy-start
  17.3 0.0 copy-start.3
  17.3 4.5 %project1.1 = (f32[4,2,2,2,16,256]{5,4,3,2,1,0:T(8,128)S(1)}, bf16[4,2,2,2,16,256]{5,4,3,2,1,0:T(8,128)(2,1)S(1)}, s32[16,8,128]{2,1,0:T(8,128)S(1)}, s32[16,8,128]{2,1,0:T(8,128)S(1)}, s32[16,8,128]{2,1,0:T(8,128)S(1)}) custom-call(s32[4]{0:T(128)S(1)} %copy-done.2, s32[16,16]{1,0:T(8,128)S(1)} %copy-done.1, bf16[2,4,1344,256]{3,2,1,0:T(8,128)(2,1)} %vec_hbm.3, ...), custom_call_target="tpu_custom_call" | custom-call | flops 1400000000 | bytes 6000000 | tf_op jit(solution)/shard_map/project1/pallas_call | solution.py:137
  21.7 1.5 %collective-permute-start.1 = (bf16[4,2,2,2,16,256]{5,4,3,2,1,0:T(8,128)(2,1)S(1)}, bf16[4,2,2,2,16,256]{5,4,3,2,1,0:T(8,128)(2,1)S(1)}, u32[]{:S(2)}, u32[]{:S(2)}) collective-permute-start(bf16[4,2,2,2,16,256]{5,4,3,2,1,0:T(8,128)(2,1)S(1)} %get-tuple-element.78), channel_id=1, source_target_pairs={{0,1},{1,0},{2,3},{3,2},{4,5},{5,4},{6,7},{7,6},{8,9},{9,8},{10,11... | collective-permute-start | bytes 786440 | tf_op jit(solution)/shard_map/ppermute | solution.py:205
  23.2 9.3 %all-to-all-done.3.recv_ref = bf16[16,2,2,16,256]{4,3,2,1,0:T(8,128)(2,1)S(1)} async-done(((bf16[16,2,2,16,256]{4,3,2,1,0:T(8,128)(2,1)}), bf16[16,2,2,16,256]{4,3,2,1,0:T(8,128)(2,1)S(1)}, u32[]{:S(2)}, u32[]{:S(2)}) %all-to-all-start.3) | async-done | bytes 524320 | tf_op jit(solution)/shard_map/all_to_all | solution.py:286
  32.5 0.7 reduce.5
  33.2 9.0 %all-to-all-start.4 = ((bf16[16,16,128]{2,1,0:T(8,128)(2,1)}), bf16[16,16,128]{2,1,0:T(8,128)(2,1)S(1)}, u32[]{:S(2)}, u32[]{:S(2)}) async-start(bf16[16,16,128]{2,1,0:T(8,128)(2,1)} %get-tuple-element.75.after_ref), calls=%async_computation.4 | async-start | bytes 131072 | tf_op jit(solution)/shard_map/all_to_all | solution.py:286
  42.1 0.0 collective-permute-done.1.came_ref
  42.1 0.1 pair.1
  42.2 0.1 collective-permute-start.2
  42.3 2.5 %collective-permute-start.3 = (bf16[2,2,2,16,256]{4,3,2,1,0:T(8,128)(2,1)S(1)}, bf16[2,2,2,16,256]{4,3,2,1,0:T(8,128)(2,1)S(1)}, u32[]{:S(2)}, u32[]{:S(2)}) collective-permute-start(bf16[2,2,2,16,256]{4,3,2,1,0:T(8,128)(2,1)S(1)} %get-tuple-element.81), channel_id=1, source_target_pairs={{0,4},{1,5},{2,6},{3,7},{4,0},{5,1},{6,2},{7,3},{8,12},{9,13},{10,... | collective-permute-start | bytes 196616 | tf_op jit(solution)/shard_map/ppermute | solution.py:205
  44.8 1.1 %collective-permute-start.4 = (bf16[2,2,2,16,256]{4,3,2,1,0:T(8,128)(2,1)S(1)}, bf16[2,2,2,16,256]{4,3,2,1,0:T(8,128)(2,1)S(1)}, u32[]{:S(2)}, u32[]{:S(2)}) collective-permute-start(bf16[2,2,2,16,256]{4,3,2,1,0:T(8,128)(2,1)S(1)} %get-tuple-element.82), channel_id=1, source_target_pairs={{0,6},{1,7},{2,0},{3,1},{4,2},{5,3},{6,4},{7,5},{8,14},{9,15},{10,... | collective-permute-start | bytes 196616 | tf_op jit(solution)/shard_map/ppermute | solution.py:205
  45.9 2.1 %all-to-all-done.4.parts_ref = bf16[16,16,128]{2,1,0:T(8,128)(2,1)S(1)} async-done(((bf16[16,16,128]{2,1,0:T(8,128)(2,1)}), bf16[16,16,128]{2,1,0:T(8,128)(2,1)S(1)}, u32[]{:S(2)}, u32[]{:S(2)}) %all-to-all-start.4) | async-done | bytes 65568 | tf_op jit(solution)/shard_map/all_to_all | solution.py:286
  48.0 0.6 pick.3.after_ref
  48.6 5.2 %all-to-all-start.5 = ((bf16[16,16,128]{2,1,0:T(8,128)(2,1)}), bf16[16,16,128]{2,1,0:T(8,128)(2,1)S(1)}, u32[]{:S(2)}, u32[]{:S(2)}) async-start(bf16[16,16,128]{2,1,0:T(8,128)(2,1)} %pick.3.after_ref), calls=%async_computation.5 | async-start | bytes 131072 | tf_op jit(solution)/shard_map/all_to_all | solution.py:286
  53.9 0.0 collective-permute-done.2.refs_0_
  53.9 0.0 collective-permute-done.3.refs_1_
  53.9 0.0 collective-permute-done.4.refs_2_
  53.9 3.0 %collective-permute-start.5 = (f32[2,2,16,256]{3,2,1,0:T(8,128)S(1)}, f32[2,2,16,256]{3,2,1,0:T(8,128)S(1)}, u32[]{:S(2)}, u32[]{:S(2)}) collective-permute-start(f32[2,2,16,256]{3,2,1,0:T(8,128)S(1)} %get-tuple-element.84), channel_id=1, source_target_pairs={{0,8},{8,0},{1,9},{9,1},{2,10},{10,2},{3,11},{11,3},{4,12},{12,4},... | collective-permute-start | bytes 196616 | tf_op jit(solution)/shard_map/ppermute | solution.py:349
  56.9 1.8 %collective-permute-done.5.recv_ref = f32[2,2,16,256]{3,2,1,0:T(8,128)S(1)} collective-permute-done((f32[2,2,16,256]{3,2,1,0:T(8,128)S(1)}, f32[2,2,16,256]{3,2,1,0:T(8,128)S(1)}, u32[]{:S(2)}, u32[]{:S(2)}) %collective-permute-start.5) | collective-permute-done | bytes 65568 | tf_op jit(solution)/shard_map/ppermute | solution.py:349
  58.6 0.0 copy-done
  58.7 1.0 %weigh.1 = (bf16[16,32,256]{2,1,0:T(8,128)(2,1)S(1)}, bf16[16,16,128]{2,1,0:T(8,128)(2,1)S(1)}) custom-call(s32[4]{0:T(128)S(1)} %copy-done.2, s32[16,16]{1,0:T(8,128)S(1)} %copy-done.1, s32[16,8,128]{2,1,0:T(8,128)S(1)} %get-tuple-element.73.place_ref, bf16[2,2,16,256]{3,2,1,0:T(8,128)(2,1)S(1)} %get-tuple-element.76.early_ref, ...), custom_call_target="tpu_custom_call" | custom-call | flops 70000000 | bytes 2000000 | tf_op jit(solution)/shard_map/weigh/pallas_call | solution.py:350
  59.7 3.2 %all-to-all-done.5.rows_ref = bf16[16,16,128]{2,1,0:T(8,128)(2,1)S(1)} async-done(((bf16[16,16,128]{2,1,0:T(8,128)(2,1)}), bf16[16,16,128]{2,1,0:T(8,128)(2,1)S(1)}, u32[]{:S(2)}, u32[]{:S(2)}) %all-to-all-start.5) | async-done | bytes 65568 | tf_op jit(solution)/shard_map/all_to_all | solution.py:286
  62.8 0.0 copy-done.3
  62.8 0.3 pack.3
  63.1 14.5 %all_to_all.35 = bf16[8,6,32,256]{3,2,1,0:T(8,128)(2,1)S(1)} all-to-all(bf16[8,6,32,256]{3,2,1,0:T(8,128)(2,1)S(1)} %pack.3), channel_id=1, replica_groups=mesh['yl'=2,'x'=4,'core'=2,'yh'=2,'z'=8] {'yl','x'}, dimensions={0} | all-to-all | bytes 1572864 | tf_op jit(solution)/shard_map/all_to_all | solution.py:286
  77.6 3.6 %collective-permute-start.6 = (bf16[8,6,32,256]{3,2,1,0:T(8,128)(2,1)S(1)}, bf16[8,6,32,256]{3,2,1,0:T(8,128)(2,1)S(1)}, u32[]{:S(2)}, u32[]{:S(2)}) collective-permute-start(bf16[8,6,32,256]{3,2,1,0:T(8,128)(2,1)S(1)} %all_to_all.35), channel_id=1, source_target_pairs={{0,16},{16,0},{1,17},{17,1},{2,18},{18,2},{3,19},{19,3},{4,20},{20... | collective-permute-start | bytes 2359304 | tf_op jit(solution)/shard_map/ppermute | solution.py:311
  81.2 0.2 fusion.1
  81.4 0.2 convert_reduce_fusion
  81.6 0.6 broadcast_compare_fusion
  82.9 0.2 collective-permute-done.6
  83.1 1.5 %final.1 = bf16[16,2,16,256]{3,2,1,0:T(8,128)(2,1)} custom-call(s32[16,8,128]{2,1,0:T(8,128)S(1)} %get-tuple-element.71.source_ref, bf16[8,6,32,256]{3,2,1,0:T(8,128)(2,1)S(1)} %get-tuple-element.87.own_ref, bf16[8,6,32,256]{3,2,1,0:T(8,128)(2,1)S(1)} %get-tuple-element.88.other_ref), custom_call_target="tpu_custom_call" | custom-call | tf_op jit(solution)/shard_map/final/pallas_call | solution.py:377
  (4 shorter events, 0.1 us)
Async XLA Ops:
  0.0 17.2 %copy-start.2 = (s32[4]{0:T(128)S(1)}, s32[4]{0:T(128)}, u32[]{:S(2)}) copy-start(s32[4]{0:T(128)} %src_ref.4) | copy-start | bytes 52
  0.0 17.2 %copy-start.1 = (s32[16,16]{1,0:T(8,128)S(1)}, s32[16,16]{1,0:T(8,128)}, u32[]{:S(2)}) copy-start(s32[16,16]{1,0:T(8,128)} %owner_ref.5) | copy-start | bytes 3076
  5.5 27.0 %all-to-all-start.3 = ((bf16[16,2,2,16,256]{4,3,2,1,0:T(8,128)(2,1)}), bf16[16,2,2,16,256]{4,3,2,1,0:T(8,128)(2,1)S(1)}, u32[]{:S(2)}, u32[]{:S(2)}) async-start(bf16[16,2,2,16,256]{4,3,2,1,0:T(8,128)(2,1)} %project0.1), calls=%async_computation.3 | async-start | bytes 1048576 | tf_op jit(solution)/shard_map/all_to_all | solution.py:286
  17.2 41.4 %copy-start = (bf16[2,4,256,256]{3,2,1,0:T(8,128)(2,1)S(1)}, bf16[2,4,256,256]{3,2,1,0:T(8,128)(2,1)}, u32[]{:S(2)}) copy-start(bf16[2,4,256,256]{3,2,1,0:T(8,128)(2,1)} %elem_ref.1) | copy-start | bytes 3145732
  17.3 45.6 %copy-start.3 = (s32[64]{0:T(128)S(1)}, s32[64]{0:T(128)}, u32[]{:S(2)}) copy-start(s32[64]{0:T(128)} %param.17) | copy-start | bytes 772
  21.7 20.4 %collective-permute-start.1 = (bf16[4,2,2,2,16,256]{5,4,3,2,1,0:T(8,128)(2,1)S(1)}, bf16[4,2,2,2,16,256]{5,4,3,2,1,0:T(8,128)(2,1)S(1)}, u32[]{:S(2)}, u32[]{:S(2)}) collective-permute-start(bf16[4,2,2,2,16,256]{5,4,3,2,1,0:T(8,128)(2,1)S(1)} %get-tuple-element.78), channel_id=1, source_target_pairs={{0,1},{1,0},{2,3},{3,2},{4,5},{5,4},{6,7},{7,6},{8,9},{9,8},{10,11... | collective-permute-start | bytes 786440 | tf_op jit(solution)/shard_map/ppermute | solution.py:205
  33.2 14.8 %all-to-all-start.4 = ((bf16[16,16,128]{2,1,0:T(8,128)(2,1)}), bf16[16,16,128]{2,1,0:T(8,128)(2,1)S(1)}, u32[]{:S(2)}, u32[]{:S(2)}) async-start(bf16[16,16,128]{2,1,0:T(8,128)(2,1)} %get-tuple-element.75.after_ref), calls=%async_computation.4 | async-start | bytes 131072 | tf_op jit(solution)/shard_map/all_to_all | solution.py:286
  42.2 11.6 %collective-permute-start.2 = (bf16[2,2,2,16,256]{4,3,2,1,0:T(8,128)(2,1)S(1)}, bf16[2,2,2,16,256]{4,3,2,1,0:T(8,128)(2,1)S(1)}, u32[]{:S(2)}, u32[]{:S(2)}) collective-permute-start(bf16[2,2,2,16,256]{4,3,2,1,0:T(8,128)(2,1)S(1)} %get-tuple-element.80), channel_id=1, source_target_pairs={{0,2},{1,3},{2,4},{3,5},{4,6},{5,7},{6,0},{7,1},{8,10},{9,11},{10,... | collective-permute-start | bytes 196616 | tf_op jit(solution)/shard_map/ppermute | solution.py:205
  42.3 11.6 %collective-permute-start.3 = (bf16[2,2,2,16,256]{4,3,2,1,0:T(8,128)(2,1)S(1)}, bf16[2,2,2,16,256]{4,3,2,1,0:T(8,128)(2,1)S(1)}, u32[]{:S(2)}, u32[]{:S(2)}) collective-permute-start(bf16[2,2,2,16,256]{4,3,2,1,0:T(8,128)(2,1)S(1)} %get-tuple-element.81), channel_id=1, source_target_pairs={{0,4},{1,5},{2,6},{3,7},{4,0},{5,1},{6,2},{7,3},{8,12},{9,13},{10,... | collective-permute-start | bytes 196616 | tf_op jit(solution)/shard_map/ppermute | solution.py:205
  44.8 9.1 %collective-permute-start.4 = (bf16[2,2,2,16,256]{4,3,2,1,0:T(8,128)(2,1)S(1)}, bf16[2,2,2,16,256]{4,3,2,1,0:T(8,128)(2,1)S(1)}, u32[]{:S(2)}, u32[]{:S(2)}) collective-permute-start(bf16[2,2,2,16,256]{4,3,2,1,0:T(8,128)(2,1)S(1)} %get-tuple-element.82), channel_id=1, source_target_pairs={{0,6},{1,7},{2,0},{3,1},{4,2},{5,3},{6,4},{7,5},{8,14},{9,15},{10,... | collective-permute-start | bytes 196616 | tf_op jit(solution)/shard_map/ppermute | solution.py:205
  48.6 14.2 %all-to-all-start.5 = ((bf16[16,16,128]{2,1,0:T(8,128)(2,1)}), bf16[16,16,128]{2,1,0:T(8,128)(2,1)S(1)}, u32[]{:S(2)}, u32[]{:S(2)}) async-start(bf16[16,16,128]{2,1,0:T(8,128)(2,1)} %pick.3.after_ref), calls=%async_computation.5 | async-start | bytes 131072 | tf_op jit(solution)/shard_map/all_to_all | solution.py:286
  53.9 4.7 %collective-permute-start.5 = (f32[2,2,16,256]{3,2,1,0:T(8,128)S(1)}, f32[2,2,16,256]{3,2,1,0:T(8,128)S(1)}, u32[]{:S(2)}, u32[]{:S(2)}) collective-permute-start(f32[2,2,16,256]{3,2,1,0:T(8,128)S(1)} %get-tuple-element.84), channel_id=1, source_target_pairs={{0,8},{8,0},{1,9},{9,1},{2,10},{10,2},{3,11},{11,3},{4,12},{12,4},... | collective-permute-start | bytes 196616 | tf_op jit(solution)/shard_map/ppermute | solution.py:349
  77.6 5.5 %collective-permute-start.6 = (bf16[8,6,32,256]{3,2,1,0:T(8,128)(2,1)S(1)}, bf16[8,6,32,256]{3,2,1,0:T(8,128)(2,1)S(1)}, u32[]{:S(2)}, u32[]{:S(2)}) collective-permute-start(bf16[8,6,32,256]{3,2,1,0:T(8,128)(2,1)S(1)} %all_to_all.35), channel_id=1, source_target_pairs={{0,16},{16,0},{1,17},{17,1},{2,18},{18,2},{3,19},{19,3},{4,20},{20... | collective-permute-start | bytes 2359304 | tf_op jit(solution)/shard_map/ppermute | solution.py:311

commit v5 on v4

--- a/solution.py
+++ b/solution.py
@@ -20,7 +20,7 @@
 WIDTH = 16
 SPINS = 4
 LANES = 128
-BLOCK = (2, HALF, 2, WIDTH, 256)
+BLOCK = (HALF, 2, WIDTH, 256)
 F32 = jnp.float32
 BF16 = jnp.bfloat16
 PARAMS = pltpu.CompilerParams(vmem_limit_bytes=40 * 2**20)
@@ -68,7 +68,7 @@
     return slot_list(lambda s: src_ref[s], lax.axis_index(TM))
 
 
-def write_masks(src_ref, owner_ref, place_ref, root_ref, source_ref):
+def write_masks(src_ref, owner_ref, place_ref, root_ref, source_ref, slot_ref):
     me = lax.axis_index(TM)
     slots = my_slots(src_ref)
     full = functools.partial(jnp.full, (8, LANES), dtype=jnp.int32)
@@ -83,10 +83,14 @@
         for j in range(TD * NS):
             source = jnp.where(owner_ref[e, j] == me, j % NS, source)
         source_ref[e] = full(source)
-
-
-def project_kernel(half, src_ref, owner_ref, vec_hbm, sol_hbm, *refs):
-    outs, (vec_ref, sol_ref, sems) = refs[: 1 + half * 4], refs[1 + half * 4 : 4 + half * 4]
+    for j in range(TD * NS):
+        slot_ref[owner_ref[me, j]] = full(slots[j // NS])
+
+
+def project_kernel(half, src_ref, vec_hbm, sol_hbm, *refs):
+    if half == 1:
+        (owner_ref, elem_ref), refs = refs[:2], refs[2:]
+    outs, (vec_ref, sol_ref, sems) = refs[: 1 + half * 8], refs[1 + half * 8 : 4 + half * 8]
     slots = my_slots(src_ref)
     copies = []
     for k in range(HALF):
@@ -97,7 +101,10 @@
     for copy in copies:
         copy.start()
     if half == 1:
-        write_masks(src_ref, owner_ref, *outs[2:])
+        write_masks(src_ref, owner_ref, *outs[5:])
+        for k in range(TD):
+            for part in range(2):
+                outs[4][k, part] = elem_ref[part, timeslice_at(slots, k)]
     dims = (((0,), (0,)), ((), ()))
     for k in range(HALF):
         for copy in copies[4 * k : 4 * k + 4]:
@@ -116,12 +123,16 @@
                     refs[-1][:, yh, k, part] = value[yh]
     if half == 1:
         parity = lax.rem(lax.axis_index("z"), 2)
+        yh = lax.axis_index("yh")
         for k in range(NZ // 2):
-            outs[0][k] = refs[-1][2 * k + parity]
-            outs[1][k] = refs[-1][2 * k + 1 - parity].astype(BF16)
-
-
-def project(half, src, owner, eigvecs, solutions):
+            same, other = 2 * k + parity, 2 * k + 1 - parity
+            outs[0][k] = refs[-1][same, yh]
+            outs[1][k] = refs[-1][other, yh].astype(BF16)
+            outs[2][k] = refs[-1][same, 1 - yh].astype(BF16)
+            outs[3][k] = refs[-1][other, 1 - yh].astype(BF16)
+
+
+def project(half, src, eigvecs, solutions, *more):
     depth = eigvecs.shape[2]
     scratch = [
         pltpu.VMEM((HALF, 2, depth, NEV), BF16),
@@ -131,19 +142,20 @@
     if half == 0:
         shapes = [jax.ShapeDtypeStruct((NC, HALF, 2, WIDTH, NEV), BF16)]
     else:
-        shapes = [jax.ShapeDtypeStruct((NZ // 2,) + BLOCK, dtype) for dtype in (F32, BF16)]
-        shapes += [jax.ShapeDtypeStruct((NC, 8, LANES), jnp.int32)] * 3
-        scratch.append(pltpu.VMEM((NZ,) + BLOCK, F32))
+        shapes = [jax.ShapeDtypeStruct((NZ // 2,) + BLOCK, dtype) for dtype in (F32, BF16, BF16, BF16)]
+        shapes.append(jax.ShapeDtypeStruct((TD, 2, NEV, NEV), BF16))
+        shapes += [jax.ShapeDtypeStruct((NC, 8, LANES), jnp.int32)] * 4
+        scratch.append(pltpu.VMEM((NZ, 2) + BLOCK, F32))
     return pl.pallas_call(
         functools.partial(project_kernel, half),
-        in_specs=[smem()] * 2 + [pl.BlockSpec(memory_space=pl.ANY)] * 2,
+        in_specs=[smem()] + [pl.BlockSpec(memory_space=pl.ANY)] * 2 + [smem(), vmem()][: len(more)],
         out_specs=[vmem()] * len(shapes),
         out_shape=shapes,
         scratch_shapes=scratch,
         compiler_params=pltpu.CompilerParams(vmem_limit_bytes=(58, 50)[half] * 2**20),
         cost_estimate=pl.CostEstimate(flops=1_400_000_000, bytes_accessed=6_000_000, transcendentals=0),
         name="project%d" % half,
-    )(src, owner, eigvecs, solutions)
+    )(src, eigvecs, solutions, *more)
 
 
 def scatter_sources(place_ref, half, totals, scatter_ref):
@@ -169,57 +181,49 @@
     scatter_sources(place_ref, 0, totals, scatter_ref)
 
 
-def pair_kernel(after_ref, kept_ref, came_ref, own_ref, *send_refs):
+def pair_kernel(after_ref, kept_ref, *refs):
     del after_ref
+    came_refs, own_ref, send_refs = refs[:3], refs[3], refs[4:]
     half = lax.div(lax.axis_index("z"), 2)
-    own_ref[...] = kept_ref[half] + came_ref[half].astype(F32)
-    for d, ref in enumerate(send_refs):
-        at = lax.rem(half + d + 1, NZ // 2)
-        ref[...] = (kept_ref[at] + came_ref[at].astype(F32)).astype(BF16)
-
-
-def sum_kernel(after_ref, own_ref, *refs):
-    del after_ref
-    terms, (keep_ref, send_ref) = refs[:-2], refs[-2:]
-    yh = lax.axis_index("yh")
-    for ref, at in ((keep_ref, yh), (send_ref, 1 - yh)):
-        total = own_ref[at]
-        for term in terms:
-            total = total + term[at].astype(F32)
-        ref[...] = total
-
-
-def second_call(kernel, name, shapes, *operands):
-    return pl.pallas_call(
-        kernel,
-        in_specs=[pl.BlockSpec(memory_space=pl.ANY)] + [vmem()] * (len(operands) - 1),
-        out_specs=[vmem()] * len(shapes),
-        out_shape=shapes,
-        compiler_params=PARAMS,
-        cost_estimate=pl.CostEstimate(flops=500_000, bytes_accessed=500_000, transcendentals=0),
-        name=name,
-    )(*operands)
+    for d in range(NZ // 2):
+        at = lax.rem(half + d, NZ // 2)
+        total = kept_ref[at]
+        for ref in came_refs:
+            total = total + ref[at].astype(F32)
+        if d == 0:
+            own_ref[...] = total
+        else:
+            send_refs[d - 1][...] = total.astype(BF16)
 
 
 def along_z(x, to):
     return lax.ppermute(x, "z", [(z, to(z)) for z in range(NZ)])
 
 
-def weigh_kernel(src_ref, owner_ref, place_ref, early_ref, keep_ref, recv_ref, elem_ref, out_ref, late_ref, all_ref):
-    slots = my_slots(src_ref)
-    totals = [keep_ref[k] + recv_ref[k] for k in range(HALF)]
-    scatter_sources(place_ref, 1, totals, late_ref)
+def weigh_kernel(slot_ref, place_ref, early_ref, elem_ref, *refs):
+    terms, (out_ref, late_ref) = refs[:-2], refs[-2:]
+    totals = []
+    for k in range(HALF):
+        total = terms[0][k]
+        for term in terms[1:]:
+            total = total + term[k].astype(F32)
+        totals.append(total)
+    weighted = []
     for k in range(TD):
-        t = timeslice_at(slots, k)
         both = early_ref[k] if k < HALF else totals[k - HALF].astype(BF16)
         both = both.reshape(2 * WIDTH, NEV)
-        by_real = jnp.dot(both, elem_ref[0, t], preferred_element_type=F32)
-        by_imag = jnp.dot(both, elem_ref[1, t], preferred_element_type=F32)
-        all_ref[k, :WIDTH] = (by_real[:WIDTH] + by_imag[WIDTH:]).astype(BF16)
-        all_ref[k, WIDTH:] = (by_real[WIDTH:] - by_imag[:WIDTH]).astype(BF16)
-    group = lax.axis_index(TM)
-    for j in range(TD * NS):
-        out_ref[owner_ref[group, j]] = all_ref[slots[j // NS]]
+        by_real = jnp.dot(both, elem_ref[k, 0], preferred_element_type=F32)
+        by_imag = jnp.dot(both, elem_ref[k, 1], preferred_element_type=F32)
+        real = by_real[:WIDTH] + by_imag[WIDTH:]
+        imag = by_real[WIDTH:] - by_imag[:WIDTH]
+        weighted.append(jnp.concatenate([real, imag], axis=0))
+    for d in range(NC):
+        slot = jnp.tile(slot_ref[d], (2 * WIDTH // 8, NEV // LANES))
+        value = weighted[0]
+        for k in range(1, TD):
+            value = jnp.where(slot == k, weighted[k], value)
+        out_ref[d] = value.astype(BF16)
+    scatter_sources(place_ref, 1, totals, late_ref)
 
 
 def pick_kernel(root_ref, parts_ref, out_ref):
@@ -322,10 +326,12 @@
 
 def per_device(eigvecs, solutions, elementals, source_list, pair_owner, dilution_order):
     order = dilution_order.reshape(1, -1)
-    (first,) = project(0, source_list, pair_owner, eigvecs, solutions)
+    (first,) = project(0, source_list, eigvecs, solutions)
     first, later = lax.optimization_barrier((first, source_list))
     recv = all_to_all(first, SPACE)
-    kept, send, place, root, source = project(1, later, pair_owner, eigvecs, solutions)
+    kept, to_z, to_y, to_both, elems, place, root, source, slot = project(
+        1, later, eigvecs, solutions, pair_owner, elementals
+    )
     early, scatter = pl.pallas_call(
         reduce_kernel,
         in_specs=[vmem()] * 2,
@@ -339,27 +345,37 @@
         name="reduce",
     )(place, recv)
 
-    block = [jax.ShapeDtypeStruct(BLOCK, dtype) for dtype in (F32, BF16, BF16, BF16)]
-    terms = list(second_call(pair_kernel, "pair", block, scatter, kept, along_z(send, lambda z: z ^ 1)))
+    came = [
+        along_z(to_z, lambda z: z ^ 1),
+        lax.ppermute(to_y, "yh", [(0, 1), (1, 0)]),
+        lax.ppermute(to_both, SPACE, [(c, c ^ 9) for c in range(NC)]),
+    ]
+    terms = pl.pallas_call(
+        pair_kernel,
+        in_specs=[pl.BlockSpec(memory_space=pl.ANY)] + [vmem()] * 4,
+        out_specs=[vmem()] * 4,
+        out_shape=[jax.ShapeDtypeStruct(BLOCK, dtype) for dtype in (F32, BF16, BF16, BF16)],
+        compiler_params=PARAMS,
+        cost_estimate=pl.CostEstimate(flops=500_000, bytes_accessed=500_000, transcendentals=0),
+        name="pair",
+    )(scatter, kept, *came)
+    terms = list(terms)
     for d in range(1, NZ // 2):
         terms[d] = along_z(terms[d], lambda z: (z + 2 * d) % NZ)
     picked = spread(scatter, root)
     rows = all_to_all(picked, SPACE)
-    keep, send = second_call(sum_kernel, "sum", [jax.ShapeDtypeStruct(BLOCK[1:], F32)] * 2, picked, *terms)
-    added = lax.ppermute(send, "yh", [(0, 1), (1, 0)])
     weighted, late = pl.pallas_call(
         weigh_kernel,
-        in_specs=[smem(), smem()] + [vmem()] * 5,
+        in_specs=[vmem()] * (4 + len(terms)),
         out_specs=[vmem()] * 2,
         out_shape=[
             jax.ShapeDtypeStruct((NC, 2 * WIDTH, NEV), BF16),
             jax.ShapeDtypeStruct((NC, WIDTH, LANES), BF16),
         ],
-        scratch_shapes=[pltpu.VMEM((TD, 2 * WIDTH, NEV), BF16)],
         compiler_params=PARAMS,
         cost_estimate=pl.CostEstimate(flops=70_000_000, bytes_accessed=2_000_000, transcendentals=0),
         name="weigh",
-    )(source_list, pair_owner, place, early, keep, added, elementals)
+    )(slot, place, early, elems, *terms)
 
     own, other = gather(rows, order, weighted)
 

time: 85 us -> 83.2 us (0.979)
  starting transfers between devices: 37.6 us -> 41 us
  waiting for transfers between devices: 16.5 us -> 14.2 us
  blocking collectives: 14.5 us -> 12.5 us
  Pallas kernels: 14.2 us -> 13.3 us
    ppermute x4, starting transfers between devices: 5.13 us -> 9.7 us  [along_z(): return lax.ppermute(x, 'z', [(z, to(z)) for z in range(NZ)])]
    all_to_all x3, waiting for transfers between devices: 14.5 us -> 12.4 us  [all_to_all(): return lax.all_to_all(x, axes, split_axis=0, concat_axis=0, tiled=True)]
    all_to_all x3, starting transfers between devices: 26 us -> 24 us  [all_to_all(): return lax.all_to_all(x, axes, split_axis=0, concat_axis=0, tiled=True)]
    all_to_all x1, blocking collectives: 14.5 us -> 12.5 us  [all_to_all(): return lax.all_to_all(x, axes, split_axis=0, concat_axis=0, tiled=True)]
    ppermute x1 -> x2, waiting for transfers between devices: 1.75 us -> 0.01 us  [the longest x1 0.01 us: per_device(): lax.ppermute(to_y, 'yh', [(0, 1), (1, 0)])]
    ppermute x4, waiting for transfers between devices: 0.01 us -> 1.57 us  [along_z(): return lax.ppermute(x, 'z', [(z, to(z)) for z in range(NZ)])]
    ppermute x1 -> x2, starting transfers between devices: 2.96 us -> 3.37 us  [the longest x1 2.08 us: per_device(): lax.ppermute(to_y, 'yh', [(0, 1), (1, 0)])]
  transfers between devices with their start and end apart: 9 -> 10, of which waited for: 5 -> 5; matrix products, arithmetic and copies ran while one was open for 1% -> 1% of each run, Pallas kernels for 8% -> 7%
where the time goes in v5:
time: 83.2 us; the launch traced here: 82.9 us
  starting transfers between devices  41 us (49%)
  waiting for transfers between devices  14.2 us (17%)
  Pallas kernels  13.3 us (16%)
  blocking collectives  12.5 us (15%)
  other arithmetic  1.03 us (1%)
    all_to_all x3, starting transfers between devices, all_to_all(): return lax.all_to_all(x, axes, split_axis=0, concat_axis=0, tiled=True)  24 us
    all_to_all x1, blocking collectives, all_to_all(): return lax.all_to_all(x, axes, split_axis=0, concat_axis=0, tiled=True)  12.5 us
    all_to_all x3, waiting for transfers between devices, all_to_all(): return lax.all_to_all(x, axes, split_axis=0, concat_axis=0, tiled=True)  12.4 us
    pallas_call x2, Pallas kernels, project(): pl.pallas_call(functools.partial(project_kernel, half), in_specs=[smem()]...  9.77 us
    ppermute x4, starting transfers between devices, along_z(): return lax.ppermute(x, 'z', [(z, to(z)) for z in range(NZ)])  9.7 us
    ppermute x1, starting transfers between devices, gather(): return (own, lax.ppermute(own, 'core', [(0, 1), (1, 0)]))  3.9 us
    ppermute x1, starting transfers between devices, per_device(): lax.ppermute(to_y, 'yh', [(0, 1), (1, 0)])  2.08 us
  transfers between devices with their start and end apart: 10, of which 5 were waited for; matrix products, arithmetic and copies ran while one was open for 1% of the time, Pallas kernels for 7%

profile of v5, /device:TPU:1, one launch (start us, length us, event | category | flops | bytes accessed | tf_op | source)
XLA Modules:
  0.0 82.9 jit_solution(11797538007892755838)
XLA Ops:
  0.0 0.0 copy-start.2
  0.0 0.0 copy-start.1
  0.0 0.0 copy-start
  0.0 5.3 %project0.1 = bf16[16,2,2,16,256]{4,3,2,1,0:T(8,128)(2,1)} custom-call(s32[4]{0:T(128)} %src_ref.2, bf16[2,4,1344,256]{3,2,1,0:T(8,128)(2,1)} %vec_hbm.3, bf16[2,4,1344,256]{3,2,1,0:T(8,128)(2,1)} %sol_hbm.3), custom_call_target="tpu_custom_call" | custom-call | flops 1400000000 | bytes 6000000 | tf_op jit(solution)/shard_map/project0/pallas_call | solution.py:149
  5.3 11.8 %all-to-all-start.3 = ((bf16[16,2,2,16,256]{4,3,2,1,0:T(8,128)(2,1)}), bf16[16,2,2,16,256]{4,3,2,1,0:T(8,128)(2,1)S(1)}, u32[]{:S(2)}, u32[]{:S(2)}) async-start(bf16[16,2,2,16,256]{4,3,2,1,0:T(8,128)(2,1)} %project0.1), calls=%async_computation.3 | async-start | bytes 1048576 | tf_op jit(solution)/shard_map/all_to_all | solution.py:290
  17.1 0.0 copy-done.2
  17.1 0.0 copy-done.1
  17.1 0.0 copy-done
  17.1 0.0 copy-start.3
  17.1 4.5 %project1.1 = (f32[4,2,2,16,256]{4,3,2,1,0:T(8,128)S(1)}, bf16[4,2,2,16,256]{4,3,2,1,0:T(8,128)(2,1)S(1)}, bf16[4,2,2,16,256]{4,3,2,1,0:T(8,128)(2,1)S(1)}, bf16...) custom-call(s32[4]{0:T(128)S(1)} %copy-done.2, ...), custom_call_target="tpu_custom_call" | custom-call | flops 1400000000 | bytes 6000000 | tf_op jit(solution)/shard_map/project1/pallas_call | solution.py:149
  21.6 10.7 %all-to-all-done.3.recv_ref = bf16[16,2,2,16,256]{4,3,2,1,0:T(8,128)(2,1)S(1)} async-done(((bf16[16,2,2,16,256]{4,3,2,1,0:T(8,128)(2,1)}), bf16[16,2,2,16,256]{4,3,2,1,0:T(8,128)(2,1)S(1)}, u32[]{:S(2)}, u32[]{:S(2)}) %all-to-all-start.3) | async-done | bytes 524320 | tf_op jit(solution)/shard_map/all_to_all | solution.py:290
  32.3 0.7 reduce.5
  33.0 7.3 %all-to-all-start.4 = ((bf16[16,16,128]{2,1,0:T(8,128)(2,1)}), bf16[16,16,128]{2,1,0:T(8,128)(2,1)S(1)}, u32[]{:S(2)}, u32[]{:S(2)}) async-start(bf16[16,16,128]{2,1,0:T(8,128)(2,1)} %get-tuple-element.77.after_ref), calls=%async_computation.4 | async-start | bytes 131072 | tf_op jit(solution)/shard_map/all_to_all | solution.py:290
  40.4 0.8 collective-permute-start.1
  41.2 2.1 %collective-permute-start.2 = (bf16[4,2,2,16,256]{4,3,2,1,0:T(8,128)(2,1)S(1)}, bf16[4,2,2,16,256]{4,3,2,1,0:T(8,128)(2,1)S(1)}, u32[]{:S(2)}, u32[]{:S(2)}) collective-permute-start(bf16[4,2,2,16,256]{4,3,2,1,0:T(8,128)(2,1)S(1)} %get-tuple-element.83), channel_id=1, source_target_pairs={{0,8},{8,0},{1,9},{9,1},{2,10},{10,2},{3,11},{11,3},{4,12},{12,4},... | collective-permute-start | bytes 393224 | tf_op jit(solution)/shard_map/ppermute | solution.py:350
  43.2 1.3 %collective-permute-start.3 = (bf16[4,2,2,16,256]{4,3,2,1,0:T(8,128)(2,1)S(1)}, bf16[4,2,2,16,256]{4,3,2,1,0:T(8,128)(2,1)S(1)}, u32[]{:S(2)}, u32[]{:S(2)}) collective-permute-start(bf16[4,2,2,16,256]{4,3,2,1,0:T(8,128)(2,1)S(1)} %get-tuple-element.84), channel_id=1, source_target_pairs={{0,9},{1,8},{2,11},{3,10},{4,13},{5,12},{6,15},{7,14},{8,1},{9,0},... | collective-permute-start | bytes 393224 | tf_op jit(solution)/shard_map/ppermute | solution.py:351
  44.5 1.7 %all-to-all-done.4.parts_ref = bf16[16,16,128]{2,1,0:T(8,128)(2,1)S(1)} async-done(((bf16[16,16,128]{2,1,0:T(8,128)(2,1)}), bf16[16,16,128]{2,1,0:T(8,128)(2,1)S(1)}, u32[]{:S(2)}, u32[]{:S(2)}) %all-to-all-start.4) | async-done | bytes 65568 | tf_op jit(solution)/shard_map/all_to_all | solution.py:290
  46.2 0.7 pick.3
  46.9 4.9 %all-to-all-start.5 = ((bf16[16,16,128]{2,1,0:T(8,128)(2,1)}), bf16[16,16,128]{2,1,0:T(8,128)(2,1)S(1)}, u32[]{:S(2)}, u32[]{:S(2)}) async-start(bf16[16,16,128]{2,1,0:T(8,128)(2,1)} %pick.3), calls=%async_computation.5 | async-start | bytes 131072 | tf_op jit(solution)/shard_map/all_to_all | solution.py:290
  51.7 0.0 collective-permute-done.1.refs_0_
  51.8 0.0 collective-permute-done.2.refs_1_
  51.8 0.0 collective-permute-done.3.refs_2_
  51.8 0.1 pair.1
  51.9 2.3 %collective-permute-start.4 = (bf16[2,2,16,256]{3,2,1,0:T(8,128)(2,1)S(1)}, bf16[2,2,16,256]{3,2,1,0:T(8,128)(2,1)S(1)}, u32[]{:S(2)}, u32[]{:S(2)}) collective-permute-start(bf16[2,2,16,256]{3,2,1,0:T(8,128)(2,1)S(1)} %get-tuple-element.86), channel_id=1, source_target_pairs={{0,2},{1,3},{2,4},{3,5},{4,6},{5,7},{6,0},{7,1},{8,10},{9,11},{10,... | collective-permute-start | bytes 98312 | tf_op jit(solution)/shard_map/ppermute | solution.py:200
  54.2 3.3 %collective-permute-start.5 = (bf16[2,2,16,256]{3,2,1,0:T(8,128)(2,1)S(1)}, bf16[2,2,16,256]{3,2,1,0:T(8,128)(2,1)S(1)}, u32[]{:S(2)}, u32[]{:S(2)}) collective-permute-start(bf16[2,2,16,256]{3,2,1,0:T(8,128)(2,1)S(1)} %get-tuple-element.87), channel_id=1, source_target_pairs={{0,4},{1,5},{2,6},{3,7},{4,0},{5,1},{6,2},{7,3},{8,12},{9,13},{10,... | collective-permute-start | bytes 98312 | tf_op jit(solution)/shard_map/ppermute | solution.py:200
  57.5 3.3 %collective-permute-start.6 = (bf16[2,2,16,256]{3,2,1,0:T(8,128)(2,1)S(1)}, bf16[2,2,16,256]{3,2,1,0:T(8,128)(2,1)S(1)}, u32[]{:S(2)}, u32[]{:S(2)}) collective-permute-start(bf16[2,2,16,256]{3,2,1,0:T(8,128)(2,1)S(1)} %get-tuple-element.88), channel_id=1, source_target_pairs={{0,6},{1,7},{2,0},{3,1},{4,2},{5,3},{6,4},{7,5},{8,14},{9,15},{10,... | collective-permute-start | bytes 98312 | tf_op jit(solution)/shard_map/ppermute | solution.py:200
  60.8 0.0 collective-permute-done.4.refs_1_
  60.8 0.7 collective-permute-done.5.refs_2_
  61.5 0.8 %collective-permute-done.6.refs_3_ = bf16[2,2,16,256]{3,2,1,0:T(8,128)(2,1)S(1)} collective-permute-done((bf16[2,2,16,256]{3,2,1,0:T(8,128)(2,1)S(1)}, bf16[2,2,16,256]{3,2,1,0:T(8,128)(2,1)S(1)}, u32[]{:S(2)}, u32[]{:S(2)}) %collective-permute-start.6) | collective-permute-done | bytes 32800 | tf_op jit(solution)/shard_map/ppermute | solution.py:200
  62.4 0.3 weigh.1
  62.7 0.0 all-to-all-done.5.rows_ref
  62.7 0.0 copy-done.3
  62.7 0.3 pack.3
  63.0 12.5 %all_to_all.35 = bf16[8,6,32,256]{3,2,1,0:T(8,128)(2,1)S(1)} all-to-all(bf16[8,6,32,256]{3,2,1,0:T(8,128)(2,1)S(1)} %pack.3), channel_id=1, replica_groups=mesh['yl'=2,'x'=4,'core'=2,'yh'=2,'z'=8] {'yl','x'}, dimensions={0} | all-to-all | bytes 1572864 | tf_op jit(solution)/shard_map/all_to_all | solution.py:290
  75.5 3.9 %collective-permute-start.7 = (bf16[8,6,32,256]{3,2,1,0:T(8,128)(2,1)S(1)}, bf16[8,6,32,256]{3,2,1,0:T(8,128)(2,1)S(1)}, u32[]{:S(2)}, u32[]{:S(2)}) collective-permute-start(bf16[8,6,32,256]{3,2,1,0:T(8,128)(2,1)S(1)} %all_to_all.35), channel_id=1, source_target_pairs={{0,16},{16,0},{1,17},{17,1},{2,18},{18,2},{3,19},{19,3},{4,20},{20... | collective-permute-start | bytes 2359304 | tf_op jit(solution)/shard_map/ppermute | solution.py:315
  79.4 0.2 fusion.1
  79.6 0.2 convert_reduce_fusion
  79.8 0.6 broadcast_compare_fusion
  81.1 0.2 collective-permute-done.7
  81.3 1.5 %final.1 = bf16[16,2,16,256]{3,2,1,0:T(8,128)(2,1)} custom-call(s32[16,8,128]{2,1,0:T(8,128)S(1)} %get-tuple-element.73.source_ref, bf16[8,6,32,256]{3,2,1,0:T(8,128)(2,1)S(1)} %get-tuple-element.91.own_ref, bf16[8,6,32,256]{3,2,1,0:T(8,128)(2,1)S(1)} %get-tuple-element.92.other_ref), custom_call_target="tpu_custom_call" | custom-call | tf_op jit(solution)/shard_map/final/pallas_call | solution.py:393
  (3 shorter events, 0.0 us)
Async XLA Ops:
  0.0 17.1 %copy-start.2 = (s32[4]{0:T(128)S(1)}, s32[4]{0:T(128)}, u32[]{:S(2)}) copy-start(s32[4]{0:T(128)} %src_ref.2) | copy-start | bytes 52
  0.0 17.1 %copy-start.1 = (s32[16,16]{1,0:T(8,128)S(1)}, s32[16,16]{1,0:T(8,128)}, u32[]{:S(2)}) copy-start(s32[16,16]{1,0:T(8,128)} %refs_0_.1) | copy-start | bytes 3076
  0.0 17.1 %copy-start = (bf16[2,4,256,256]{3,2,1,0:T(8,128)(2,1)S(1)}, bf16[2,4,256,256]{3,2,1,0:T(8,128)(2,1)}, u32[]{:S(2)}) copy-start(bf16[2,4,256,256]{3,2,1,0:T(8,128)(2,1)} %refs_1_.1) | copy-start | bytes 3145732
  5.3 27.0 %all-to-all-start.3 = ((bf16[16,2,2,16,256]{4,3,2,1,0:T(8,128)(2,1)}), bf16[16,2,2,16,256]{4,3,2,1,0:T(8,128)(2,1)S(1)}, u32[]{:S(2)}, u32[]{:S(2)}) async-start(bf16[16,2,2,16,256]{4,3,2,1,0:T(8,128)(2,1)} %project0.1), calls=%async_computation.3 | async-start | bytes 1048576 | tf_op jit(solution)/shard_map/all_to_all | solution.py:290
  17.1 45.6 %copy-start.3 = (s32[64]{0:T(128)S(1)}, s32[64]{0:T(128)}, u32[]{:S(2)}) copy-start(s32[64]{0:T(128)} %param.17) | copy-start | bytes 772
  33.0 13.2 %all-to-all-start.4 = ((bf16[16,16,128]{2,1,0:T(8,128)(2,1)}), bf16[16,16,128]{2,1,0:T(8,128)(2,1)S(1)}, u32[]{:S(2)}, u32[]{:S(2)}) async-start(bf16[16,16,128]{2,1,0:T(8,128)(2,1)} %get-tuple-element.77.after_ref), calls=%async_computation.4 | async-start | bytes 131072 | tf_op jit(solution)/shard_map/all_to_all | solution.py:290
  40.4 11.4 %collective-permute-start.1 = (bf16[4,2,2,16,256]{4,3,2,1,0:T(8,128)(2,1)S(1)}, bf16[4,2,2,16,256]{4,3,2,1,0:T(8,128)(2,1)S(1)}, u32[]{:S(2)}, u32[]{:S(2)}) collective-permute-start(bf16[4,2,2,16,256]{4,3,2,1,0:T(8,128)(2,1)S(1)} %get-tuple-element.82), channel_id=1, source_target_pairs={{0,1},{1,0},{2,3},{3,2},{4,5},{5,4},{6,7},{7,6},{8,9},{9,8},{10,11... | collective-permute-start | bytes 393224 | tf_op jit(solution)/shard_map/ppermute | solution.py:200
  41.2 10.6 %collective-permute-start.2 = (bf16[4,2,2,16,256]{4,3,2,1,0:T(8,128)(2,1)S(1)}, bf16[4,2,2,16,256]{4,3,2,1,0:T(8,128)(2,1)S(1)}, u32[]{:S(2)}, u32[]{:S(2)}) collective-permute-start(bf16[4,2,2,16,256]{4,3,2,1,0:T(8,128)(2,1)S(1)} %get-tuple-element.83), channel_id=1, source_target_pairs={{0,8},{8,0},{1,9},{9,1},{2,10},{10,2},{3,11},{11,3},{4,12},{12,4},... | collective-permute-start | bytes 393224 | tf_op jit(solution)/shard_map/ppermute | solution.py:350
  43.2 8.5 %collective-permute-start.3 = (bf16[4,2,2,16,256]{4,3,2,1,0:T(8,128)(2,1)S(1)}, bf16[4,2,2,16,256]{4,3,2,1,0:T(8,128)(2,1)S(1)}, u32[]{:S(2)}, u32[]{:S(2)}) collective-permute-start(bf16[4,2,2,16,256]{4,3,2,1,0:T(8,128)(2,1)S(1)} %get-tuple-element.84), channel_id=1, source_target_pairs={{0,9},{1,8},{2,11},{3,10},{4,13},{5,12},{6,15},{7,14},{8,1},{9,0},... | collective-permute-start | bytes 393224 | tf_op jit(solution)/shard_map/ppermute | solution.py:351
  46.9 15.8 %all-to-all-start.5 = ((bf16[16,16,128]{2,1,0:T(8,128)(2,1)}), bf16[16,16,128]{2,1,0:T(8,128)(2,1)S(1)}, u32[]{:S(2)}, u32[]{:S(2)}) async-start(bf16[16,16,128]{2,1,0:T(8,128)(2,1)} %pick.3), calls=%async_computation.5 | async-start | bytes 131072 | tf_op jit(solution)/shard_map/all_to_all | solution.py:290
  51.9 8.9 %collective-permute-start.4 = (bf16[2,2,16,256]{3,2,1,0:T(8,128)(2,1)S(1)}, bf16[2,2,16,256]{3,2,1,0:T(8,128)(2,1)S(1)}, u32[]{:S(2)}, u32[]{:S(2)}) collective-permute-start(bf16[2,2,16,256]{3,2,1,0:T(8,128)(2,1)S(1)} %get-tuple-element.86), channel_id=1, source_target_pairs={{0,2},{1,3},{2,4},{3,5},{4,6},{5,7},{6,0},{7,1},{8,10},{9,11},{10,... | collective-permute-start | bytes 98312 | tf_op jit(solution)/shard_map/ppermute | solution.py:200
  54.2 7.3 %collective-permute-start.5 = (bf16[2,2,16,256]{3,2,1,0:T(8,128)(2,1)S(1)}, bf16[2,2,16,256]{3,2,1,0:T(8,128)(2,1)S(1)}, u32[]{:S(2)}, u32[]{:S(2)}) collective-permute-start(bf16[2,2,16,256]{3,2,1,0:T(8,128)(2,1)S(1)} %get-tuple-element.87), channel_id=1, source_target_pairs={{0,4},{1,5},{2,6},{3,7},{4,0},{5,1},{6,2},{7,3},{8,12},{9,13},{10,... | collective-permute-start | bytes 98312 | tf_op jit(solution)/shard_map/ppermute | solution.py:200
  57.5 4.9 %collective-permute-start.6 = (bf16[2,2,16,256]{3,2,1,0:T(8,128)(2,1)S(1)}, bf16[2,2,16,256]{3,2,1,0:T(8,128)(2,1)S(1)}, u32[]{:S(2)}, u32[]{:S(2)}) collective-permute-start(bf16[2,2,16,256]{3,2,1,0:T(8,128)(2,1)S(1)} %get-tuple-element.88), channel_id=1, source_target_pairs={{0,6},{1,7},{2,0},{3,1},{4,2},{5,3},{6,4},{7,5},{8,14},{9,15},{10,... | collective-permute-start | bytes 98312 | tf_op jit(solution)/shard_map/ppermute | solution.py:200
  75.5 5.8 %collective-permute-start.7 = (bf16[8,6,32,256]{3,2,1,0:T(8,128)(2,1)S(1)}, bf16[8,6,32,256]{3,2,1,0:T(8,128)(2,1)S(1)}, u32[]{:S(2)}, u32[]{:S(2)}) collective-permute-start(bf16[8,6,32,256]{3,2,1,0:T(8,128)(2,1)S(1)} %all_to_all.35), channel_id=1, source_target_pairs={{0,16},{16,0},{1,17},{17,1},{2,18},{18,2},{3,19},{19,3},{4,20},{20... | collective-permute-start | bytes 2359304 | tf_op jit(solution)/shard_map/ppermute | solution.py:315

commit v6 on v5

--- a/solution.py
+++ b/solution.py
@@ -92,14 +92,20 @@
         (owner_ref, elem_ref), refs = refs[:2], refs[2:]
     outs, (vec_ref, sol_ref, sems) = refs[: 1 + half * 8], refs[1 + half * 8 : 4 + half * 8]
     slots = my_slots(src_ref)
-    copies = []
+    depth = vec_ref.shape[2]
+    cuts = [(0, depth)] * HALF if half else [(0, 512, depth)] + [(0, depth)] * (HALF - 1)
+    copies = {}
     for k in range(HALF):
         t = timeslice_at(slots, half * HALF + k)
-        for part in range(2):
-            copies.append(pltpu.make_async_copy(vec_hbm.at[part, t], vec_ref.at[k, part], sems.at[k, part, 0]))
-            copies.append(pltpu.make_async_copy(sol_hbm.at[part, t], sol_ref.at[k, part], sems.at[k, part, 1]))
-    for copy in copies:
-        copy.start()
+        for piece, (low, high) in enumerate(zip(cuts[k][:-1], cuts[k][1:])):
+            rows = pl.ds(low, high - low)
+            copies[k, piece] = [
+                pltpu.make_async_copy(hbm.at[part, t, rows], ref.at[k, part, rows], sems.at[k, piece, part, i])
+                for part in range(2)
+                for i, (hbm, ref) in enumerate(((vec_hbm, vec_ref), (sol_hbm, sol_ref)))
+            ]
+            for copy in copies[k, piece]:
+                copy.start()
     if half == 1:
         write_masks(src_ref, owner_ref, *outs[5:])
         for k in range(TD):
@@ -107,14 +113,18 @@
                 outs[4][k, part] = elem_ref[part, timeslice_at(slots, k)]
     dims = (((0,), (0,)), ((), ()))
     for k in range(HALF):
-        for copy in copies[4 * k : 4 * k + 4]:
-            copy.wait()
-        depth = vec_ref.shape[2]
-        sol = sol_ref[k].reshape(2 * depth, SC)
-        straight = vec_ref[k].reshape(2 * depth, NEV)
-        turned = jnp.concatenate([-vec_ref[k, 1], vec_ref[k, 0]], axis=0)
-        for part, right in enumerate((straight, turned)):
-            value = lax.dot_general(sol, right, dims, preferred_element_type=F32)
+        values = [None, None]
+        for piece, (low, high) in enumerate(zip(cuts[k][:-1], cuts[k][1:])):
+            for copy in copies[k, piece]:
+                copy.wait()
+            sol = sol_ref[k, :, low:high].reshape(2 * (high - low), SC)
+            vec = vec_ref[k, :, low:high]
+            straight = vec.reshape(2 * (high - low), NEV)
+            turned = jnp.concatenate([-vec[1], vec[0]], axis=0)
+            for part, right in enumerate((straight, turned)):
+                value = lax.dot_general(sol, right, dims, preferred_element_type=F32)
+                values[part] = value if piece == 0 else values[part] + value
+        for part, value in enumerate(values):
             if half == 0:
                 outs[0][:, k, part] = value.astype(BF16).reshape(NC, WIDTH, NEV)
             else:
@@ -137,7 +147,7 @@
     scratch = [
         pltpu.VMEM((HALF, 2, depth, NEV), BF16),
         pltpu.VMEM((HALF, 2, depth, SC), BF16),
-        pltpu.SemaphoreType.DMA((HALF, 2, 2)),
+        pltpu.SemaphoreType.DMA((HALF, 2, 2, 2)),
     ]
     if half == 0:
         shapes = [jax.ShapeDtypeStruct((NC, HALF, 2, WIDTH, NEV), BF16)]

time: 83.2 us -> 83.3 us (level)
  no operation moved by 1% of the time
where the time goes in v6:
time: 83.3 us; the launch traced here: 82.9 us
  starting transfers between devices  40.9 us (49%)
  waiting for transfers between devices  14.2 us (17%)
  Pallas kernels  13.5 us (16%)
  blocking collectives  12.5 us (15%)
  other arithmetic  1.03 us (1%)
    all_to_all x3, starting transfers between devices, all_to_all(): return lax.all_to_all(x, axes, split_axis=0, concat_axis=0, tiled=True)  23.9 us
    all_to_all x1, blocking collectives, all_to_all(): return lax.all_to_all(x, axes, split_axis=0, concat_axis=0, tiled=True)  12.5 us
    all_to_all x3, waiting for transfers between devices, all_to_all(): return lax.all_to_all(x, axes, split_axis=0, concat_axis=0, tiled=True)  12.4 us
    pallas_call x2, Pallas kernels, project(): pl.pallas_call(functools.partial(project_kernel, half), in_specs=[smem()]...  9.91 us
    ppermute x4, starting transfers between devices, along_z(): return lax.ppermute(x, 'z', [(z, to(z)) for z in range(NZ)])  9.75 us
    ppermute x1, starting transfers between devices, gather(): return (own, lax.ppermute(own, 'core', [(0, 1), (1, 0)]))  3.9 us
    ppermute x1, starting transfers between devices, per_device(): lax.ppermute(to_y, 'yh', [(0, 1), (1, 0)])  2.04 us
  transfers between devices with their start and end apart: 10, of which 5 were waited for; matrix products, arithmetic and copies ran while one was open for 1% of the time, Pallas kernels for 7%

profile of v6, /device:TPU:1, one launch (start us, length us, event | category | flops | bytes accessed | tf_op | source)
XLA Modules:
  0.0 82.9 jit_solution(3845863913911387466)
XLA Ops:
  0.0 0.0 copy-start.2
  0.0 0.0 copy-start.1
  0.0 0.0 copy-start
  0.0 5.4 %project0.1 = bf16[16,2,2,16,256]{4,3,2,1,0:T(8,128)(2,1)} custom-call(s32[4]{0:T(128)} %src_ref.2, bf16[2,4,1344,256]{3,2,1,0:T(8,128)(2,1)} %vec_hbm.3, bf16[2,4,1344,256]{3,2,1,0:T(8,128)(2,1)} %sol_hbm.3), custom_call_target="tpu_custom_call" | custom-call | flops 1400000000 | bytes 6000000 | tf_op jit(solution)/shard_map/project0/pallas_call | solution.py:159
  5.4 11.8 %all-to-all-start.3 = ((bf16[16,2,2,16,256]{4,3,2,1,0:T(8,128)(2,1)}), bf16[16,2,2,16,256]{4,3,2,1,0:T(8,128)(2,1)S(1)}, u32[]{:S(2)}, u32[]{:S(2)}) async-start(bf16[16,2,2,16,256]{4,3,2,1,0:T(8,128)(2,1)} %project0.1), calls=%async_computation.3 | async-start | bytes 1048576 | tf_op jit(solution)/shard_map/all_to_all | solution.py:300
  17.2 0.0 copy-done.2
  17.2 0.0 copy-done.1
  17.2 0.0 copy-done
  17.2 0.0 copy-start.3
  17.2 4.5 %project1.1 = (f32[4,2,2,16,256]{4,3,2,1,0:T(8,128)S(1)}, bf16[4,2,2,16,256]{4,3,2,1,0:T(8,128)(2,1)S(1)}, bf16[4,2,2,16,256]{4,3,2,1,0:T(8,128)(2,1)S(1)}, bf16...) custom-call(s32[4]{0:T(128)S(1)} %copy-done.2, ...), custom_call_target="tpu_custom_call" | custom-call | flops 1400000000 | bytes 6000000 | tf_op jit(solution)/shard_map/project1/pallas_call | solution.py:159
  21.7 10.7 %all-to-all-done.3.recv_ref = bf16[16,2,2,16,256]{4,3,2,1,0:T(8,128)(2,1)S(1)} async-done(((bf16[16,2,2,16,256]{4,3,2,1,0:T(8,128)(2,1)}), bf16[16,2,2,16,256]{4,3,2,1,0:T(8,128)(2,1)S(1)}, u32[]{:S(2)}, u32[]{:S(2)}) %all-to-all-start.3) | async-done | bytes 524320 | tf_op jit(solution)/shard_map/all_to_all | solution.py:300
  32.4 0.7 reduce.5
  33.1 7.3 %all-to-all-start.4 = ((bf16[16,16,128]{2,1,0:T(8,128)(2,1)}), bf16[16,16,128]{2,1,0:T(8,128)(2,1)S(1)}, u32[]{:S(2)}, u32[]{:S(2)}) async-start(bf16[16,16,128]{2,1,0:T(8,128)(2,1)} %get-tuple-element.77.after_ref), calls=%async_computation.4 | async-start | bytes 131072 | tf_op jit(solution)/shard_map/all_to_all | solution.py:300
  40.4 0.8 %collective-permute-start.1 = (bf16[4,2,2,16,256]{4,3,2,1,0:T(8,128)(2,1)S(1)}, bf16[4,2,2,16,256]{4,3,2,1,0:T(8,128)(2,1)S(1)}, u32[]{:S(2)}, u32[]{:S(2)}) collective-permute-start(bf16[4,2,2,16,256]{4,3,2,1,0:T(8,128)(2,1)S(1)} %get-tuple-element.82), channel_id=1, source_target_pairs={{0,1},{1,0},{2,3},{3,2},{4,5},{5,4},{6,7},{7,6},{8,9},{9,8},{10,11... | collective-permute-start | bytes 393224 | tf_op jit(solution)/shard_map/ppermute | solution.py:210
  41.3 2.0 %collective-permute-start.2 = (bf16[4,2,2,16,256]{4,3,2,1,0:T(8,128)(2,1)S(1)}, bf16[4,2,2,16,256]{4,3,2,1,0:T(8,128)(2,1)S(1)}, u32[]{:S(2)}, u32[]{:S(2)}) collective-permute-start(bf16[4,2,2,16,256]{4,3,2,1,0:T(8,128)(2,1)S(1)} %get-tuple-element.83), channel_id=1, source_target_pairs={{0,8},{8,0},{1,9},{9,1},{2,10},{10,2},{3,11},{11,3},{4,12},{12,4},... | collective-permute-start | bytes 393224 | tf_op jit(solution)/shard_map/ppermute | solution.py:360
  43.3 1.3 %collective-permute-start.3 = (bf16[4,2,2,16,256]{4,3,2,1,0:T(8,128)(2,1)S(1)}, bf16[4,2,2,16,256]{4,3,2,1,0:T(8,128)(2,1)S(1)}, u32[]{:S(2)}, u32[]{:S(2)}) collective-permute-start(bf16[4,2,2,16,256]{4,3,2,1,0:T(8,128)(2,1)S(1)} %get-tuple-element.84), channel_id=1, source_target_pairs={{0,9},{1,8},{2,11},{3,10},{4,13},{5,12},{6,15},{7,14},{8,1},{9,0},... | collective-permute-start | bytes 393224 | tf_op jit(solution)/shard_map/ppermute | solution.py:361
  44.6 1.7 %all-to-all-done.4.parts_ref = bf16[16,16,128]{2,1,0:T(8,128)(2,1)S(1)} async-done(((bf16[16,16,128]{2,1,0:T(8,128)(2,1)}), bf16[16,16,128]{2,1,0:T(8,128)(2,1)S(1)}, u32[]{:S(2)}, u32[]{:S(2)}) %all-to-all-start.4) | async-done | bytes 65568 | tf_op jit(solution)/shard_map/all_to_all | solution.py:300
  46.3 0.7 pick.3
  46.9 4.9 %all-to-all-start.5 = ((bf16[16,16,128]{2,1,0:T(8,128)(2,1)}), bf16[16,16,128]{2,1,0:T(8,128)(2,1)S(1)}, u32[]{:S(2)}, u32[]{:S(2)}) async-start(bf16[16,16,128]{2,1,0:T(8,128)(2,1)} %pick.3), calls=%async_computation.5 | async-start | bytes 131072 | tf_op jit(solution)/shard_map/all_to_all | solution.py:300
  51.8 0.0 collective-permute-done.1.refs_0_
  51.8 0.0 collective-permute-done.2.refs_1_
  51.8 0.0 collective-permute-done.3.refs_2_
  51.8 0.1 pair.1
  51.9 2.3 %collective-permute-start.4 = (bf16[2,2,16,256]{3,2,1,0:T(8,128)(2,1)S(1)}, bf16[2,2,16,256]{3,2,1,0:T(8,128)(2,1)S(1)}, u32[]{:S(2)}, u32[]{:S(2)}) collective-permute-start(bf16[2,2,16,256]{3,2,1,0:T(8,128)(2,1)S(1)} %get-tuple-element.86), channel_id=1, source_target_pairs={{0,2},{1,3},{2,4},{3,5},{4,6},{5,7},{6,0},{7,1},{8,10},{9,11},{10,... | collective-permute-start | bytes 98312 | tf_op jit(solution)/shard_map/ppermute | solution.py:210
  54.3 3.3 %collective-permute-start.5 = (bf16[2,2,16,256]{3,2,1,0:T(8,128)(2,1)S(1)}, bf16[2,2,16,256]{3,2,1,0:T(8,128)(2,1)S(1)}, u32[]{:S(2)}, u32[]{:S(2)}) collective-permute-start(bf16[2,2,16,256]{3,2,1,0:T(8,128)(2,1)S(1)} %get-tuple-element.87), channel_id=1, source_target_pairs={{0,4},{1,5},{2,6},{3,7},{4,0},{5,1},{6,2},{7,3},{8,12},{9,13},{10,... | collective-permute-start | bytes 98312 | tf_op jit(solution)/shard_map/ppermute | solution.py:210
  57.5 3.3 %collective-permute-start.6 = (bf16[2,2,16,256]{3,2,1,0:T(8,128)(2,1)S(1)}, bf16[2,2,16,256]{3,2,1,0:T(8,128)(2,1)S(1)}, u32[]{:S(2)}, u32[]{:S(2)}) collective-permute-start(bf16[2,2,16,256]{3,2,1,0:T(8,128)(2,1)S(1)} %get-tuple-element.88), channel_id=1, source_target_pairs={{0,6},{1,7},{2,0},{3,1},{4,2},{5,3},{6,4},{7,5},{8,14},{9,15},{10,... | collective-permute-start | bytes 98312 | tf_op jit(solution)/shard_map/ppermute | solution.py:210
  60.8 0.0 collective-permute-done.4.refs_1_
  60.8 0.7 collective-permute-done.5.refs_2_
  61.6 0.8 %collective-permute-done.6.refs_3_ = bf16[2,2,16,256]{3,2,1,0:T(8,128)(2,1)S(1)} collective-permute-done((bf16[2,2,16,256]{3,2,1,0:T(8,128)(2,1)S(1)}, bf16[2,2,16,256]{3,2,1,0:T(8,128)(2,1)S(1)}, u32[]{:S(2)}, u32[]{:S(2)}) %collective-permute-start.6) | collective-permute-done | bytes 32800 | tf_op jit(solution)/shard_map/ppermute | solution.py:210
  62.4 0.3 weigh.1
  62.8 0.0 all-to-all-done.5.rows_ref
  62.8 0.0 copy-done.3
  62.8 0.3 pack.3
  63.1 12.5 %all_to_all.35 = bf16[8,6,32,256]{3,2,1,0:T(8,128)(2,1)S(1)} all-to-all(bf16[8,6,32,256]{3,2,1,0:T(8,128)(2,1)S(1)} %pack.3), channel_id=1, replica_groups=mesh['yl'=2,'x'=4,'core'=2,'yh'=2,'z'=8] {'yl','x'}, dimensions={0} | all-to-all | bytes 1572864 | tf_op jit(solution)/shard_map/all_to_all | solution.py:300
  75.6 3.9 %collective-permute-start.7 = (bf16[8,6,32,256]{3,2,1,0:T(8,128)(2,1)S(1)}, bf16[8,6,32,256]{3,2,1,0:T(8,128)(2,1)S(1)}, u32[]{:S(2)}, u32[]{:S(2)}) collective-permute-start(bf16[8,6,32,256]{3,2,1,0:T(8,128)(2,1)S(1)} %all_to_all.35), channel_id=1, source_target_pairs={{0,16},{16,0},{1,17},{17,1},{2,18},{18,2},{3,19},{19,3},{4,20},{20... | collective-permute-start | bytes 2359304 | tf_op jit(solution)/shard_map/ppermute | solution.py:325
  79.5 0.2 fusion.1
  79.7 0.2 convert_reduce_fusion
  79.9 0.6 broadcast_compare_fusion
  81.2 0.2 collective-permute-done.7
  81.4 1.5 %final.1 = bf16[16,2,16,256]{3,2,1,0:T(8,128)(2,1)} custom-call(s32[16,8,128]{2,1,0:T(8,128)S(1)} %get-tuple-element.73.source_ref, bf16[8,6,32,256]{3,2,1,0:T(8,128)(2,1)S(1)} %get-tuple-element.91.own_ref, bf16[8,6,32,256]{3,2,1,0:T(8,128)(2,1)S(1)} %get-tuple-element.92.other_ref), custom_call_target="tpu_custom_call" | custom-call | tf_op jit(solution)/shard_map/final/pallas_call | solution.py:403
  (3 shorter events, 0.0 us)
Async XLA Ops:
  0.0 17.2 %copy-start.2 = (s32[4]{0:T(128)S(1)}, s32[4]{0:T(128)}, u32[]{:S(2)}) copy-start(s32[4]{0:T(128)} %src_ref.2) | copy-start | bytes 52
  0.0 17.2 %copy-start.1 = (s32[16,16]{1,0:T(8,128)S(1)}, s32[16,16]{1,0:T(8,128)}, u32[]{:S(2)}) copy-start(s32[16,16]{1,0:T(8,128)} %refs_0_.1) | copy-start | bytes 3076
  0.0 17.2 %copy-start = (bf16[2,4,256,256]{3,2,1,0:T(8,128)(2,1)S(1)}, bf16[2,4,256,256]{3,2,1,0:T(8,128)(2,1)}, u32[]{:S(2)}) copy-start(bf16[2,4,256,256]{3,2,1,0:T(8,128)(2,1)} %refs_1_.1) | copy-start | bytes 3145732
  5.4 27.0 %all-to-all-start.3 = ((bf16[16,2,2,16,256]{4,3,2,1,0:T(8,128)(2,1)}), bf16[16,2,2,16,256]{4,3,2,1,0:T(8,128)(2,1)S(1)}, u32[]{:S(2)}, u32[]{:S(2)}) async-start(bf16[16,2,2,16,256]{4,3,2,1,0:T(8,128)(2,1)} %project0.1), calls=%async_computation.3 | async-start | bytes 1048576 | tf_op jit(solution)/shard_map/all_to_all | solution.py:300
  17.2 45.6 %copy-start.3 = (s32[64]{0:T(128)S(1)}, s32[64]{0:T(128)}, u32[]{:S(2)}) copy-start(s32[64]{0:T(128)} %param.17) | copy-start | bytes 772
  33.1 13.1 %all-to-all-start.4 = ((bf16[16,16,128]{2,1,0:T(8,128)(2,1)}), bf16[16,16,128]{2,1,0:T(8,128)(2,1)S(1)}, u32[]{:S(2)}, u32[]{:S(2)}) async-start(bf16[16,16,128]{2,1,0:T(8,128)(2,1)} %get-tuple-element.77.after_ref), calls=%async_computation.4 | async-start | bytes 131072 | tf_op jit(solution)/shard_map/all_to_all | solution.py:300
  40.4 11.4 %collective-permute-start.1 = (bf16[4,2,2,16,256]{4,3,2,1,0:T(8,128)(2,1)S(1)}, bf16[4,2,2,16,256]{4,3,2,1,0:T(8,128)(2,1)S(1)}, u32[]{:S(2)}, u32[]{:S(2)}) collective-permute-start(bf16[4,2,2,16,256]{4,3,2,1,0:T(8,128)(2,1)S(1)} %get-tuple-element.82), channel_id=1, source_target_pairs={{0,1},{1,0},{2,3},{3,2},{4,5},{5,4},{6,7},{7,6},{8,9},{9,8},{10,11... | collective-permute-start | bytes 393224 | tf_op jit(solution)/shard_map/ppermute | solution.py:210
  41.3 10.6 %collective-permute-start.2 = (bf16[4,2,2,16,256]{4,3,2,1,0:T(8,128)(2,1)S(1)}, bf16[4,2,2,16,256]{4,3,2,1,0:T(8,128)(2,1)S(1)}, u32[]{:S(2)}, u32[]{:S(2)}) collective-permute-start(bf16[4,2,2,16,256]{4,3,2,1,0:T(8,128)(2,1)S(1)} %get-tuple-element.83), channel_id=1, source_target_pairs={{0,8},{8,0},{1,9},{9,1},{2,10},{10,2},{3,11},{11,3},{4,12},{12,4},... | collective-permute-start | bytes 393224 | tf_op jit(solution)/shard_map/ppermute | solution.py:360
  43.3 8.5 %collective-permute-start.3 = (bf16[4,2,2,16,256]{4,3,2,1,0:T(8,128)(2,1)S(1)}, bf16[4,2,2,16,256]{4,3,2,1,0:T(8,128)(2,1)S(1)}, u32[]{:S(2)}, u32[]{:S(2)}) collective-permute-start(bf16[4,2,2,16,256]{4,3,2,1,0:T(8,128)(2,1)S(1)} %get-tuple-element.84), channel_id=1, source_target_pairs={{0,9},{1,8},{2,11},{3,10},{4,13},{5,12},{6,15},{7,14},{8,1},{9,0},... | collective-permute-start | bytes 393224 | tf_op jit(solution)/shard_map/ppermute | solution.py:361
  46.9 15.9 %all-to-all-start.5 = ((bf16[16,16,128]{2,1,0:T(8,128)(2,1)}), bf16[16,16,128]{2,1,0:T(8,128)(2,1)S(1)}, u32[]{:S(2)}, u32[]{:S(2)}) async-start(bf16[16,16,128]{2,1,0:T(8,128)(2,1)} %pick.3), calls=%async_computation.5 | async-start | bytes 131072 | tf_op jit(solution)/shard_map/all_to_all | solution.py:300
  51.9 8.9 %collective-permute-start.4 = (bf16[2,2,16,256]{3,2,1,0:T(8,128)(2,1)S(1)}, bf16[2,2,16,256]{3,2,1,0:T(8,128)(2,1)S(1)}, u32[]{:S(2)}, u32[]{:S(2)}) collective-permute-start(bf16[2,2,16,256]{3,2,1,0:T(8,128)(2,1)S(1)} %get-tuple-element.86), channel_id=1, source_target_pairs={{0,2},{1,3},{2,4},{3,5},{4,6},{5,7},{6,0},{7,1},{8,10},{9,11},{10,... | collective-permute-start | bytes 98312 | tf_op jit(solution)/shard_map/ppermute | solution.py:210
  54.3 7.3 %collective-permute-start.5 = (bf16[2,2,16,256]{3,2,1,0:T(8,128)(2,1)S(1)}, bf16[2,2,16,256]{3,2,1,0:T(8,128)(2,1)S(1)}, u32[]{:S(2)}, u32[]{:S(2)}) collective-permute-start(bf16[2,2,16,256]{3,2,1,0:T(8,128)(2,1)S(1)} %get-tuple-element.87), channel_id=1, source_target_pairs={{0,4},{1,5},{2,6},{3,7},{4,0},{5,1},{6,2},{7,3},{8,12},{9,13},{10,... | collective-permute-start | bytes 98312 | tf_op jit(solution)/shard_map/ppermute | solution.py:210
  57.5 4.9 %collective-permute-start.6 = (bf16[2,2,16,256]{3,2,1,0:T(8,128)(2,1)S(1)}, bf16[2,2,16,256]{3,2,1,0:T(8,128)(2,1)S(1)}, u32[]{:S(2)}, u32[]{:S(2)}) collective-permute-start(bf16[2,2,16,256]{3,2,1,0:T(8,128)(2,1)S(1)} %get-tuple-element.88), channel_id=1, source_target_pairs={{0,6},{1,7},{2,0},{3,1},{4,2},{5,3},{6,4},{7,5},{8,14},{9,15},{10,... | collective-permute-start | bytes 98312 | tf_op jit(solution)/shard_map/ppermute | solution.py:210
  75.6 5.8 %collective-permute-start.7 = (bf16[8,6,32,256]{3,2,1,0:T(8,128)(2,1)S(1)}, bf16[8,6,32,256]{3,2,1,0:T(8,128)(2,1)S(1)}, u32[]{:S(2)}, u32[]{:S(2)}) collective-permute-start(bf16[8,6,32,256]{3,2,1,0:T(8,128)(2,1)S(1)} %all_to_all.35), channel_id=1, source_target_pairs={{0,16},{16,0},{1,17},{17,1},{2,18},{18,2},{3,19},{19,3},{4,20},{20... | collective-permute-start | bytes 2359304 | tf_op jit(solution)/shard_map/ppermute | solution.py:325
